TPU v7x, 32 devices: a whole 2x2x4 slice. The times are simulated.
32 devices in a mesh: parts: 2 (over x), grid: 16 (over z, y, core).
Axes of the slice: x: 2, y: 2, z: 4, core: 2. Of those that a mesh axis runs over, the one named last changes fastest.
Arguments:
- block_values: bfloat16 [96, 8, 256, 256], P(('parts', 'grid')), parts along dimension 0, may hold values from -0.59765625 to 0.59765625
- pattern: int32 [96, 8], P('parts'), parts along dimension 0, may hold values from 0 to 47, as said below
Outputs:
- purified: bfloat16 [96, 8, 256, 256], P(('parts', 'grid')), parts along dimension 0
There are 2 independent parts, one for each index of `parts`. A program takes and returns all parts, laid end to end along the dimension named above; each array names one. Nothing has to cross between parts.
Inputs may be any that keep to these rules, and one draw needn't show every extreme that they name: `pattern`: within a row the 8 columns are distinct and include the row's own index; row i, on device d = i // 3, names only block rows of devices d - 1 to d + 1, counted cyclically over 48 block rows.
All inputs are finite; a program needn't handle non-finite values.
Results may differ from a plain program's by a relative error of at most 0.0049.
Values may be sent and summed in bfloat16 or wider, within the bound.
No kernel may reach another device: no remote copies, remote signals or barrier semaphores. Data moves between devices by JAX's collectives and lax.ppermute only.
A program may use at most 128 MiB of HBM per device.

v0:
```python
import jax
import jax.numpy as jnp
from jax import lax
from jax.sharding import PartitionSpec as P

REACH = 1


def shifted(block, axis, distance):
    devices = range(lax.axis_size(axis))
    route = [((i - distance) % len(devices), i) for i in devices]
    return lax.ppermute(block, axis, route)


def gather_band(local_rows):
    moving_up = local_rows
    moving_down = local_rows
    moving_up = shifted(moving_up, "grid", 1)
    upper = [moving_up]
    moving_down = shifted(moving_down, "grid", -1)
    lower = [moving_down]
    return jnp.concatenate(upper[::-1] + [local_rows] + lower, axis=0)


def filtered_product(left_blocks, band_rows, pattern, band_start, first_row):
    rows_here = left_blocks.shape[0]
    total_rows = pattern.shape[0]
    row_ids = (first_row + jnp.arange(rows_here, dtype=jnp.int32)) % total_rows
    own_all = pattern[row_ids]

    def one_row(row_slot):
        own_cols = own_all[row_slot]
        position = (own_cols - band_start) % total_rows
        picked = jnp.take(band_rows, position, axis=0)
        inner = pattern[own_cols]
        matches = (inner[:, :, None] == own_cols[None, None, :]).astype(jnp.bfloat16)
        chosen = jnp.einsum(
            "qst,qsyz->qtyz", matches, picked, preferred_element_type=jnp.float32
        ).astype(jnp.bfloat16)
        return jnp.einsum(
            "qxy,qtyz->txz", left_blocks[row_slot], chosen, preferred_element_type=jnp.float32
        )

    return lax.map(one_row, jnp.arange(rows_here, dtype=jnp.int32))


def local(block_values, pattern):
    rows_here = block_values.shape[0]
    total_rows = pattern.shape[0]
    device = lax.axis_index("grid")
    first_row = device * rows_here
    band_start = (device - REACH) * rows_here % total_rows
    band_values = gather_band(block_values)
    square = filtered_product(block_values, band_values, pattern, band_start, first_row).astype(
        jnp.bfloat16
    )
    band_square = gather_band(square)
    cube = filtered_product(block_values, band_square, pattern, band_start, first_row)
    return (3.0 * square.astype(jnp.float32) - 2.0 * cube).astype(jnp.bfloat16)


def solution(mesh):
    return jax.shard_map(
        local,
        mesh=mesh,
        in_specs=(P(("parts", "grid"), None, None, None), P("parts", None)),
        out_specs=P(("parts", "grid"), None, None, None),
        check_vma=False,
    )
```

profile of v0, /device:TPU:1, one launch (start us, length us, event | category | flops | bytes accessed | tf_op | source)
XLA Modules:
  0.0 474.2 jit_solution(15240371639143029175)
XLA Ops:
  0.0 2.6 collective-permute-start
  2.6 0.8 copy.3
  3.4 0.6 gather_fusion.4
  4.0 2.0 broadcast_convert_fusion
  6.0 64.9 %collective-permute-done = bf16[3,8,256,256]{3,2,1,0:T(8,128)(2,1)} collective-permute-done((bf16[3,8,256,256]{3,2,1,0:T(8,128)(2,1)}, bf16[3,8,256,256]{3,2,1,0:T(8,128)(2,1)}, u32[]{:S(2)}, u32[]{:S(2)}) %collective-permute-start) | collective-permute-done | bytes 3145760 | tf_op jit(solution)/shard_map/ppermute | solution.py:12
  70.9 2.5 collective-permute-done.1
  73.3 7.7 %pad_maximum_fusion = bf16[9,8,256,256]{3,2,1,0:T(8,128)(2,1)} fusion(bf16[3,8,256,256]{3,2,1,0:T(8,128)(2,1)} %collective-permute-done.1, bf16[3,8,256,256]{3,2,1,0:T(8,128)(2,1)} %param.8, bf16[3,8,256,256]{3,2,1,0:T(8,128)(2,1)} %collective-permute-done), kind=kLoop, calls=%fused_computation.51 | loop fusion | flops 9437184 | bytes 18874368 | tf_op jit(solution)/shard_map/concatenate | solution.py:22
  81.1 150.5 %while.26 = (s32[]{:T(128)}, bf16[3,8,256,256]{3,2,1,0:T(8,128)(2,1)}, s32[3]{0:T(128)S(1)}, s32[3,8]{1,0:T(4,128)S(1)}, s32[48,8]{1,0:T(8,128)S(1)}, /*index=5*...) while((s32[]{:T(128)}, bf16[3,8,256,256]{3,2,1,0:T(8,128)(2,1)}, ...), condition=%wide.region_1.3_spmd.clone, body=%wide.region_0.2_spmd.sunk.clone | while | flops 2218789376 | bytes 81798872 | solution.py:44
  81.1 0.7 dynamic_slice.71
  83.8 8.4 %gather_fusion = bf16[8,8,256,256]{3,2,1,0:T(8,128)(2,1)} fusion(bf16[9,8,256,256]{3,2,1,0:T(8,128)(2,1)} %get-tuple-element.444, s32[1024]{0:T(1024)S(1)} %pad_clamp_fusion.13), kind=kCustom, calls=%fused_computation.clone.clone.1.clone | custom fusion | bytes 16777248 | tf_op jit(solution)/shard_map/while/body/eval_jaxpr/jit(_take)/gather | solution.py:34
  92.3 7.6 %broadcast_select_fusion.6 = bf16[8,8,256,256]{3,2,1,0:T(8,128)(2,1)} fusion(bf16[8,8,256,256]{3,2,1,0:T(8,128)(2,1)} %gather_fusion, pred[8]{0:T(512)(128)(4,1)S(1)} %get-tuple-element.386), kind=kLoop, calls=%fused_computation.9.clone.1.clone | loop fusion | flops 4194304 | bytes 16777224 | tf_op jit(solution)/shard_map/while/body/eval_jaxpr/jit(_take)/select_n | solution.py:34
  99.9 0.6 gather_fusion.1
  100.4 10.9 %fusion.70 = bf16[8,8,256,256]{3,1,2,0:T(8,128)(2,1)} fusion(bf16[8,8,256,256]{3,2,1,0:T(8,128)(2,1)} %broadcast_select_fusion.6, s32[8]{0:T(128)S(1)} %get-tuple-element.387, s32[8,8]{1,0:T(8,128)S(1)} %gather_fusion.1), kind=kOutput, calls=%fused_computation.5.clone.1.clone | convolution fusion | flops 67109376 | bytes 16777504 | tf_op jit(solution)/shard_map/while/body/eval_jaxpr/qst,qsyz->qtyz/dot_general | solution.py:37
  111.3 12.4 %copy.37 = bf16[8,8,256,256]{2,3,0,1:T(8,128)(2,1)} copy(bf16[8,8,256,256]{3,1,2,0:T(8,128)(2,1)} %fusion.70) | data formatting | bytes 16777216 | tf_op jit(solution)/shard_map/while/body/eval_jaxpr/qst,qsyz->qtyz/dot_general | solution.py:37
  123.6 6.0 %fusion.71 = bf16[1,8,256,256]{2,3,1,0:T(8,128)(2,1)S(1)} fusion(bf16[8,8,256,256]{2,3,0,1:T(8,128)(2,1)} %copy.37, bf16[3,8,256,256]{3,2,1,0:T(8,128)(2,1)} %get-tuple-element.445, s32[]{:T(128)S(6)} %select_n.151), kind=kOutput, calls=%fused_computation.10.clone.1.clone | convolution fusion | flops 2147483648 | bytes 10485764 | tf_op jit(solution)/shard_map/while/body/eval_jaxpr/qxy,qtyz->txz/dot_general | solution.py:40
  129.6 0.5 copy.38
  130.2 1.0 constant_dynamic-update-slice_fusion.6
  131.2 0.7 dynamic_slice.71
  134.0 8.4 %gather_fusion = bf16[8,8,256,256]{3,2,1,0:T(8,128)(2,1)} fusion(bf16[9,8,256,256]{3,2,1,0:T(8,128)(2,1)} %get-tuple-element.444, s32[1024]{0:T(1024)S(1)} %pad_clamp_fusion.13), kind=kCustom, calls=%fused_computation.clone.clone.1.clone | custom fusion | bytes 16777248 | tf_op jit(solution)/shard_map/while/body/eval_jaxpr/jit(_take)/gather | solution.py:34
  142.4 7.6 %broadcast_select_fusion.6 = bf16[8,8,256,256]{3,2,1,0:T(8,128)(2,1)} fusion(bf16[8,8,256,256]{3,2,1,0:T(8,128)(2,1)} %gather_fusion, pred[8]{0:T(512)(128)(4,1)S(1)} %get-tuple-element.386), kind=kLoop, calls=%fused_computation.9.clone.1.clone | loop fusion | flops 4194304 | bytes 16777224 | tf_op jit(solution)/shard_map/while/body/eval_jaxpr/jit(_take)/select_n | solution.py:34
  150.0 0.6 gather_fusion.1
  150.6 10.9 %fusion.70 = bf16[8,8,256,256]{3,1,2,0:T(8,128)(2,1)} fusion(bf16[8,8,256,256]{3,2,1,0:T(8,128)(2,1)} %broadcast_select_fusion.6, s32[8]{0:T(128)S(1)} %get-tuple-element.387, s32[8,8]{1,0:T(8,128)S(1)} %gather_fusion.1), kind=kOutput, calls=%fused_computation.5.clone.1.clone | convolution fusion | flops 67109376 | bytes 16777504 | tf_op jit(solution)/shard_map/while/body/eval_jaxpr/qst,qsyz->qtyz/dot_general | solution.py:37
  161.4 12.4 %copy.37 = bf16[8,8,256,256]{2,3,0,1:T(8,128)(2,1)} copy(bf16[8,8,256,256]{3,1,2,0:T(8,128)(2,1)} %fusion.70) | data formatting | bytes 16777216 | tf_op jit(solution)/shard_map/while/body/eval_jaxpr/qst,qsyz->qtyz/dot_general | solution.py:37
  173.8 6.0 %fusion.71 = bf16[1,8,256,256]{2,3,1,0:T(8,128)(2,1)S(1)} fusion(bf16[8,8,256,256]{2,3,0,1:T(8,128)(2,1)} %copy.37, bf16[3,8,256,256]{3,2,1,0:T(8,128)(2,1)} %get-tuple-element.445, s32[]{:T(128)S(6)} %select_n.151), kind=kOutput, calls=%fused_computation.10.clone.1.clone | convolution fusion | flops 2147483648 | bytes 10485764 | tf_op jit(solution)/shard_map/while/body/eval_jaxpr/qxy,qtyz->txz/dot_general | solution.py:40
  180.3 1.0 constant_dynamic-update-slice_fusion.6
  181.4 0.7 dynamic_slice.71
  184.1 8.4 %gather_fusion = bf16[8,8,256,256]{3,2,1,0:T(8,128)(2,1)} fusion(bf16[9,8,256,256]{3,2,1,0:T(8,128)(2,1)} %get-tuple-element.444, s32[1024]{0:T(1024)S(1)} %pad_clamp_fusion.13), kind=kCustom, calls=%fused_computation.clone.clone.1.clone | custom fusion | bytes 16777248 | tf_op jit(solution)/shard_map/while/body/eval_jaxpr/jit(_take)/gather | solution.py:34
  192.6 7.6 %broadcast_select_fusion.6 = bf16[8,8,256,256]{3,2,1,0:T(8,128)(2,1)} fusion(bf16[8,8,256,256]{3,2,1,0:T(8,128)(2,1)} %gather_fusion, pred[8]{0:T(512)(128)(4,1)S(1)} %get-tuple-element.386), kind=kLoop, calls=%fused_computation.9.clone.1.clone | loop fusion | flops 4194304 | bytes 16777224 | tf_op jit(solution)/shard_map/while/body/eval_jaxpr/jit(_take)/select_n | solution.py:34
  200.2 0.6 gather_fusion.1
  200.7 10.9 %fusion.70 = bf16[8,8,256,256]{3,1,2,0:T(8,128)(2,1)} fusion(bf16[8,8,256,256]{3,2,1,0:T(8,128)(2,1)} %broadcast_select_fusion.6, s32[8]{0:T(128)S(1)} %get-tuple-element.387, s32[8,8]{1,0:T(8,128)S(1)} %gather_fusion.1), kind=kOutput, calls=%fused_computation.5.clone.1.clone | convolution fusion | flops 67109376 | bytes 16777504 | tf_op jit(solution)/shard_map/while/body/eval_jaxpr/qst,qsyz->qtyz/dot_general | solution.py:37
  211.6 12.4 %copy.37 = bf16[8,8,256,256]{2,3,0,1:T(8,128)(2,1)} copy(bf16[8,8,256,256]{3,1,2,0:T(8,128)(2,1)} %fusion.70) | data formatting | bytes 16777216 | tf_op jit(solution)/shard_map/while/body/eval_jaxpr/qst,qsyz->qtyz/dot_general | solution.py:37
  223.9 6.1 %fusion.71 = bf16[1,8,256,256]{2,3,1,0:T(8,128)(2,1)S(1)} fusion(bf16[8,8,256,256]{2,3,0,1:T(8,128)(2,1)} %copy.37, bf16[3,8,256,256]{3,2,1,0:T(8,128)(2,1)} %get-tuple-element.445, s32[]{:T(128)S(6)} %select_n.151), kind=kOutput, calls=%fused_computation.10.clone.1.clone | convolution fusion | flops 2147483648 | bytes 10485764 | tf_op jit(solution)/shard_map/while/body/eval_jaxpr/qxy,qtyz->txz/dot_general | solution.py:40
  230.5 1.0 constant_dynamic-update-slice_fusion.6
  232.1 67.7 %collective-permute-done.2 = bf16[3,8,256,256]{3,2,1,0:T(8,128)(2,1)} collective-permute-done((bf16[3,8,256,256]{3,2,1,0:T(8,128)(2,1)}, bf16[3,8,256,256]{3,2,1,0:T(8,128)(2,1)}, u32[]{:S(2)}, u32[]{:S(2)}) %collective-permute-start.2) | collective-permute-done | bytes 3145760 | tf_op jit(solution)/shard_map/ppermute | solution.py:12
  299.8 7.7 %pad_maximum_fusion.1 = bf16[9,8,256,256]{3,2,1,0:T(8,128)(2,1)} fusion(bf16[3,8,256,256]{3,2,1,0:T(8,128)(2,1)} %collective-permute-done.3, bf16[3,8,256,256]{3,2,1,0:T(8,128)(2,1)} %get-tuple-element.210, bf16[3,8,256,256]{3,2,1,0:T(8,128)(2,1)} %collective-permute-done.2), kind=kLoop, calls=%fused_computation.52 | loop fusion | flops 9437184 | bytes 18874368 | tf_op jit(solution)/shard_map/concatenate | solution.py:22
  307.5 160.2 %while.27 = (s32[]{:T(128)}, f32[3,8,256,256]{3,2,1,0:T(8,128)}, s32[3]{0:T(128)S(1)}, s32[3,8]{1,0:T(4,128)S(1)}, s32[48,8]{1,0:T(8,128)S(1)}, /*index=5*/s32[]...) while((s32[]{:T(128)}, f32[3,8,256,256]{3,2,1,0:T(8,128)}, s32[3]{0:T(128)S(1)}, ...), condition=%wide.region_3.5_spmd.clone, body=%wide.region_2.4_spmd.sunk.clone | while | flops 2218789376 | bytes 87041752 | solution.py:44
  307.5 0.7 dynamic_slice.74
  310.3 8.4 %gather_fusion.2 = bf16[8,8,256,256]{3,2,1,0:T(8,128)(2,1)} fusion(bf16[9,8,256,256]{3,2,1,0:T(8,128)(2,1)} %get-tuple-element.468, s32[1024]{0:T(1024)S(1)} %pad_clamp_fusion.15), kind=kCustom, calls=%fused_computation.2.clone.clone.1.clone | custom fusion | bytes 16777248 | tf_op jit(solution)/shard_map/while/body/eval_jaxpr/jit(_take)/gather | solution.py:34
  318.8 7.6 %broadcast_select_fusion.7 = bf16[8,8,256,256]{3,2,1,0:T(8,128)(2,1)} fusion(bf16[8,8,256,256]{3,2,1,0:T(8,128)(2,1)} %gather_fusion.2, pred[8]{0:T(512)(128)(4,1)S(1)} %get-tuple-element.409), kind=kLoop, calls=%fused_computation.32.clone.1.clone | loop fusion | flops 4194304 | bytes 16777224 | tf_op jit(solution)/shard_map/while/body/eval_jaxpr/jit(_take)/select_n | solution.py:34
  326.3 0.6 gather_fusion.3
  326.9 10.9 %fusion.77 = bf16[8,8,256,256]{3,1,2,0:T(8,128)(2,1)} fusion(bf16[8,8,256,256]{3,2,1,0:T(8,128)(2,1)} %broadcast_select_fusion.7, s32[8]{0:T(128)S(1)} %get-tuple-element.410, s32[8,8]{1,0:T(8,128)S(1)} %gather_fusion.3), kind=kOutput, calls=%fused_computation.28.clone.1.clone | convolution fusion | flops 67109376 | bytes 16777504 | tf_op jit(solution)/shard_map/while/body/eval_jaxpr/qst,qsyz->qtyz/dot_general | solution.py:37
  337.7 12.4 %copy.40 = bf16[8,8,256,256]{2,3,0,1:T(8,128)(2,1)} copy(bf16[8,8,256,256]{3,1,2,0:T(8,128)(2,1)} %fusion.77) | data formatting | bytes 16777216 | tf_op jit(solution)/shard_map/while/body/eval_jaxpr/qst,qsyz->qtyz/dot_general | solution.py:37
  350.1 7.3 %fusion.78 = f32[1,8,256,256]{2,3,1,0:T(8,128)} fusion(bf16[8,8,256,256]{2,3,0,1:T(8,128)(2,1)} %copy.40, bf16[3,8,256,256]{3,2,1,0:T(8,128)(2,1)} %get-tuple-element.469, s32[]{:T(128)S(6)} %select_n.154), kind=kOutput, calls=%fused_computation.33.clone.1.clone | convolution fusion | flops 2147483648 | bytes 11534340 | tf_op jit(solution)/shard_map/while/body/eval_jaxpr/qxy,qtyz->txz/dot_general | solution.py:40
  357.4 1.9 copy.41
  359.3 1.5 constant_dynamic-update-slice_fusion.7
  360.9 0.7 dynamic_slice.74
  363.7 8.4 %gather_fusion.2 = bf16[8,8,256,256]{3,2,1,0:T(8,128)(2,1)} fusion(bf16[9,8,256,256]{3,2,1,0:T(8,128)(2,1)} %get-tuple-element.468, s32[1024]{0:T(1024)S(1)} %pad_clamp_fusion.15), kind=kCustom, calls=%fused_computation.2.clone.clone.1.clone | custom fusion | bytes 16777248 | tf_op jit(solution)/shard_map/while/body/eval_jaxpr/jit(_take)/gather | solution.py:34
  372.1 7.6 %broadcast_select_fusion.7 = bf16[8,8,256,256]{3,2,1,0:T(8,128)(2,1)} fusion(bf16[8,8,256,256]{3,2,1,0:T(8,128)(2,1)} %gather_fusion.2, pred[8]{0:T(512)(128)(4,1)S(1)} %get-tuple-element.409), kind=kLoop, calls=%fused_computation.32.clone.1.clone | loop fusion | flops 4194304 | bytes 16777224 | tf_op jit(solution)/shard_map/while/body/eval_jaxpr/jit(_take)/select_n | solution.py:34
  379.7 0.6 gather_fusion.3
  380.2 10.9 %fusion.77 = bf16[8,8,256,256]{3,1,2,0:T(8,128)(2,1)} fusion(bf16[8,8,256,256]{3,2,1,0:T(8,128)(2,1)} %broadcast_select_fusion.7, s32[8]{0:T(128)S(1)} %get-tuple-element.410, s32[8,8]{1,0:T(8,128)S(1)} %gather_fusion.3), kind=kOutput, calls=%fused_computation.28.clone.1.clone | convolution fusion | flops 67109376 | bytes 16777504 | tf_op jit(solution)/shard_map/while/body/eval_jaxpr/qst,qsyz->qtyz/dot_general | solution.py:37
  391.1 12.4 %copy.40 = bf16[8,8,256,256]{2,3,0,1:T(8,128)(2,1)} copy(bf16[8,8,256,256]{3,1,2,0:T(8,128)(2,1)} %fusion.77) | data formatting | bytes 16777216 | tf_op jit(solution)/shard_map/while/body/eval_jaxpr/qst,qsyz->qtyz/dot_general | solution.py:37
  403.5 7.3 %fusion.78 = f32[1,8,256,256]{2,3,1,0:T(8,128)} fusion(bf16[8,8,256,256]{2,3,0,1:T(8,128)(2,1)} %copy.40, bf16[3,8,256,256]{3,2,1,0:T(8,128)(2,1)} %get-tuple-element.469, s32[]{:T(128)S(6)} %select_n.154), kind=kOutput, calls=%fused_computation.33.clone.1.clone | convolution fusion | flops 2147483648 | bytes 11534340 | tf_op jit(solution)/shard_map/while/body/eval_jaxpr/qxy,qtyz->txz/dot_general | solution.py:40
  410.8 1.9 copy.41
  412.7 1.7 constant_dynamic-update-slice_fusion.7
  414.4 0.7 dynamic_slice.74
  417.1 8.4 %gather_fusion.2 = bf16[8,8,256,256]{3,2,1,0:T(8,128)(2,1)} fusion(bf16[9,8,256,256]{3,2,1,0:T(8,128)(2,1)} %get-tuple-element.468, s32[1024]{0:T(1024)S(1)} %pad_clamp_fusion.15), kind=kCustom, calls=%fused_computation.2.clone.clone.1.clone | custom fusion | bytes 16777248 | tf_op jit(solution)/shard_map/while/body/eval_jaxpr/jit(_take)/gather | solution.py:34
  425.6 7.6 %broadcast_select_fusion.7 = bf16[8,8,256,256]{3,2,1,0:T(8,128)(2,1)} fusion(bf16[8,8,256,256]{3,2,1,0:T(8,128)(2,1)} %gather_fusion.2, pred[8]{0:T(512)(128)(4,1)S(1)} %get-tuple-element.409), kind=kLoop, calls=%fused_computation.32.clone.1.clone | loop fusion | flops 4194304 | bytes 16777224 | tf_op jit(solution)/shard_map/while/body/eval_jaxpr/jit(_take)/select_n | solution.py:34
  433.1 0.6 gather_fusion.3
  433.7 10.9 %fusion.77 = bf16[8,8,256,256]{3,1,2,0:T(8,128)(2,1)} fusion(bf16[8,8,256,256]{3,2,1,0:T(8,128)(2,1)} %broadcast_select_fusion.7, s32[8]{0:T(128)S(1)} %get-tuple-element.410, s32[8,8]{1,0:T(8,128)S(1)} %gather_fusion.3), kind=kOutput, calls=%fused_computation.28.clone.1.clone | convolution fusion | flops 67109376 | bytes 16777504 | tf_op jit(solution)/shard_map/while/body/eval_jaxpr/qst,qsyz->qtyz/dot_general | solution.py:37
  444.6 12.4 %copy.40 = bf16[8,8,256,256]{2,3,0,1:T(8,128)(2,1)} copy(bf16[8,8,256,256]{3,1,2,0:T(8,128)(2,1)} %fusion.77) | data formatting | bytes 16777216 | tf_op jit(solution)/shard_map/while/body/eval_jaxpr/qst,qsyz->qtyz/dot_general | solution.py:37
  456.9 7.4 %fusion.78 = f32[1,8,256,256]{2,3,1,0:T(8,128)} fusion(bf16[8,8,256,256]{2,3,0,1:T(8,128)(2,1)} %copy.40, bf16[3,8,256,256]{3,2,1,0:T(8,128)(2,1)} %get-tuple-element.469, s32[]{:T(128)S(6)} %select_n.154), kind=kOutput, calls=%fused_computation.33.clone.1.clone | convolution fusion | flops 2147483648 | bytes 11534340 | tf_op jit(solution)/shard_map/while/body/eval_jaxpr/qxy,qtyz->txz/dot_general | solution.py:40
  464.3 1.9 copy.41
  466.2 1.5 constant_dynamic-update-slice_fusion.7
  467.8 6.4 %subtract_convert_fusion = bf16[3,8,256,256]{3,2,1,0:T(8,128)(2,1)} fusion(f32[3,8,256,256]{3,2,1,0:T(8,128)} %get-tuple-element.211, bf16[3,8,256,256]{3,2,1,0:T(8,128)(2,1)} %get-tuple-element.210), kind=kLoop, calls=%fused_computation.53 | loop fusion | flops 7864320 | bytes 12582912 | tf_op jit(solution)/shard_map/convert_element_type | solution.py:59
  (35 shorter events, 1.9 us)
Async XLA Ops:
  0.0 70.9 %collective-permute-start = (bf16[3,8,256,256]{3,2,1,0:T(8,128)(2,1)}, bf16[3,8,256,256]{3,2,1,0:T(8,128)(2,1)}, u32[]{:S(2)}, u32[]{:S(2)}) collective-permute-start(bf16[3,8,256,256]{3,2,1,0:T(8,128)(2,1)} %param.8), channel_id=1, source_target_pairs={{15,0},{0,1},{1,2},{2,3},{3,4},{4,5},{5,6},{6,7},{7,8},{8,9},{9,10... | collective-permute-start | bytes 9437192 | tf_op jit(solution)/shard_map/ppermute | solution.py:12
  2.6 70.7 %collective-permute-start.1 = (bf16[3,8,256,256]{3,2,1,0:T(8,128)(2,1)}, bf16[3,8,256,256]{3,2,1,0:T(8,128)(2,1)}, u32[]{:S(2)}, u32[]{:S(2)}) collective-permute-start(bf16[3,8,256,256]{3,2,1,0:T(8,128)(2,1)} %param.8), channel_id=1, source_target_pairs={{1,0},{2,1},{3,2},{4,3},{5,4},{6,5},{7,6},{8,7},{9,8},{10,9},{11,1... | collective-permute-start | bytes 9437192 | tf_op jit(solution)/shard_map/ppermute | solution.py:12
  231.6 68.2 %collective-permute-start.2 = (bf16[3,8,256,256]{3,2,1,0:T(8,128)(2,1)}, bf16[3,8,256,256]{3,2,1,0:T(8,128)(2,1)}, u32[]{:S(2)}, u32[]{:S(2)}) collective-permute-start(bf16[3,8,256,256]{3,2,1,0:T(8,128)(2,1)} %get-tuple-element.210), channel_id=1, source_target_pairs={{15,0},{0,1},{1,2},{2,3},{3,4},{4,5},{5,6},{6,7},{7,8},{8,9},{9,10... | collective-permute-start | bytes 9437192 | tf_op jit(solution)/shard_map/ppermute | solution.py:12
  231.6 68.2 %collective-permute-start.3 = (bf16[3,8,256,256]{3,2,1,0:T(8,128)(2,1)}, bf16[3,8,256,256]{3,2,1,0:T(8,128)(2,1)}, u32[]{:S(2)}, u32[]{:S(2)}) collective-permute-start(bf16[3,8,256,256]{3,2,1,0:T(8,128)(2,1)} %get-tuple-element.210), channel_id=1, source_target_pairs={{1,0},{2,1},{3,2},{4,3},{5,4},{6,5},{7,6},{8,7},{9,8},{10,9},{11,1... | collective-permute-start | bytes 9437192 | tf_op jit(solution)/shard_map/ppermute | solution.py:12
where the time goes:
time: 477 us; the launch traced here: 474 us
  local copies, waits for them, and re-layouts  149 us (31%)
  waiting for transfers between devices  135 us (28%)
  matrix products  105 us (22%)
  other arithmetic  69.5 us (15%)
  loops' own time  12.6 us (3%)
    ppermute x4, waiting for transfers between devices, shifted(): return lax.ppermute(block, axis, route)  135 us
    dot_general x6, local copies, waits for them, and re-layouts, one_row(): jnp.einsum('qst,qsyz->qtyz', matches, picked, preferred_element_type=jnp....  74.2 us
    dot_general x6, matrix products, one_row(): jnp.einsum('qst,qsyz->qtyz', matches, picked, preferred_element_type=jnp....  65.1 us
    gather x6, local copies, waits for them, and re-layouts, one_row(): picked = jnp.take(band_rows, position, axis=0)  50.7 us
    select_n x6, other arithmetic, one_row(): picked = jnp.take(band_rows, position, axis=0)  45.3 us
    dot_general x6, matrix products, one_row(): jnp.einsum('qxy,qtyz->txz', left_blocks[row_slot], chosen, preferred_elem...  40 us
    concatenate x2, other arithmetic, gather_band(): return jnp.concatenate(upper[::-1] + [local_rows] + lower, axis=0)  15.4 us
    dynamic_update_slice x12, local copies, waits for them, and re-layouts, filtered_product(): return lax.map(one_row, jnp.arange(rows_here, dtype=jnp.int32))  15.2 us
  transfers between devices with their start and end apart: 4, of which 3 were waited for; matrix products, arithmetic and copies ran while one was open for 1% of the time, Pallas kernels for 0%

commit v1 on v0

v1 whole, which is shorter than its diff:
```python
import functools

import jax
import jax.numpy as jnp
from jax import lax
from jax.experimental import pallas as pl
from jax.experimental.pallas import tpu as pltpu
from jax.sharding import PartitionSpec as P


F32 = jnp.float32
BF16 = jnp.bfloat16
ANY = pl.BlockSpec(memory_space=pl.ANY)
HBM = pl.BlockSpec(memory_space=pltpu.HBM)
VMEM = pl.BlockSpec(memory_space=pltpu.VMEM)
SMEM = pl.BlockSpec(memory_space=pltpu.SMEM)
VMEM_LIMIT = 40 * 1024 * 1024


def neighbours(devices):
    me = lax.axis_index("grid")
    odd = lax.rem(me, 2)
    above = lax.rem(me + 1, devices)
    below = lax.rem(me + devices - 1, devices)
    return me, jnp.where(odd == 1, above, below), jnp.where(odd == 1, below, above)


def slot_of(pattern, row, column):
    slot = jnp.int32(-1)
    for s in range(pattern.shape[1]):
        slot = jnp.where(pattern[row, s] == column, s, slot)
    return slot


def panel_product(left, right, c, rb, bs):
    total = jnp.dot(left[0], right[c, pl.ds(0, bs), :], preferred_element_type=F32)
    for k in range(1, rb):
        total += jnp.dot(left[k], right[c, pl.ds(k * bs, bs), :], preferred_element_type=F32)
    return total


def drop_absent(ref, pattern, row_device, column_device, rb, bs):
    for r in range(rb):
        for j in range(rb):
            slot = slot_of(pattern, row_device * rb + r, column_device * rb + j)

            @pl.when(slot < 0)
            def _():
                ref[j, pl.ds(r * bs, bs), :] = jnp.zeros((bs, bs), ref.dtype)


def pack_kernel(devices, rb, bs, pattern_hbm, blocks, *rest):
    cuts, (pattern, held, zeros, pattern_sem, in_sems, out_sems) = rest[:3], rest[3:]
    fetch = pltpu.make_async_copy(pattern_hbm, pattern, pattern_sem)
    fetch.start()
    loads = [pltpu.make_async_copy(blocks.at[r], held.at[r], in_sems.at[r]) for r in range(rb)]
    for load in loads:
        load.start()
    zeros[...] = jnp.zeros_like(zeros)
    people = neighbours(devices)
    me = people[0]
    fetch.wait()
    stores = []
    for n, (column_device, out) in enumerate(zip((people[1], me, people[2]), cuts)):
        for r in range(rb):
            if n == 0:
                loads[r].wait()
            for j in range(rb):
                slot = slot_of(pattern, me * rb + r, column_device * rb + j)
                sem = out_sems.at[(n * rb + r) * rb + j]
                dst = out.at[j, pl.ds(r * bs, bs), :]
                found = pltpu.make_async_copy(held.at[r, jnp.maximum(slot, 0)], dst, sem)
                absent = pltpu.make_async_copy(zeros, dst, sem)
                pl.when(slot >= 0)(found.start)
                pl.when(slot < 0)(absent.start)
                stores.append(absent)
    for store in stores:
        store.wait()


def pack(devices, pattern, blocks):
    rb, _, bs, _ = blocks.shape
    return pl.pallas_call(
        functools.partial(pack_kernel, devices, rb, bs),
        out_shape=[jax.ShapeDtypeStruct((rb, rb * bs, bs), blocks.dtype)] * 3,
        in_specs=[HBM, HBM],
        out_specs=[ANY] * 3,
        scratch_shapes=[
            pltpu.SMEM(pattern.shape, pattern.dtype),
            pltpu.VMEM(blocks.shape, blocks.dtype),
            pltpu.VMEM((bs, bs), blocks.dtype),
            pltpu.SemaphoreType.DMA,
            pltpu.SemaphoreType.DMA((rb,)),
            pltpu.SemaphoreType.DMA((3 * rb * rb,)),
        ],
        compiler_params=pltpu.CompilerParams(vmem_limit_bytes=VMEM_LIMIT),
        cost_estimate=pl.CostEstimate(
            flops=0, bytes_accessed=6 * rb * rb * bs * bs * 2, transcendentals=0
        ),
        name="pack",
    )(pattern, blocks)


def call(kernel, devices, rb, bs, products, operands, out_dtypes, name, **more):
    cut = (rb, rb * bs, bs)
    return pl.pallas_call(
        functools.partial(kernel, devices, rb, bs),
        out_shape=[jax.ShapeDtypeStruct(cut, t) for t in out_dtypes],
        in_specs=[SMEM] + [VMEM] * (len(operands) - 1),
        out_specs=[VMEM] * len(out_dtypes),
        compiler_params=pltpu.CompilerParams(vmem_limit_bytes=VMEM_LIMIT),
        cost_estimate=pl.CostEstimate(
            flops=products * 2 * (rb * bs) ** 3,
            bytes_accessed=(len(operands) + len(out_dtypes)) * rb * rb * bs * bs * 2,
            transcendentals=0,
        ),
        name=name,
        **more,
    )(*operands)


def inner_kernel(devices, rb, bs, pattern, own, inner, from_inner, inner_own, s_inner, s_from_inner, part):
    me, _, partner = neighbours(devices)

    @pl.loop(0, rb)
    def _(c):
        s_inner[c] = (panel_product(own, inner, c, rb, bs) + panel_product(inner, inner_own, c, rb, bs)).astype(BF16)
        s_from_inner[c] = (
            panel_product(from_inner, own, c, rb, bs) + panel_product(inner_own, from_inner, c, rb, bs)
        ).astype(BF16)
        part[c] = panel_product(own, own, c, rb, bs) + panel_product(inner, from_inner, c, rb, bs)

    drop_absent(s_inner, pattern, me, partner, rb, bs)
    drop_absent(s_from_inner, pattern, partner, me, rb, bs)


def own_kernel(devices, rb, bs, pattern, outer, from_outer, part, s_own):
    me, _, _ = neighbours(devices)

    @pl.loop(0, rb)
    def _(c):
        s_own[c] = (part[c] + panel_product(outer, from_outer, c, rb, bs)).astype(BF16)

    drop_absent(s_own, pattern, me, me, rb, bs)


def scatter(out, pattern, me, column_device, panels, sems, base, rb, bs):
    waits = []
    for r in range(rb):
        for j in range(rb):
            slot = slot_of(pattern, me * rb + r, column_device * rb + j)
            copy = pltpu.make_async_copy(
                panels.at[j, pl.ds(r * bs, bs), :],
                out.at[r, jnp.maximum(slot, 0)],
                sems.at[base + r * rb + j],
            )
            pl.when(slot >= 0)(copy.start)
            waits.append((slot, copy))
    return waits


def settle(waits):
    for slot, copy in waits:
        pl.when(slot >= 0)(copy.wait)


def middle_kernel(
    devices, rb, bs, pattern, own, outer, inner, outer_own, from_outer, s_own, s_inner, s_from_inner, s_inner_own,
    out, rest, s_outer, s_from_outer, out_own, out_inner, sems,
):
    me, other, partner = neighbours(devices)

    @pl.loop(0, rb)
    def _(c):
        out_inner[c] = (
            3.0 * s_inner[c].astype(F32)
            - 2.0 * (panel_product(own, s_inner, c, rb, bs) + panel_product(inner, s_inner_own, c, rb, bs))
        ).astype(BF16)

    waits = scatter(out, pattern, me, partner, out_inner, sems, 0, rb, bs)

    @pl.loop(0, rb)
    def _(c):
        s_outer[c] = (panel_product(own, outer, c, rb, bs) + panel_product(outer, outer_own, c, rb, bs)).astype(BF16)
        s_from_outer[c] = (
            panel_product(from_outer, own, c, rb, bs) + panel_product(outer_own, from_outer, c, rb, bs)
        ).astype(BF16)

    drop_absent(s_outer, pattern, me, other, rb, bs)
    drop_absent(s_from_outer, pattern, other, me, rb, bs)

    @pl.loop(0, rb)
    def _(c):
        rest[c] = 3.0 * s_outer[c].astype(F32) - 2.0 * panel_product(own, s_outer, c, rb, bs)
        cube = panel_product(own, s_own, c, rb, bs)
        cube += panel_product(outer, s_from_outer, c, rb, bs)
        cube += panel_product(inner, s_from_inner, c, rb, bs)
        out_own[c] = (3.0 * s_own[c].astype(F32) - 2.0 * cube).astype(BF16)

    waits += scatter(out, pattern, me, me, out_own, sems, rb * rb, rb, bs)
    settle(waits)


def last_kernel(devices, rb, bs, pattern, outer, s_outer_own, rest, _, out, panels, sems):
    me, other, _ = neighbours(devices)

    @pl.loop(0, rb)
    def _(c):
        panels[c] = (rest[c] - 2.0 * panel_product(outer, s_outer_own, c, rb, bs)).astype(BF16)

    settle(scatter(out, pattern, me, other, panels, sems, 0, rb, bs))


def local(devices, block_values, pattern):
    rb, _, bs, _ = block_values.shape
    cut = (rb, rb * bs, bs)
    one = 2 * rb * rb * bs * bs
    over = [(i, (i + 1 if i % 2 else i - 1) % devices) for i in range(devices)]
    across = [(i, i ^ 1) for i in range(devices)]
    to_outer = lambda x: lax.ppermute(x, "grid", over)
    to_inner = lambda x: lax.ppermute(x, "grid", across)

    outer, own, inner = pack(devices, pattern, block_values)
    from_outer = to_outer(outer)
    outer_own = to_outer(own)
    from_inner, inner_own = to_inner(inner), to_inner(own)

    s_inner, s_from_inner, part = call(
        inner_kernel, devices, rb, bs, 6, (pattern, own, inner, from_inner, inner_own), (BF16, BF16, F32), "inner"
    )
    (s_own,) = call(own_kernel, devices, rb, bs, 1, (pattern, outer, from_outer, part), (BF16,), "square")
    s_outer_own = to_outer(s_own)
    s_inner_own = to_inner(s_own)

    operands = (pattern, own, outer, inner, outer_own, from_outer, s_own, s_inner, s_from_inner, s_inner_own)
    out, rest = pl.pallas_call(
        functools.partial(middle_kernel, devices, rb, bs),
        out_shape=[jax.ShapeDtypeStruct(block_values.shape, BF16), jax.ShapeDtypeStruct(cut, F32)],
        in_specs=[SMEM] + [VMEM] * 9,
        out_specs=[ANY, VMEM],
        scratch_shapes=[pltpu.VMEM(cut, BF16)] * 4 + [pltpu.SemaphoreType.DMA((2 * rb * rb,))],
        compiler_params=pltpu.CompilerParams(vmem_limit_bytes=VMEM_LIMIT),
        cost_estimate=pl.CostEstimate(
            flops=10 * 2 * (rb * bs) ** 3, bytes_accessed=13 * one, transcendentals=0
        ),
        name="middle",
    )(*operands)
    return pl.pallas_call(
        functools.partial(last_kernel, devices, rb, bs),
        out_shape=jax.ShapeDtypeStruct(block_values.shape, BF16),
        in_specs=[SMEM] + [VMEM] * 3 + [ANY],
        out_specs=ANY,
        input_output_aliases={4: 0},
        scratch_shapes=[pltpu.VMEM(cut, BF16), pltpu.SemaphoreType.DMA((rb * rb,))],
        compiler_params=pltpu.CompilerParams(vmem_limit_bytes=VMEM_LIMIT),
        cost_estimate=pl.CostEstimate(flops=2 * (rb * bs) ** 3, bytes_accessed=5 * one, transcendentals=0),
        name="last",
    )(pattern, outer, s_outer_own, rest, out)


def solution(mesh):
    return jax.shard_map(
        functools.partial(local, mesh.shape["grid"]),
        mesh=mesh,
        in_specs=(P(("parts", "grid"), None, None, None), P("parts", None)),
        out_specs=P(("parts", "grid"), None, None, None),
        check_vma=False,
    )
```

time: 477 us -> 94.1 us (0.20)
  local copies, waits for them, and re-layouts: 149 us -> 2.65 us
  matrix products: 105 us -> 0 us
  waiting for transfers between devices: 135 us -> 52.8 us
  other arithmetic: 69.5 us -> 0 us
  Pallas kernels: 0 us -> 33.3 us
  loops' own time: 12.6 us -> 0 us
    dot_general x12 -> x0, matrix products: 105 us -> none  [the longest x6 65.1 us: one_row(): jnp.einsum('qst,qsyz->qtyz', matches, picked, preferred_element_type=jnp....]
    ppermute x4 -> x6, waiting for transfers between devices: 135 us -> 52.8 us  [the longest x3 51.4 us: local(): to_outer = lambda x: lax.ppermute(x, 'grid', over)]
    dot_general x6 -> x0, local copies, waits for them, and re-layouts: 74.2 us -> none  [one_row(): jnp.einsum('qst,qsyz->qtyz', matches, picked, preferred_element_type=jnp....]
    gather x13 -> x0, local copies, waits for them, and re-layouts: 54.5 us -> none  [the longest x6 50.7 us: one_row(): picked = jnp.take(band_rows, position, axis=0)]
    select_n x13 -> x0, other arithmetic: 45.4 us -> none  [the longest x6 45.3 us: one_row(): picked = jnp.take(band_rows, position, axis=0)]
    pallas_call x0 -> x5, Pallas kernels: none -> 33.3 us  [the longest x1 13.1 us: local(): pl.pallas_call(functools.partial(middle_kernel, devices, rb, bs), out_sha...]
    concatenate x2 -> x0, other arithmetic: 15.4 us -> none  [gather_band(): return jnp.concatenate(upper[::-1] + [local_rows] + lower, axis=0)]
    dynamic_update_slice x12 -> x0, local copies, waits for them, and re-layouts: 15.2 us -> none  [filtered_product(): return lax.map(one_row, jnp.arange(rows_here, dtype=jnp.int32))]
  transfers between devices with their start and end apart: 4 -> 6, of which waited for: 3 -> 3; matrix products, arithmetic and copies ran while one was open for 1% -> 0% of each run, Pallas kernels for 0% -> 24%
where the time goes in v1:
time: 94.1 us; the launch traced here: 93.9 us
  waiting for transfers between devices  52.8 us (56%)
  Pallas kernels  33.3 us (35%)
  starting transfers between devices  5.11 us (5%)
  local copies, waits for them, and re-layouts  2.65 us (3%)
    ppermute x3, waiting for transfers between devices, local(): to_outer = lambda x: lax.ppermute(x, 'grid', over)  51.4 us
    pallas_call x1, Pallas kernels, local(): pl.pallas_call(functools.partial(middle_kernel, devices, rb, bs), out_sha...  13.1 us
    pallas_call x2, Pallas kernels, call(): pl.pallas_call(functools.partial(kernel, devices, rb, bs), out_shape=[jax...  9.74 us
    pallas_call x1, Pallas kernels, pack(): pl.pallas_call(functools.partial(pack_kernel, devices, rb, bs), out_shape...  6.97 us
    ppermute x3, starting transfers between devices, local(): to_outer = lambda x: lax.ppermute(x, 'grid', over)  4.47 us
    pallas_call x1, Pallas kernels, local(): pl.pallas_call(functools.partial(last_kernel, devices, rb, bs), out_shape...  3.46 us
    unnamed x3, local copies, waits for them, and re-layouts  2.65 us
  transfers between devices with their start and end apart: 6, of which 3 were waited for; matrix products, arithmetic and copies ran while one was open for 0% of the time, Pallas kernels for 24%

profile of v1, /device:TPU:1, one launch (start us, length us, event | category | flops | bytes accessed | tf_op | source)
XLA Modules:
  0.0 93.9 jit_solution(3727556632729104322)
XLA Ops:
  0.0 0.8 copy.8.pattern_hbm.pattern
  0.8 0.0 copy-start
  0.8 1.9 %copy-done = bf16[3,8,256,256]{3,2,1,0:T(8,128)(2,1)S(1)} copy-done((bf16[3,8,256,256]{3,2,1,0:T(8,128)(2,1)S(1)}, bf16[3,8,256,256]{3,2,1,0:T(8,128)(2,1)}, u32[]{:S(2)}) %copy-start) | copy-done | bytes 3145752
  2.7 7.0 %pack.1 = (bf16[3,768,256]{2,1,0:T(8,128)(2,1)S(1)}, bf16[3,768,256]{2,1,0:T(8,128)(2,1)S(1)}, bf16[3,768,256]{2,1,0:T(8,128)(2,1)S(1)}) custom-call(s32[48,8]{1,0:T(8,128)S(1)} %copy.8.pattern_hbm.pattern, bf16[3,8,256,256]{3,2,1,0:T(8,128)(2,1)S(1)} %copy-done), custom_call_target="tpu_custom_call" | custom-call | bytes 7077888 | tf_op jit(solution)/shard_map/pack/pallas_call | solution.py:83
  9.6 0.1 collective-permute-start.1
  9.8 0.5 collective-permute-start.2
  10.2 2.6 %collective-permute-start = (bf16[3,768,256]{2,1,0:T(8,128)(2,1)S(1)}, bf16[3,768,256]{2,1,0:T(8,128)(2,1)S(1)}, u32[]{:S(2)}, u32[]{:S(2)}) collective-permute-start(bf16[3,768,256]{2,1,0:T(8,128)(2,1)S(1)} %get-tuple-element.13.outer), channel_id=1, source_target_pairs={{0,15},{1,2},{2,1},{3,4},{4,3},{5,6},{6,5},{7,8},{8,7},{9,10},{10,... | collective-permute-start | bytes 3538952 | tf_op jit(solution)/shard_map/ppermute | solution.py:220
  12.8 0.0 collective-permute-start.4
  12.9 0.0 collective-permute-done.1.from_inner
  12.9 1.4 %collective-permute-done.2.inner_own = bf16[3,768,256]{2,1,0:T(8,128)(2,1)S(1)} collective-permute-done((bf16[3,768,256]{2,1,0:T(8,128)(2,1)S(1)}, bf16[3,768,256]{2,1,0:T(8,128)(2,1)S(1)}, u32[]{:S(2)}, u32[]{:S(2)}) %collective-permute-start.2) | collective-permute-done | bytes 1179680 | tf_op jit(solution)/shard_map/ppermute | solution.py:221
  14.2 7.2 %inner.1 = (bf16[3,768,256]{2,1,0:T(8,128)(2,1)S(1)}, bf16[3,768,256]{2,1,0:T(8,128)(2,1)S(1)}, f32[3,768,256]{2,1,0:T(8,128)S(1)}) custom-call(s32[48,8]{1,0:T(8,128)S(1)} %copy.8.pattern_hbm.pattern, bf16[3,768,256]{2,1,0:T(8,128)(2,1)S(1)} %get-tuple-element.14.own, bf16[3,768,256]{2,1,0:T(8,128)(2,1)S(1)} %get-tuple-element.15.inner, ...), custom_call_target="tpu_custom_call" | custom-call | flops 5435817984 | bytes 9437184 | tf_op jit(solution)/shard_map/inner/pallas_call | solution.py:106
  21.5 30.5 %collective-permute-done.from_outer = bf16[3,768,256]{2,1,0:T(8,128)(2,1)S(1)} collective-permute-done((bf16[3,768,256]{2,1,0:T(8,128)(2,1)S(1)}, bf16[3,768,256]{2,1,0:T(8,128)(2,1)S(1)}, u32[]{:S(2)}, u32[]{:S(2)}) %collective-permute-start) | collective-permute-done | bytes 1179680 | tf_op jit(solution)/shard_map/ppermute | solution.py:220
  52.0 2.5 %square.1.s_own = bf16[3,768,256]{2,1,0:T(8,128)(2,1)S(1)} custom-call(s32[48,8]{1,0:T(8,128)S(1)} %copy.8.pattern_hbm.pattern, bf16[3,768,256]{2,1,0:T(8,128)(2,1)S(1)} %get-tuple-element.13.outer, bf16[3,768,256]{2,1,0:T(8,128)(2,1)S(1)} %collective-permute-done.from_outer, f32[3,768,256]{2,1,0:T(8,128)S(1)} %get-tuple-element.16.part), custom_call_target="tpu_custom_call" | custom-call | flops 905969664 | bytes 5898240 | tf_op jit(solution)/shard_map/square/pallas_call | solution.py:106
  54.5 0.1 collective-permute-start.5
  54.6 1.8 %collective-permute-start.3 = (bf16[3,768,256]{2,1,0:T(8,128)(2,1)S(1)}, bf16[3,768,256]{2,1,0:T(8,128)(2,1)S(1)}, u32[]{:S(2)}, u32[]{:S(2)}) collective-permute-start(bf16[3,768,256]{2,1,0:T(8,128)(2,1)S(1)} %square.1.s_own), channel_id=1, source_target_pairs={{0,15},{1,2},{2,1},{3,4},{4,3},{5,6},{6,5},{7,8},{8,7},{9,10},{10,... | collective-permute-start | bytes 3538952 | tf_op jit(solution)/shard_map/ppermute | solution.py:220
  56.4 20.9 %collective-permute-done.4.outer_own = bf16[3,768,256]{2,1,0:T(8,128)(2,1)S(1)} collective-permute-done((bf16[3,768,256]{2,1,0:T(8,128)(2,1)S(1)}, bf16[3,768,256]{2,1,0:T(8,128)(2,1)S(1)}, u32[]{:S(2)}, u32[]{:S(2)}) %collective-permute-start.4) | collective-permute-done | bytes 1179680 | tf_op jit(solution)/shard_map/ppermute | solution.py:220
  77.3 0.0 collective-permute-done.5.s_inner_own
  77.3 13.1 %middle.1 = (bf16[3,8,256,256]{3,2,1,0:T(8,128)(2,1)}, f32[3,768,256]{2,1,0:T(8,128)S(1)}) custom-call(s32[48,8]{1,0:T(8,128)S(1)} %copy.8.pattern_hbm.pattern, bf16[3,768,256]{2,1,0:T(8,128)(2,1)S(1)} %get-tuple-element.14.own, bf16[3,768,256]{2,1,0:T(8,128)(2,1)S(1)} %get-tuple-element.13.outer, bf16[3,768,256]{2,1,0:T(8,128)(2,1)S(1)} %get-tuple-element.15.inner, ...), custom_call_target="tpu_custom_call" | custom-call | flops 9059696640 | bytes 15335424 | tf_op jit(solution)/shard_map/middle/pallas_call | solution.py:236
  90.4 0.0 collective-permute-done.3.s_outer_own
  90.5 3.5 %last.1 = bf16[3,8,256,256]{3,2,1,0:T(8,128)(2,1)} custom-call(s32[48,8]{1,0:T(8,128)S(1)} %copy.8.pattern_hbm.pattern, bf16[3,768,256]{2,1,0:T(8,128)(2,1)S(1)} %get-tuple-element.13.outer, bf16[3,768,256]{2,1,0:T(8,128)(2,1)S(1)} %collective-permute-done.3.s_outer_own, f32[3,768,256]{2,1,0:T(8,128)S(1)} %get-tuple-element.19.rest, ...), custom_call_target="tpu_custom_call", output_to_operand_aliasing={{}: (4, {})} | custom-call | flops 905969664 | bytes 5898240 | tf_op jit(solution)/shard_map/last/pallas_call | solution.py:248
Async XLA Ops:
  0.8 1.9 %copy-start = (bf16[3,8,256,256]{3,2,1,0:T(8,128)(2,1)S(1)}, bf16[3,8,256,256]{3,2,1,0:T(8,128)(2,1)}, u32[]{:S(2)}) copy-start(bf16[3,8,256,256]{3,2,1,0:T(8,128)(2,1)} %blocks.1) | copy-start | bytes 9437188
  9.6 3.2 %collective-permute-start.1 = (bf16[3,768,256]{2,1,0:T(8,128)(2,1)S(1)}, bf16[3,768,256]{2,1,0:T(8,128)(2,1)S(1)}, u32[]{:S(2)}, u32[]{:S(2)}) collective-permute-start(bf16[3,768,256]{2,1,0:T(8,128)(2,1)S(1)} %get-tuple-element.15.inner), channel_id=1, source_target_pairs={{0,1},{1,0},{2,3},{3,2},{4,5},{5,4},{6,7},{7,6},{8,9},{9,8},{10,11... | collective-permute-start | bytes 3538952 | tf_op jit(solution)/shard_map/ppermute | solution.py:221
  9.8 4.5 %collective-permute-start.2 = (bf16[3,768,256]{2,1,0:T(8,128)(2,1)S(1)}, bf16[3,768,256]{2,1,0:T(8,128)(2,1)S(1)}, u32[]{:S(2)}, u32[]{:S(2)}) collective-permute-start(bf16[3,768,256]{2,1,0:T(8,128)(2,1)S(1)} %get-tuple-element.14.own), channel_id=1, source_target_pairs={{0,1},{1,0},{2,3},{3,2},{4,5},{5,4},{6,7},{7,6},{8,9},{9,8},{10,11... | collective-permute-start | bytes 3538952 | tf_op jit(solution)/shard_map/ppermute | solution.py:221
  10.2 41.8 %collective-permute-start = (bf16[3,768,256]{2,1,0:T(8,128)(2,1)S(1)}, bf16[3,768,256]{2,1,0:T(8,128)(2,1)S(1)}, u32[]{:S(2)}, u32[]{:S(2)}) collective-permute-start(bf16[3,768,256]{2,1,0:T(8,128)(2,1)S(1)} %get-tuple-element.13.outer), channel_id=1, source_target_pairs={{0,15},{1,2},{2,1},{3,4},{4,3},{5,6},{6,5},{7,8},{8,7},{9,10},{10,... | collective-permute-start | bytes 3538952 | tf_op jit(solution)/shard_map/ppermute | solution.py:220
  12.8 64.4 %collective-permute-start.4 = (bf16[3,768,256]{2,1,0:T(8,128)(2,1)S(1)}, bf16[3,768,256]{2,1,0:T(8,128)(2,1)S(1)}, u32[]{:S(2)}, u32[]{:S(2)}) collective-permute-start(bf16[3,768,256]{2,1,0:T(8,128)(2,1)S(1)} %get-tuple-element.14.own), channel_id=1, source_target_pairs={{0,15},{1,2},{2,1},{3,4},{4,3},{5,6},{6,5},{7,8},{8,7},{9,10},{10,... | collective-permute-start | bytes 3538952 | tf_op jit(solution)/shard_map/ppermute | solution.py:220
  54.5 22.8 %collective-permute-start.5 = (bf16[3,768,256]{2,1,0:T(8,128)(2,1)S(1)}, bf16[3,768,256]{2,1,0:T(8,128)(2,1)S(1)}, u32[]{:S(2)}, u32[]{:S(2)}) collective-permute-start(bf16[3,768,256]{2,1,0:T(8,128)(2,1)S(1)} %square.1.s_own), channel_id=1, source_target_pairs={{0,1},{1,0},{2,3},{3,2},{4,5},{5,4},{6,7},{7,6},{8,9},{9,8},{10,11... | collective-permute-start | bytes 3538952 | tf_op jit(solution)/shard_map/ppermute | solution.py:221
  54.6 35.8 %collective-permute-start.3 = (bf16[3,768,256]{2,1,0:T(8,128)(2,1)S(1)}, bf16[3,768,256]{2,1,0:T(8,128)(2,1)S(1)}, u32[]{:S(2)}, u32[]{:S(2)}) collective-permute-start(bf16[3,768,256]{2,1,0:T(8,128)(2,1)S(1)} %square.1.s_own), channel_id=1, source_target_pairs={{0,15},{1,2},{2,1},{3,4},{4,3},{5,6},{6,5},{7,8},{8,7},{9,10},{10,... | collective-permute-start | bytes 3538952 | tf_op jit(solution)/shard_map/ppermute | solution.py:220

commit v2 on v1

v2 whole, which is shorter than its diff:
```python
import functools

import jax
import jax.numpy as jnp
from jax import lax
from jax.experimental import pallas as pl
from jax.experimental.pallas import tpu as pltpu
from jax.sharding import PartitionSpec as P


F32 = jnp.float32
BF16 = jnp.bfloat16
ANY = pl.BlockSpec(memory_space=pl.ANY)
HBM = pl.BlockSpec(memory_space=pltpu.HBM)
VMEM = pl.BlockSpec(memory_space=pltpu.VMEM)
SMEM = pl.BlockSpec(memory_space=pltpu.SMEM)
BRIEF = pl.CostEstimate(flops=1, bytes_accessed=1, transcendentals=0)
VMEM_LIMIT = 24 * 1024 * 1024


def neighbours(devices):
    me = lax.axis_index("grid")
    odd = lax.rem(me, 2)
    above = lax.rem(me + 1, devices)
    below = lax.rem(me + devices - 1, devices)
    return me, jnp.where(odd == 1, above, below), jnp.where(odd == 1, below, above)


def slot_of(pattern, row, column):
    slot = jnp.int32(-1)
    for s in range(pattern.shape[0]):
        slot = jnp.where(pattern[s, row] == column, s, slot)
    return slot


def panel_product(left, right, c, rb, bs):
    total = jnp.dot(left[0], right[c, pl.ds(0, bs), :], preferred_element_type=F32)
    for k in range(1, rb):
        total += jnp.dot(left[k], right[c, pl.ds(k * bs, bs), :], preferred_element_type=F32)
    return total


def drop_absent(ref, pattern, row_device, column_device, rb, bs):
    for r in range(rb):
        for j in range(rb):
            slot = slot_of(pattern, row_device * rb + r, column_device * rb + j)

            @pl.when(slot < 0)
            def _():
                ref[j, pl.ds(r * bs, bs), :] = jnp.zeros((bs, bs), ref.dtype)


def pack_kernel(devices, rb, bs, pattern_hbm, blocks, *rest):
    cuts, (pattern, held, pattern_sem, sems) = rest[:3], rest[3:]
    fetch = pltpu.make_async_copy(pattern_hbm, pattern, pattern_sem)
    fetch.start()
    loads = [pltpu.make_async_copy(blocks.at[r], held.at[r], sems.at[r]) for r in range(rb)]
    for load in loads:
        load.start()
    me, other, partner = neighbours(devices)
    fetch.wait()
    for r in range(rb):
        slots = [
            [slot_of(pattern, me * rb + r, column_device * rb + j) for j in range(rb)]
            for column_device in (other, me, partner)
        ]
        loads[r].wait()
        for cut, row in zip(cuts, slots):
            for j, slot in enumerate(row):
                block = held[r, jnp.maximum(slot, 0)]
                cut[j, pl.ds(r * bs, bs), :] = jnp.where(slot >= 0, block, jnp.zeros_like(block))


def pack(devices, pattern, blocks):
    rb, _, bs, _ = blocks.shape
    return pl.pallas_call(
        functools.partial(pack_kernel, devices, rb, bs),
        out_shape=[jax.ShapeDtypeStruct((rb, rb * bs, bs), blocks.dtype)] * 3,
        in_specs=[ANY, ANY],
        out_specs=[VMEM] * 3,
        scratch_shapes=[
            pltpu.SMEM(pattern.shape, pattern.dtype),
            pltpu.VMEM(blocks.shape, blocks.dtype),
            pltpu.SemaphoreType.DMA,
            pltpu.SemaphoreType.DMA((rb,)),
        ],
        compiler_params=pltpu.CompilerParams(vmem_limit_bytes=VMEM_LIMIT),
        cost_estimate=BRIEF,
        name="pack",
    )(
        pltpu.with_memory_space_constraint(pattern, pltpu.HBM),
        pltpu.with_memory_space_constraint(blocks, pltpu.HBM),
    )


def scatter(out, pattern, me, column_device, panels, j, sems, base, rb, bs):
    waits = []
    for r in range(rb):
        slot = slot_of(pattern, me * rb + r, column_device * rb + j)
        copy = pltpu.make_async_copy(
            panels.at[j, pl.ds(r * bs, bs), :], out.at[r, jnp.maximum(slot, 0)], sems.at[base + r * rb + j]
        )
        pl.when(slot >= 0)(copy.start)
        waits.append((slot, copy))
    return waits


def settle(waits):
    for slot, copy in waits:
        pl.when(slot >= 0)(copy.wait)


def inner_kernel(
    devices, rb, bs, pattern, own, inner, outer, from_inner, inner_own, s_inner, s_from_inner, own_part, outer_part
):
    me, _, partner = neighbours(devices)

    @pl.loop(0, rb)
    def _(c):
        s_inner[c] = (panel_product(own, inner, c, rb, bs) + panel_product(inner, inner_own, c, rb, bs)).astype(BF16)
        s_from_inner[c] = (
            panel_product(from_inner, own, c, rb, bs) + panel_product(inner_own, from_inner, c, rb, bs)
        ).astype(BF16)
        own_part[c] = panel_product(own, own, c, rb, bs) + panel_product(inner, from_inner, c, rb, bs)
        outer_part[c] = panel_product(own, outer, c, rb, bs)

    drop_absent(s_inner, pattern, me, partner, rb, bs)
    drop_absent(s_from_inner, pattern, partner, me, rb, bs)


def square_kernel(
    devices, rb, bs, pattern, own, inner, outer, from_outer, s_inner, s_from_inner, own_part,
    s_own, s_head, s_tail, from_outer_part, cube_part, inner_part,
):
    me, _, _ = neighbours(devices)

    @pl.loop(0, rb)
    def _(c):
        s_own[c] = (own_part[c] + panel_product(outer, from_outer, c, rb, bs)).astype(BF16)

    drop_absent(s_own, pattern, me, me, rb, bs)
    s_head[...] = s_own[pl.ds(0, rb - 1)]
    s_tail[...] = s_own[pl.ds(rb - 1, 1)]

    @pl.loop(0, rb)
    def _(c):
        from_outer_part[c] = panel_product(from_outer, own, c, rb, bs)
        cube_part[c] = panel_product(own, s_own, c, rb, bs) + panel_product(inner, s_from_inner, c, rb, bs)
        inner_part[c] = 3.0 * s_inner[c].astype(F32) - 2.0 * panel_product(own, s_inner, c, rb, bs)


def late_kernel(
    devices, rb, bs, pattern, own, outer, inner, outer_own, from_outer, s_own, s_inner_own, outer_part,
    from_outer_part, cube_part, inner_part, out, rest, s_outer, s_from_outer, out_own, out_inner, sems,
):
    me, other, partner = neighbours(devices)
    waits = []
    for c in range(rb):
        out_inner[c] = (inner_part[c] - 2.0 * panel_product(inner, s_inner_own, c, rb, bs)).astype(BF16)
        waits += scatter(out, pattern, me, partner, out_inner, c, sems, 0, rb, bs)

    @pl.loop(0, rb)
    def _(c):
        s_from_outer[c] = (from_outer_part[c] + panel_product(outer_own, from_outer, c, rb, bs)).astype(BF16)
        s_outer[c] = (outer_part[c] + panel_product(outer, outer_own, c, rb, bs)).astype(BF16)

    drop_absent(s_outer, pattern, me, other, rb, bs)
    drop_absent(s_from_outer, pattern, other, me, rb, bs)
    for c in range(rb):
        cube = cube_part[c] + panel_product(outer, s_from_outer, c, rb, bs)
        out_own[c] = (3.0 * s_own[c].astype(F32) - 2.0 * cube).astype(BF16)
        waits += scatter(out, pattern, me, me, out_own, c, sems, rb * rb, rb, bs)

    @pl.loop(0, rb)
    def _(c):
        rest[c] = 3.0 * s_outer[c].astype(F32) - 2.0 * panel_product(own, s_outer, c, rb, bs)

    settle(waits)


def last_kernel(first, devices, rb, bs, pattern, outer, s_outer_own, rest, _, out, out_outer, sems):
    me, other, _ = neighbours(devices)
    waits = []
    for c in range(s_outer_own.shape[0]):
        cube = panel_product(outer, s_outer_own, c, rb, bs)
        out_outer[first + c] = (rest[first + c] - 2.0 * cube).astype(BF16)
        waits += scatter(out, pattern, me, other, out_outer, first + c, sems, 0, rb, bs)
    settle(waits)


def local(devices, block_values, pattern):
    rb, _, bs, _ = block_values.shape
    pattern = pattern.T
    over = [(i, (i + 1 if i % 2 else i - 1) % devices) for i in range(devices)]
    across = [(i, i ^ 1) for i in range(devices)]
    to_outer = lambda x: lax.ppermute(x, "grid", over)
    to_inner = lambda x: lax.ppermute(x, "grid", across)
    low_of = lambda panels: jax.ShapeDtypeStruct((panels, rb * bs, bs), BF16)
    low = low_of(rb)
    high = jax.ShapeDtypeStruct(low.shape, F32)
    full = jax.ShapeDtypeStruct(block_values.shape, BF16)

    def call(kernel, operands, outs, scratch=(), into=None):
        operands = (pltpu.with_memory_space_constraint(pattern, pltpu.SMEM), *operands)
        in_specs = [SMEM] + [VMEM] * (len(operands) - 1)
        aliases = {}
        if into is not None:
            aliases = {len(operands): 0}
            operands, in_specs = (*operands, into), in_specs + [ANY]
        scratch = [pltpu.VMEM(low.shape, BF16)] * scratch + [pltpu.SemaphoreType.DMA((2 * rb * rb,))] if scratch else []
        return pl.pallas_call(
            functools.partial(kernel, devices, rb, bs),
            out_shape=outs,
            in_specs=in_specs,
            out_specs=[ANY if out is full else VMEM for out in outs],
            scratch_shapes=scratch,
            input_output_aliases=aliases,
            compiler_params=pltpu.CompilerParams(vmem_limit_bytes=VMEM_LIMIT),
            cost_estimate=BRIEF,
            name=getattr(kernel, "func", kernel).__name__,
        )(*operands)

    outer, own, inner = pack(devices, pattern, block_values)
    from_outer = to_outer(outer)
    outer_own = to_outer(own)
    from_inner, inner_own = to_inner(inner), to_inner(own)

    s_inner, s_from_inner, own_part, outer_part = call(
        inner_kernel, (own, inner, outer, from_inner, inner_own), (low, low, high, high)
    )
    s_own, s_head, s_tail, from_outer_part, cube_part, inner_part = call(
        square_kernel,
        (own, inner, outer, from_outer, s_inner, s_from_inner, own_part),
        (low, low_of(rb - 1), low_of(1), high, high, high),
    )
    s_outer_head, s_outer_tail = to_outer(s_head), to_outer(s_tail)
    s_inner_own = to_inner(s_own)
    out, rest = call(
        late_kernel,
        (
            own, outer, inner, outer_own, from_outer, s_own, s_inner_own, outer_part, from_outer_part, cube_part,
            inner_part,
        ),
        (full, high),
        4,
    )
    (out,) = call(functools.partial(last_kernel, 0), (outer, s_outer_head, rest), (full,), 1, into=out)
    (out,) = call(functools.partial(last_kernel, rb - 1), (outer, s_outer_tail, rest), (full,), 1, into=out)
    return out


def solution(mesh):
    return jax.shard_map(
        functools.partial(local, mesh.shape["grid"]),
        mesh=mesh,
        in_specs=(P(("parts", "grid"), None, None, None), P("parts", None)),
        out_specs=P(("parts", "grid"), None, None, None),
        check_vma=False,
    )
```

time: 94.1 us -> 84.5 us (0.90)
  Pallas kernels: 33.3 us -> 27.9 us
  local copies, waits for them, and re-layouts: 2.65 us -> 0.01 us
  waiting for transfers between devices: 52.8 us -> 51.2 us
    pallas_call x1, Pallas kernels: 6.97 us -> 2.06 us  [pack(): pl.pallas_call(functools.partial(pack_kernel, devices, rb, bs), out_shape...]
    unnamed x3 -> x2, local copies, waits for them, and re-layouts: 2.65 us -> 0.01 us
    ppermute x3 -> x4, waiting for transfers between devices: 51.4 us -> 49.8 us  [local(): to_outer = lambda x: lax.ppermute(x, 'grid', over)]
    pallas_call x4 -> x5, Pallas kernels: 26.3 us -> 25.8 us  [call(): pl.pallas_call(functools.partial(kernel, devices, rb, bs), out_shape=outs...]
    ppermute x3 -> x4, starting transfers between devices: 4.47 us -> 4.55 us  [local(): to_outer = lambda x: lax.ppermute(x, 'grid', over)]
  transfers between devices with their start and end apart: 6 -> 7, of which waited for: 3 -> 5; matrix products, arithmetic and copies ran while one was open for 0% -> 0% of each run, Pallas kernels for 24% -> 28%
where the time goes in v2:
time: 84.5 us; the launch traced here: 84.3 us
  waiting for transfers between devices  51.2 us (61%)
  Pallas kernels  27.9 us (33%)
  starting transfers between devices  5.2 us (6%)
    ppermute x4, waiting for transfers between devices, local(): to_outer = lambda x: lax.ppermute(x, 'grid', over)  49.8 us
    pallas_call x5, Pallas kernels, call(): pl.pallas_call(functools.partial(kernel, devices, rb, bs), out_shape=outs...  25.8 us
    ppermute x4, starting transfers between devices, local(): to_outer = lambda x: lax.ppermute(x, 'grid', over)  4.55 us
    pallas_call x1, Pallas kernels, pack(): pl.pallas_call(functools.partial(pack_kernel, devices, rb, bs), out_shape...  2.06 us
  transfers between devices with their start and end apart: 7, of which 5 were waited for; matrix products, arithmetic and copies ran while one was open for 0% of the time, Pallas kernels for 28%

profile of v2, /device:TPU:1, one launch (start us, length us, event | category | flops | bytes accessed | tf_op | source)
XLA Modules:
  0.0 84.3 jit_solution(17352658963605728835)
XLA Ops:
  0.0 0.0 copy-start
  0.0 2.1 %pack.1 = (bf16[3,768,256]{2,1,0:T(8,128)(2,1)S(1)}, bf16[3,768,256]{2,1,0:T(8,128)(2,1)S(1)}, bf16[3,768,256]{2,1,0:T(8,128)(2,1)S(1)}) custom-call(s32[8,48]{1,0:T(8,128)} %bitcast.1, bf16[3,8,256,256]{3,2,1,0:T(8,128)(2,1)} %blocks.1), custom_call_target="tpu_custom_call" | custom-call | flops 1 | bytes 1 | tf_op jit(solution)/shard_map/pack/pallas_call | solution.py:76
  2.1 0.1 collective-permute-start.1
  2.2 0.5 collective-permute-start.2
  2.6 2.6 %collective-permute-start = (bf16[3,768,256]{2,1,0:T(8,128)(2,1)S(1)}, bf16[3,768,256]{2,1,0:T(8,128)(2,1)S(1)}, u32[]{:S(2)}, u32[]{:S(2)}) collective-permute-start(bf16[3,768,256]{2,1,0:T(8,128)(2,1)S(1)} %get-tuple-element.20.outer), channel_id=1, source_target_pairs={{0,15},{1,2},{2,1},{3,4},{4,3},{5,6},{6,5},{7,8},{8,7},{9,10},{10,... | collective-permute-start | bytes 3538952 | tf_op jit(solution)/shard_map/ppermute | solution.py:196
  5.3 0.0 collective-permute-start.4
  5.3 0.0 collective-permute-done.1.from_inner
  5.3 1.4 %collective-permute-done.2.inner_own = bf16[3,768,256]{2,1,0:T(8,128)(2,1)S(1)} collective-permute-done((bf16[3,768,256]{2,1,0:T(8,128)(2,1)S(1)}, bf16[3,768,256]{2,1,0:T(8,128)(2,1)S(1)}, u32[]{:S(2)}, u32[]{:S(2)}) %collective-permute-start.2) | collective-permute-done | bytes 1179680 | tf_op jit(solution)/shard_map/ppermute | solution.py:197
  6.7 0.0 copy-done
  6.7 7.8 %inner_kernel.1 = (bf16[3,768,256]{2,1,0:T(8,128)(2,1)S(1)}, bf16[3,768,256]{2,1,0:T(8,128)(2,1)S(1)}, f32[3,768,256]{2,1,0:T(8,128)S(1)}, f32[3,768,256]{2,1,0:T(8,128)S(1)}) custom-call(s32[8,48]{1,0:T(8,128)S(1)} %bitcast.2, bf16[3,768,256]{2,1,0:T(8,128)(2,1)S(1)} %get-tuple-element.21.own, bf16[3,768,256]{2,1,0:T(8,128)(2,1)S(1)} %get-tuple-element.22.inner, ...), custom_call_target="tpu_custom_call" | custom-call | flops 1 | bytes 1 | tf_op jit(solution)/shard_map/inner_kernel/pallas_call | solution.py:211
  14.5 29.9 %collective-permute-done.from_outer = bf16[3,768,256]{2,1,0:T(8,128)(2,1)S(1)} collective-permute-done((bf16[3,768,256]{2,1,0:T(8,128)(2,1)S(1)}, bf16[3,768,256]{2,1,0:T(8,128)(2,1)S(1)}, u32[]{:S(2)}, u32[]{:S(2)}) %collective-permute-start) | collective-permute-done | bytes 1179680 | tf_op jit(solution)/shard_map/ppermute | solution.py:196
  44.4 6.4 %square_kernel.1 = (bf16[3,768,256]{2,1,0:T(8,128)(2,1)S(1)}, bf16[2,768,256]{2,1,0:T(8,128)(2,1)S(1)}, bf16[1,768,256]{2,1,0:T(8,128)(2,1)S(1)}, f32[3,768,256]...) custom-call(s32[8,48]{1,0:T(8,128)S(1)} %bitcast.3, ...), custom_call_target="tpu_custom_call" | custom-call | flops 1 | bytes 1 | tf_op jit(solution)/shard_map/square_kernel/pallas_call | solution.py:211
  50.9 0.1 collective-permute-start.5
  51.0 1.8 %collective-permute-start.6 = (bf16[2,768,256]{2,1,0:T(8,128)(2,1)S(1)}, bf16[2,768,256]{2,1,0:T(8,128)(2,1)S(1)}, u32[]{:S(2)}, u32[]{:S(2)}) collective-permute-start(bf16[2,768,256]{2,1,0:T(8,128)(2,1)S(1)} %get-tuple-element.33), channel_id=1, source_target_pairs={{0,15},{1,2},{2,1},{3,4},{4,3},{5,6},{6,5},{7,8},{8,7},{9,10},{10,... | collective-permute-start | bytes 2359304 | tf_op jit(solution)/shard_map/ppermute | solution.py:196
  52.8 0.1 collective-permute-start.3
  52.8 16.9 %collective-permute-done.4.outer_own = bf16[3,768,256]{2,1,0:T(8,128)(2,1)S(1)} collective-permute-done((bf16[3,768,256]{2,1,0:T(8,128)(2,1)S(1)}, bf16[3,768,256]{2,1,0:T(8,128)(2,1)S(1)}, u32[]{:S(2)}, u32[]{:S(2)}) %collective-permute-start.4) | collective-permute-done | bytes 1179680 | tf_op jit(solution)/shard_map/ppermute | solution.py:196
  69.7 0.0 collective-permute-done.5.s_inner_own
  69.7 7.2 %late_kernel.1 = (bf16[3,8,256,256]{3,2,1,0:T(8,128)(2,1)}, f32[3,768,256]{2,1,0:T(8,128)S(1)}) custom-call(s32[8,48]{1,0:T(8,128)S(1)} %bitcast.4, bf16[3,768,256]{2,1,0:T(8,128)(2,1)S(1)} %get-tuple-element.21.own, bf16[3,768,256]{2,1,0:T(8,128)(2,1)S(1)} %get-tuple-element.20.outer, bf16[3,768,256]{2,1,0:T(8,128)(2,1)S(1)} %get-tuple-element.22.inner, ...), custom_call_target="tpu_custom_call" | custom-call | flops 1 | bytes 1 | tf_op jit(solution)/shard_map/late_kernel/pallas_call | solution.py:211
  76.9 1.2 %collective-permute-done.6.s_outer_own = bf16[2,768,256]{2,1,0:T(8,128)(2,1)S(1)} collective-permute-done((bf16[2,768,256]{2,1,0:T(8,128)(2,1)S(1)}, bf16[2,768,256]{2,1,0:T(8,128)(2,1)S(1)}, u32[]{:S(2)}, u32[]{:S(2)}) %collective-permute-start.6) | collective-permute-done | bytes 786464 | tf_op jit(solution)/shard_map/ppermute | solution.py:196
  78.1 2.4 %last_kernel.2._ = bf16[3,8,256,256]{3,2,1,0:T(8,128)(2,1)} custom-call(s32[8,48]{1,0:T(8,128)S(1)} %bitcast.5, bf16[3,768,256]{2,1,0:T(8,128)(2,1)S(1)} %get-tuple-element.20.outer, bf16[2,768,256]{2,1,0:T(8,128)(2,1)S(1)} %collective-permute-done.6.s_outer_own, f32[3,768,256]{2,1,0:T(8,128)S(1)} %get-tuple-element.32.rest, ...), custom_call_target="tpu_custom_call", output_to_operand_aliasing={{}: (4, {})} | custom-call | flops 1 | bytes 1 | tf_op jit(solution)/shard_map/last_kernel/pallas_call | solution.py:211
  80.6 1.8 %collective-permute-done.3.s_outer_own = bf16[1,768,256]{2,1,0:T(8,128)(2,1)S(1)} collective-permute-done((bf16[1,768,256]{2,1,0:T(8,128)(2,1)S(1)}, bf16[1,768,256]{2,1,0:T(8,128)(2,1)S(1)}, u32[]{:S(2)}, u32[]{:S(2)}) %collective-permute-start.3) | collective-permute-done | bytes 393248 | tf_op jit(solution)/shard_map/ppermute | solution.py:196
  82.4 2.0 %last_kernel.3 = bf16[3,8,256,256]{3,2,1,0:T(8,128)(2,1)} custom-call(s32[8,48]{1,0:T(8,128)S(1)} %bitcast.6, bf16[3,768,256]{2,1,0:T(8,128)(2,1)S(1)} %get-tuple-element.20.outer, bf16[1,768,256]{2,1,0:T(8,128)(2,1)S(1)} %collective-permute-done.3.s_outer_own, f32[3,768,256]{2,1,0:T(8,128)S(1)} %get-tuple-element.32.rest, ...), custom_call_target="tpu_custom_call", output_to_operand_aliasing={{}: (4, {})} | custom-call | flops 1 | bytes 1 | tf_op jit(solution)/shard_map/last_kernel/pallas_call | solution.py:211
Async XLA Ops:
  0.0 6.7 %copy-start = (s32[48,8]{0,1:T(8,128)S(1)}, s32[48,8]{0,1:T(8,128)}, u32[]{:S(2)}) copy-start(s32[48,8]{0,1:T(8,128)} %param.3) | copy-start | bytes 4612
  2.1 3.2 %collective-permute-start.1 = (bf16[3,768,256]{2,1,0:T(8,128)(2,1)S(1)}, bf16[3,768,256]{2,1,0:T(8,128)(2,1)S(1)}, u32[]{:S(2)}, u32[]{:S(2)}) collective-permute-start(bf16[3,768,256]{2,1,0:T(8,128)(2,1)S(1)} %get-tuple-element.22.inner), channel_id=1, source_target_pairs={{0,1},{1,0},{2,3},{3,2},{4,5},{5,4},{6,7},{7,6},{8,9},{9,8},{10,11... | collective-permute-start | bytes 3538952 | tf_op jit(solution)/shard_map/ppermute | solution.py:197
  2.2 4.5 %collective-permute-start.2 = (bf16[3,768,256]{2,1,0:T(8,128)(2,1)S(1)}, bf16[3,768,256]{2,1,0:T(8,128)(2,1)S(1)}, u32[]{:S(2)}, u32[]{:S(2)}) collective-permute-start(bf16[3,768,256]{2,1,0:T(8,128)(2,1)S(1)} %get-tuple-element.21.own), channel_id=1, source_target_pairs={{0,1},{1,0},{2,3},{3,2},{4,5},{5,4},{6,7},{7,6},{8,9},{9,8},{10,11... | collective-permute-start | bytes 3538952 | tf_op jit(solution)/shard_map/ppermute | solution.py:197
  2.6 41.8 %collective-permute-start = (bf16[3,768,256]{2,1,0:T(8,128)(2,1)S(1)}, bf16[3,768,256]{2,1,0:T(8,128)(2,1)S(1)}, u32[]{:S(2)}, u32[]{:S(2)}) collective-permute-start(bf16[3,768,256]{2,1,0:T(8,128)(2,1)S(1)} %get-tuple-element.20.outer), channel_id=1, source_target_pairs={{0,15},{1,2},{2,1},{3,4},{4,3},{5,6},{6,5},{7,8},{8,7},{9,10},{10,... | collective-permute-start | bytes 3538952 | tf_op jit(solution)/shard_map/ppermute | solution.py:196
  5.3 64.4 %collective-permute-start.4 = (bf16[3,768,256]{2,1,0:T(8,128)(2,1)S(1)}, bf16[3,768,256]{2,1,0:T(8,128)(2,1)S(1)}, u32[]{:S(2)}, u32[]{:S(2)}) collective-permute-start(bf16[3,768,256]{2,1,0:T(8,128)(2,1)S(1)} %get-tuple-element.21.own), channel_id=1, source_target_pairs={{0,15},{1,2},{2,1},{3,4},{4,3},{5,6},{6,5},{7,8},{8,7},{9,10},{10,... | collective-permute-start | bytes 3538952 | tf_op jit(solution)/shard_map/ppermute | solution.py:196
  50.9 18.8 %collective-permute-start.5 = (bf16[3,768,256]{2,1,0:T(8,128)(2,1)S(1)}, bf16[3,768,256]{2,1,0:T(8,128)(2,1)S(1)}, u32[]{:S(2)}, u32[]{:S(2)}) collective-permute-start(bf16[3,768,256]{2,1,0:T(8,128)(2,1)S(1)} %get-tuple-element.27.s_own), channel_id=1, source_target_pairs={{0,1},{1,0},{2,3},{3,2},{4,5},{5,4},{6,7},{7,6},{8,9},{9,8},{10,11... | collective-permute-start | bytes 3538952 | tf_op jit(solution)/shard_map/ppermute | solution.py:197
  51.0 27.2 %collective-permute-start.6 = (bf16[2,768,256]{2,1,0:T(8,128)(2,1)S(1)}, bf16[2,768,256]{2,1,0:T(8,128)(2,1)S(1)}, u32[]{:S(2)}, u32[]{:S(2)}) collective-permute-start(bf16[2,768,256]{2,1,0:T(8,128)(2,1)S(1)} %get-tuple-element.33), channel_id=1, source_target_pairs={{0,15},{1,2},{2,1},{3,4},{4,3},{5,6},{6,5},{7,8},{8,7},{9,10},{10,... | collective-permute-start | bytes 2359304 | tf_op jit(solution)/shard_map/ppermute | solution.py:196
  52.8 29.6 %collective-permute-start.3 = (bf16[1,768,256]{2,1,0:T(8,128)(2,1)S(1)}, bf16[1,768,256]{2,1,0:T(8,128)(2,1)S(1)}, u32[]{:S(2)}, u32[]{:S(2)}) collective-permute-start(bf16[1,768,256]{2,1,0:T(8,128)(2,1)S(1)} %get-tuple-element.26), channel_id=1, source_target_pairs={{0,15},{1,2},{2,1},{3,4},{4,3},{5,6},{6,5},{7,8},{8,7},{9,10},{10,... | collective-permute-start | bytes 1179656 | tf_op jit(solution)/shard_map/ppermute | solution.py:196

commit v3 on v2

--- a/solution.py
+++ b/solution.py
@@ -59,14 +59,14 @@
         load.start()
     me, other, partner = neighbours(devices)
     fetch.wait()
+    slots = [
+        [[slot_of(pattern, me * rb + r, column_device * rb + j) for j in range(rb)] for r in range(rb)]
+        for column_device in (other, me, partner)
+    ]
     for r in range(rb):
-        slots = [
-            [slot_of(pattern, me * rb + r, column_device * rb + j) for j in range(rb)]
-            for column_device in (other, me, partner)
-        ]
         loads[r].wait()
-        for cut, row in zip(cuts, slots):
-            for j, slot in enumerate(row):
+        for cut, rows in zip(cuts, slots):
+            for j, slot in enumerate(rows[r]):
                 block = held[r, jnp.maximum(slot, 0)]
                 cut[j, pl.ds(r * bs, bs), :] = jnp.where(slot >= 0, block, jnp.zeros_like(block))
 
@@ -110,8 +110,29 @@
         pl.when(slot >= 0)(copy.wait)
 
 
-def inner_kernel(
-    devices, rb, bs, pattern, own, inner, outer, from_inner, inner_own, s_inner, s_from_inner, own_part, outer_part
+def outer_kernel(devices, rb, bs, pattern, outer, from_outer, own_part):
+    @pl.loop(0, rb)
+    def _(c):
+        own_part[c] = panel_product(outer, from_outer, c, rb, bs)
+
+
+def square_kernel(devices, rb, bs, pattern, own, inner, from_inner, own_part, s_own, s_head, s_tail):
+    me, _, _ = neighbours(devices)
+
+    @pl.loop(0, rb)
+    def _(c):
+        s_own[c] = (
+            own_part[c] + panel_product(own, own, c, rb, bs) + panel_product(inner, from_inner, c, rb, bs)
+        ).astype(BF16)
+
+    drop_absent(s_own, pattern, me, me, rb, bs)
+    s_head[...] = s_own[pl.ds(0, rb - 1)]
+    s_tail[...] = s_own[pl.ds(rb - 1, 1)]
+
+
+def early_kernel(
+    devices, rb, bs, pattern, own, inner, outer, from_inner, inner_own, from_outer, s_own,
+    cube_part, inner_part, from_outer_part, outer_part, s_inner, s_from_inner, sems,
 ):
     me, _, partner = neighbours(devices)
 
@@ -121,43 +142,23 @@
         s_from_inner[c] = (
             panel_product(from_inner, own, c, rb, bs) + panel_product(inner_own, from_inner, c, rb, bs)
         ).astype(BF16)
-        own_part[c] = panel_product(own, own, c, rb, bs) + panel_product(inner, from_inner, c, rb, bs)
+        from_outer_part[c] = panel_product(from_outer, own, c, rb, bs)
         outer_part[c] = panel_product(own, outer, c, rb, bs)
 
     drop_absent(s_inner, pattern, me, partner, rb, bs)
     drop_absent(s_from_inner, pattern, partner, me, rb, bs)
 
-
-def square_kernel(
-    devices, rb, bs, pattern, own, inner, outer, from_outer, s_inner, s_from_inner, own_part,
-    s_own, s_head, s_tail, from_outer_part, cube_part, inner_part,
-):
-    me, _, _ = neighbours(devices)
-
-    @pl.loop(0, rb)
-    def _(c):
-        s_own[c] = (own_part[c] + panel_product(outer, from_outer, c, rb, bs)).astype(BF16)
-
-    drop_absent(s_own, pattern, me, me, rb, bs)
-    s_head[...] = s_own[pl.ds(0, rb - 1)]
-    s_tail[...] = s_own[pl.ds(rb - 1, 1)]
-
-    @pl.loop(0, rb)
-    def _(c):
-        from_outer_part[c] = panel_product(from_outer, own, c, rb, bs)
+    @pl.loop(0, rb)
+    def _(c):
         cube_part[c] = panel_product(own, s_own, c, rb, bs) + panel_product(inner, s_from_inner, c, rb, bs)
         inner_part[c] = 3.0 * s_inner[c].astype(F32) - 2.0 * panel_product(own, s_inner, c, rb, bs)
 
 
 def late_kernel(
-    devices, rb, bs, pattern, own, outer, inner, outer_own, from_outer, s_own, s_inner_own, outer_part,
-    from_outer_part, cube_part, inner_part, out, rest, s_outer, s_from_outer, out_own, out_inner, sems,
+    devices, rb, bs, pattern, own, outer, outer_own, from_outer, s_own, outer_part, from_outer_part, cube_part,
+    out, rest, s_outer, s_from_outer, out_own, sems,
 ):
-    me, other, partner = neighbours(devices)
-    waits = []
-    for c in range(rb):
-        out_inner[c] = (inner_part[c] - 2.0 * panel_product(inner, s_inner_own, c, rb, bs)).astype(BF16)
-        waits += scatter(out, pattern, me, partner, out_inner, c, sems, 0, rb, bs)
+    me, other, _ = neighbours(devices)
 
     @pl.loop(0, rb)
     def _(c):
@@ -166,10 +167,11 @@
 
     drop_absent(s_outer, pattern, me, other, rb, bs)
     drop_absent(s_from_outer, pattern, other, me, rb, bs)
+    waits = []
     for c in range(rb):
         cube = cube_part[c] + panel_product(outer, s_from_outer, c, rb, bs)
         out_own[c] = (3.0 * s_own[c].astype(F32) - 2.0 * cube).astype(BF16)
-        waits += scatter(out, pattern, me, me, out_own, c, sems, rb * rb, rb, bs)
+        waits += scatter(out, pattern, me, me, out_own, c, sems, 0, rb, bs)
 
     @pl.loop(0, rb)
     def _(c):
@@ -178,14 +180,31 @@
     settle(waits)
 
 
-def last_kernel(first, devices, rb, bs, pattern, outer, s_outer_own, rest, _, out, out_outer, sems):
-    me, other, _ = neighbours(devices)
+def finish(devices, rb, bs, pattern, column_device, first, left, right, part, out, panels, sems, base):
+    me = lax.axis_index("grid")
     waits = []
-    for c in range(s_outer_own.shape[0]):
-        cube = panel_product(outer, s_outer_own, c, rb, bs)
-        out_outer[first + c] = (rest[first + c] - 2.0 * cube).astype(BF16)
-        waits += scatter(out, pattern, me, other, out_outer, first + c, sems, 0, rb, bs)
+    for c in range(right.shape[0]):
+        cube = panel_product(left, right, c, rb, bs)
+        panels[first + c] = (part[first + c] - 2.0 * cube).astype(BF16)
+        waits += scatter(out, pattern, me, column_device, panels, first + c, sems, base, rb, bs)
+    return waits
+
+
+def head_kernel(
+    devices, rb, bs, pattern, outer, s_outer_head, rest, inner, s_inner_own, inner_part, _,
+    out, out_outer, out_inner, sems,
+):
+    _, other, partner = neighbours(devices)
+    waits = finish(devices, rb, bs, pattern, other, 0, outer, s_outer_head, rest, out, out_outer, sems, 0)
+    waits += finish(
+        devices, rb, bs, pattern, partner, 0, inner, s_inner_own, inner_part, out, out_inner, sems, rb * rb
+    )
     settle(waits)
+
+
+def tail_kernel(devices, rb, bs, pattern, outer, s_outer_tail, rest, _, out, out_outer, sems):
+    _, other, _ = neighbours(devices)
+    settle(finish(devices, rb, bs, pattern, other, rb - 1, outer, s_outer_tail, rest, out, out_outer, sems, 0))
 
 
 def local(devices, block_values, pattern):
@@ -217,7 +236,7 @@
             input_output_aliases=aliases,
             compiler_params=pltpu.CompilerParams(vmem_limit_bytes=VMEM_LIMIT),
             cost_estimate=BRIEF,
-            name=getattr(kernel, "func", kernel).__name__,
+            name=kernel.__name__,
         )(*operands)
 
     outer, own, inner = pack(devices, pattern, block_values)
@@ -225,27 +244,23 @@
     outer_own = to_outer(own)
     from_inner, inner_own = to_inner(inner), to_inner(own)
 
-    s_inner, s_from_inner, own_part, outer_part = call(
-        inner_kernel, (own, inner, outer, from_inner, inner_own), (low, low, high, high)
-    )
-    s_own, s_head, s_tail, from_outer_part, cube_part, inner_part = call(
-        square_kernel,
-        (own, inner, outer, from_outer, s_inner, s_from_inner, own_part),
-        (low, low_of(rb - 1), low_of(1), high, high, high),
-    )
+    (own_part,) = call(outer_kernel, (outer, from_outer), (high,))
+    s_own, s_head, s_tail = call(square_kernel, (own, inner, from_inner, own_part), (low, low_of(rb - 1), low_of(1)))
     s_outer_head, s_outer_tail = to_outer(s_head), to_outer(s_tail)
     s_inner_own = to_inner(s_own)
+    cube_part, inner_part, from_outer_part, outer_part = call(
+        early_kernel, (own, inner, outer, from_inner, inner_own, from_outer, s_own), (high,) * 4, 2
+    )
     out, rest = call(
         late_kernel,
-        (
-            own, outer, inner, outer_own, from_outer, s_own, s_inner_own, outer_part, from_outer_part, cube_part,
-            inner_part,
-        ),
+        (own, outer, outer_own, from_outer, s_own, outer_part, from_outer_part, cube_part),
         (full, high),
-        4,
-    )
-    (out,) = call(functools.partial(last_kernel, 0), (outer, s_outer_head, rest), (full,), 1, into=out)
-    (out,) = call(functools.partial(last_kernel, rb - 1), (outer, s_outer_tail, rest), (full,), 1, into=out)
+        3,
+    )
+    (out,) = call(
+        head_kernel, (outer, s_outer_head, rest, inner, s_inner_own, inner_part), (full,), 2, into=out
+    )
+    (out,) = call(tail_kernel, (outer, s_outer_tail, rest), (full,), 1, into=out)
     return out
 
 

time: 84.5 us -> 84 us (level)
  waiting for transfers between devices: 51.2 us -> 47.3 us
  starting transfers between devices: 5.2 us -> 7.52 us
  Pallas kernels: 27.9 us -> 28.9 us
    ppermute x4, waiting for transfers between devices: 49.8 us -> 47.3 us  [local(): to_outer = lambda x: lax.ppermute(x, 'grid', over)]
    ppermute x3, starting transfers between devices: 0.65 us -> 2.95 us  [local(): to_inner = lambda x: lax.ppermute(x, 'grid', across)]
    ppermute x3, waiting for transfers between devices: 1.36 us -> 0.01 us  [local(): to_inner = lambda x: lax.ppermute(x, 'grid', across)]
    pallas_call x5 -> x6, Pallas kernels: 25.8 us -> 26.8 us  [call(): pl.pallas_call(functools.partial(kernel, devices, rb, bs), out_shape=outs...]
  transfers between devices with their start and end apart: 7 -> 7, of which waited for: 5 -> 4; matrix products, arithmetic and copies ran while one was open for 0% -> 0% of each run, Pallas kernels for 28% -> 30%
where the time goes in v3:
time: 84 us; the launch traced here: 83.8 us
  waiting for transfers between devices  47.3 us (56%)
  Pallas kernels  28.9 us (34%)
  starting transfers between devices  7.52 us (9%)
    ppermute x4, waiting for transfers between devices, local(): to_outer = lambda x: lax.ppermute(x, 'grid', over)  47.3 us
    pallas_call x6, Pallas kernels, call(): pl.pallas_call(functools.partial(kernel, devices, rb, bs), out_shape=outs...  26.8 us
    ppermute x4, starting transfers between devices, local(): to_outer = lambda x: lax.ppermute(x, 'grid', over)  4.58 us
    ppermute x3, starting transfers between devices, local(): to_inner = lambda x: lax.ppermute(x, 'grid', across)  2.95 us
    pallas_call x1, Pallas kernels, pack(): pl.pallas_call(functools.partial(pack_kernel, devices, rb, bs), out_shape...  2.06 us
  transfers between devices with their start and end apart: 7, of which 4 were waited for; matrix products, arithmetic and copies ran while one was open for 0% of the time, Pallas kernels for 30%

profile of v3, /device:TPU:1, one launch (start us, length us, event | category | flops | bytes accessed | tf_op | source)
XLA Modules:
  0.0 83.8 jit_solution(11453860493980089795)
XLA Ops:
  0.0 0.0 copy-start
  0.0 2.1 %pack.1 = (bf16[3,768,256]{2,1,0:T(8,128)(2,1)S(1)}, bf16[3,768,256]{2,1,0:T(8,128)(2,1)S(1)}, bf16[3,768,256]{2,1,0:T(8,128)(2,1)S(1)}) custom-call(s32[8,48]{1,0:T(8,128)} %bitcast.1, bf16[3,8,256,256]{3,2,1,0:T(8,128)(2,1)} %blocks.1), custom_call_target="tpu_custom_call" | custom-call | flops 1 | bytes 1 | tf_op jit(solution)/shard_map/pack/pallas_call | solution.py:76
  2.1 2.7 %collective-permute-start.1 = (bf16[3,768,256]{2,1,0:T(8,128)(2,1)S(1)}, bf16[3,768,256]{2,1,0:T(8,128)(2,1)S(1)}, u32[]{:S(2)}, u32[]{:S(2)}) collective-permute-start(bf16[3,768,256]{2,1,0:T(8,128)(2,1)S(1)} %get-tuple-element.17.outer), channel_id=1, source_target_pairs={{0,15},{1,2},{2,1},{3,4},{4,3},{5,6},{6,5},{7,8},{8,7},{9,10},{10,... | collective-permute-start | bytes 3538952 | tf_op jit(solution)/shard_map/ppermute | solution.py:215
  4.8 2.9 %collective-permute-start = (bf16[3,768,256]{2,1,0:T(8,128)(2,1)S(1)}, bf16[3,768,256]{2,1,0:T(8,128)(2,1)S(1)}, u32[]{:S(2)}, u32[]{:S(2)}) collective-permute-start(bf16[3,768,256]{2,1,0:T(8,128)(2,1)S(1)} %get-tuple-element.19.inner), channel_id=1, source_target_pairs={{0,1},{1,0},{2,3},{3,2},{4,5},{5,4},{6,7},{7,6},{8,9},{9,8},{10,11... | collective-permute-start | bytes 3538952 | tf_op jit(solution)/shard_map/ppermute | solution.py:216
  7.6 0.0 collective-permute-start.4
  7.6 0.0 collective-permute-start.3
  7.6 36.3 %collective-permute-done.1.from_outer = bf16[3,768,256]{2,1,0:T(8,128)(2,1)S(1)} collective-permute-done((bf16[3,768,256]{2,1,0:T(8,128)(2,1)S(1)}, bf16[3,768,256]{2,1,0:T(8,128)(2,1)S(1)}, u32[]{:S(2)}, u32[]{:S(2)}) %collective-permute-start.1) | collective-permute-done | bytes 1179680 | tf_op jit(solution)/shard_map/ppermute | solution.py:215
  43.9 0.0 copy-done
  43.9 2.0 %outer_kernel.1.own_part = f32[3,768,256]{2,1,0:T(8,128)S(1)} custom-call(s32[8,48]{1,0:T(8,128)S(1)} %bitcast.2, bf16[3,768,256]{2,1,0:T(8,128)(2,1)S(1)} %get-tuple-element.17.outer, bf16[3,768,256]{2,1,0:T(8,128)(2,1)S(1)} %collective-permute-done.1.from_outer), custom_call_target="tpu_custom_call" | custom-call | flops 1 | bytes 1 | tf_op jit(solution)/shard_map/outer_kernel/pallas_call | solution.py:230
  46.0 0.0 collective-permute-done.from_inner
  46.0 3.2 %square_kernel.1 = (bf16[3,768,256]{2,1,0:T(8,128)(2,1)S(1)}, bf16[2,768,256]{2,1,0:T(8,128)(2,1)S(1)}, bf16[1,768,256]{2,1,0:T(8,128)(2,1)S(1)}) custom-call(s32[8,48]{1,0:T(8,128)S(1)} %bitcast.3, bf16[3,768,256]{2,1,0:T(8,128)(2,1)S(1)} %get-tuple-element.18.own, bf16[3,768,256]{2,1,0:T(8,128)(2,1)S(1)} %get-tuple-element.19.inner, ...), custom_call_target="tpu_custom_call" | custom-call | flops 1 | bytes 1 | tf_op jit(solution)/shard_map/square_kernel/pallas_call | solution.py:230
  49.1 0.1 collective-permute-start.6
  49.2 1.8 %collective-permute-start.5 = (bf16[2,768,256]{2,1,0:T(8,128)(2,1)S(1)}, bf16[2,768,256]{2,1,0:T(8,128)(2,1)S(1)}, u32[]{:S(2)}, u32[]{:S(2)}) collective-permute-start(bf16[2,768,256]{2,1,0:T(8,128)(2,1)S(1)} %get-tuple-element.26), channel_id=1, source_target_pairs={{0,15},{1,2},{2,1},{3,4},{4,3},{5,6},{6,5},{7,8},{8,7},{9,10},{10,... | collective-permute-start | bytes 2359304 | tf_op jit(solution)/shard_map/ppermute | solution.py:215
  51.0 0.1 collective-permute-start.2
  51.1 0.0 collective-permute-done.4.inner_own
  51.1 10.3 %early_kernel.1 = (f32[3,768,256]{2,1,0:T(8,128)S(1)}, f32[3,768,256]{2,1,0:T(8,128)S(1)}, f32[3,768,256]{2,1,0:T(8,128)S(1)}, f32[3,768,256]{2,1,0:T(8,128)S(1)}) custom-call(s32[8,48]{1,0:T(8,128)S(1)} %bitcast.4, bf16[3,768,256]{2,1,0:T(8,128)(2,1)S(1)} %get-tuple-element.18.own, bf16[3,768,256]{2,1,0:T(8,128)(2,1)S(1)} %get-tuple-element.19.inner, ...), custom_call_target="tpu_custom_call" | custom-call | flops 1 | bytes 1 | tf_op jit(solution)/shard_map/early_kernel/pallas_call | solution.py:230
  61.4 7.8 %collective-permute-done.3.outer_own = bf16[3,768,256]{2,1,0:T(8,128)(2,1)S(1)} collective-permute-done((bf16[3,768,256]{2,1,0:T(8,128)(2,1)S(1)}, bf16[3,768,256]{2,1,0:T(8,128)(2,1)S(1)}, u32[]{:S(2)}, u32[]{:S(2)}) %collective-permute-start.3) | collective-permute-done | bytes 1179680 | tf_op jit(solution)/shard_map/ppermute | solution.py:215
  69.2 6.1 %late_kernel.1 = (bf16[3,8,256,256]{3,2,1,0:T(8,128)(2,1)}, f32[3,768,256]{2,1,0:T(8,128)S(1)}) custom-call(s32[8,48]{1,0:T(8,128)S(1)} %bitcast.5, bf16[3,768,256]{2,1,0:T(8,128)(2,1)S(1)} %get-tuple-element.18.own, bf16[3,768,256]{2,1,0:T(8,128)(2,1)S(1)} %get-tuple-element.17.outer, bf16[3,768,256]{2,1,0:T(8,128)(2,1)S(1)} %collective-permute-done.3.outer_own, ...), custom_call_target="tpu_custom_call" | custom-call | flops 1 | bytes 1 | tf_op jit(solution)/shard_map/late_kernel/pallas_call | solution.py:230
  75.3 2.4 %collective-permute-done.5.s_outer_head = bf16[2,768,256]{2,1,0:T(8,128)(2,1)S(1)} collective-permute-done((bf16[2,768,256]{2,1,0:T(8,128)(2,1)S(1)}, bf16[2,768,256]{2,1,0:T(8,128)(2,1)S(1)}, u32[]{:S(2)}, u32[]{:S(2)}) %collective-permute-start.5) | collective-permute-done | bytes 786464 | tf_op jit(solution)/shard_map/ppermute | solution.py:215
  77.6 0.0 collective-permute-done.6.s_inner_own
  77.6 3.3 %head_kernel.1._ = bf16[3,8,256,256]{3,2,1,0:T(8,128)(2,1)} custom-call(s32[8,48]{1,0:T(8,128)S(1)} %bitcast.6, bf16[3,768,256]{2,1,0:T(8,128)(2,1)S(1)} %get-tuple-element.17.outer, bf16[2,768,256]{2,1,0:T(8,128)(2,1)S(1)} %collective-permute-done.5.s_outer_head, f32[3,768,256]{2,1,0:T(8,128)S(1)} %get-tuple-element.25.rest, ...), custom_call_target="tpu_custom_call", output_to_operand_aliasing={{}: (7, {})} | custom-call | flops 1 | bytes 1 | tf_op jit(solution)/shard_map/head_kernel/pallas_call | solution.py:230
  80.9 0.9 %collective-permute-done.2.s_outer_tail = bf16[1,768,256]{2,1,0:T(8,128)(2,1)S(1)} collective-permute-done((bf16[1,768,256]{2,1,0:T(8,128)(2,1)S(1)}, bf16[1,768,256]{2,1,0:T(8,128)(2,1)S(1)}, u32[]{:S(2)}, u32[]{:S(2)}) %collective-permute-start.2) | collective-permute-done | bytes 393248 | tf_op jit(solution)/shard_map/ppermute | solution.py:215
  81.8 2.0 %tail_kernel.1 = bf16[3,8,256,256]{3,2,1,0:T(8,128)(2,1)} custom-call(s32[8,48]{1,0:T(8,128)S(1)} %bitcast.7, bf16[3,768,256]{2,1,0:T(8,128)(2,1)S(1)} %get-tuple-element.17.outer, bf16[1,768,256]{2,1,0:T(8,128)(2,1)S(1)} %collective-permute-done.2.s_outer_tail, f32[3,768,256]{2,1,0:T(8,128)S(1)} %get-tuple-element.25.rest, ...), custom_call_target="tpu_custom_call", output_to_operand_aliasing={{}: (4, {})} | custom-call | flops 1 | bytes 1 | tf_op jit(solution)/shard_map/tail_kernel/pallas_call | solution.py:230
Async XLA Ops:
  0.0 43.9 %copy-start = (s32[48,8]{0,1:T(8,128)S(1)}, s32[48,8]{0,1:T(8,128)}, u32[]{:S(2)}) copy-start(s32[48,8]{0,1:T(8,128)} %param.3) | copy-start | bytes 4612
  2.1 41.9 %collective-permute-start.1 = (bf16[3,768,256]{2,1,0:T(8,128)(2,1)S(1)}, bf16[3,768,256]{2,1,0:T(8,128)(2,1)S(1)}, u32[]{:S(2)}, u32[]{:S(2)}) collective-permute-start(bf16[3,768,256]{2,1,0:T(8,128)(2,1)S(1)} %get-tuple-element.17.outer), channel_id=1, source_target_pairs={{0,15},{1,2},{2,1},{3,4},{4,3},{5,6},{6,5},{7,8},{8,7},{9,10},{10,... | collective-permute-start | bytes 3538952 | tf_op jit(solution)/shard_map/ppermute | solution.py:215
  4.8 41.2 %collective-permute-start = (bf16[3,768,256]{2,1,0:T(8,128)(2,1)S(1)}, bf16[3,768,256]{2,1,0:T(8,128)(2,1)S(1)}, u32[]{:S(2)}, u32[]{:S(2)}) collective-permute-start(bf16[3,768,256]{2,1,0:T(8,128)(2,1)S(1)} %get-tuple-element.19.inner), channel_id=1, source_target_pairs={{0,1},{1,0},{2,3},{3,2},{4,5},{5,4},{6,7},{7,6},{8,9},{9,8},{10,11... | collective-permute-start | bytes 3538952 | tf_op jit(solution)/shard_map/ppermute | solution.py:216
  7.6 43.5 %collective-permute-start.4 = (bf16[3,768,256]{2,1,0:T(8,128)(2,1)S(1)}, bf16[3,768,256]{2,1,0:T(8,128)(2,1)S(1)}, u32[]{:S(2)}, u32[]{:S(2)}) collective-permute-start(bf16[3,768,256]{2,1,0:T(8,128)(2,1)S(1)} %get-tuple-element.18.own), channel_id=1, source_target_pairs={{0,1},{1,0},{2,3},{3,2},{4,5},{5,4},{6,7},{7,6},{8,9},{9,8},{10,11... | collective-permute-start | bytes 3538952 | tf_op jit(solution)/shard_map/ppermute | solution.py:216
  7.6 61.6 %collective-permute-start.3 = (bf16[3,768,256]{2,1,0:T(8,128)(2,1)S(1)}, bf16[3,768,256]{2,1,0:T(8,128)(2,1)S(1)}, u32[]{:S(2)}, u32[]{:S(2)}) collective-permute-start(bf16[3,768,256]{2,1,0:T(8,128)(2,1)S(1)} %get-tuple-element.18.own), channel_id=1, source_target_pairs={{0,15},{1,2},{2,1},{3,4},{4,3},{5,6},{6,5},{7,8},{8,7},{9,10},{10,... | collective-permute-start | bytes 3538952 | tf_op jit(solution)/shard_map/ppermute | solution.py:215
  49.1 28.5 %collective-permute-start.6 = (bf16[3,768,256]{2,1,0:T(8,128)(2,1)S(1)}, bf16[3,768,256]{2,1,0:T(8,128)(2,1)S(1)}, u32[]{:S(2)}, u32[]{:S(2)}) collective-permute-start(bf16[3,768,256]{2,1,0:T(8,128)(2,1)S(1)} %get-tuple-element.21.s_own), channel_id=1, source_target_pairs={{0,1},{1,0},{2,3},{3,2},{4,5},{5,4},{6,7},{7,6},{8,9},{9,8},{10,11... | collective-permute-start | bytes 3538952 | tf_op jit(solution)/shard_map/ppermute | solution.py:216
  49.2 28.4 %collective-permute-start.5 = (bf16[2,768,256]{2,1,0:T(8,128)(2,1)S(1)}, bf16[2,768,256]{2,1,0:T(8,128)(2,1)S(1)}, u32[]{:S(2)}, u32[]{:S(2)}) collective-permute-start(bf16[2,768,256]{2,1,0:T(8,128)(2,1)S(1)} %get-tuple-element.26), channel_id=1, source_target_pairs={{0,15},{1,2},{2,1},{3,4},{4,3},{5,6},{6,5},{7,8},{8,7},{9,10},{10,... | collective-permute-start | bytes 2359304 | tf_op jit(solution)/shard_map/ppermute | solution.py:215
  51.0 30.8 %collective-permute-start.2 = (bf16[1,768,256]{2,1,0:T(8,128)(2,1)S(1)}, bf16[1,768,256]{2,1,0:T(8,128)(2,1)S(1)}, u32[]{:S(2)}, u32[]{:S(2)}) collective-permute-start(bf16[1,768,256]{2,1,0:T(8,128)(2,1)S(1)} %get-tuple-element.20), channel_id=1, source_target_pairs={{0,15},{1,2},{2,1},{3,4},{4,3},{5,6},{6,5},{7,8},{8,7},{9,10},{10,... | collective-permute-start | bytes 1179656 | tf_op jit(solution)/shard_map/ppermute | solution.py:215

commit v4 on v3

--- a/solution.py
+++ b/solution.py
@@ -156,9 +156,11 @@
 
 def late_kernel(
     devices, rb, bs, pattern, own, outer, outer_own, from_outer, s_own, outer_part, from_outer_part, cube_part,
-    out, rest, s_outer, s_from_outer, out_own, sems,
+    out, rest, slots, s_outer, s_from_outer, out_own, sems,
 ):
     me, other, _ = neighbours(devices)
+    for r in range(rb):
+        slots[r] = jnp.full(slots.shape[1:], slot_of(pattern, me * rb + r, other * rb + rb - 1))
 
     @pl.loop(0, rb)
     def _(c):
@@ -202,9 +204,19 @@
     settle(waits)
 
 
-def tail_kernel(devices, rb, bs, pattern, outer, s_outer_tail, rest, _, out, out_outer, sems):
-    _, other, _ = neighbours(devices)
-    settle(finish(devices, rb, bs, pattern, other, rb - 1, outer, s_outer_tail, rest, out, out_outer, sems, 0))
+def tail_kernel(devices, rb, bs, slots, outer, s_outer_tail, rest, _, out, panels, sems):
+    waits = []
+    for r in range(rb):
+        rows = pl.ds(r * bs, bs)
+        slot = jnp.max(slots[r])
+        cube = jnp.dot(outer[0, rows, :], s_outer_tail[0, pl.ds(0, bs), :], preferred_element_type=F32)
+        for k in range(1, rb):
+            cube += jnp.dot(outer[k, rows, :], s_outer_tail[0, pl.ds(k * bs, bs), :], preferred_element_type=F32)
+        panels[0, rows, :] = (rest[rb - 1, rows, :] - 2.0 * cube).astype(BF16)
+        copy = pltpu.make_async_copy(panels.at[0, rows, :], out.at[r, jnp.maximum(slot, 0)], sems.at[r])
+        pl.when(slot >= 0)(copy.start)
+        waits.append((slot, copy))
+    settle(waits)
 
 
 def local(devices, block_values, pattern):
@@ -251,17 +263,26 @@
     cube_part, inner_part, from_outer_part, outer_part = call(
         early_kernel, (own, inner, outer, from_inner, inner_own, from_outer, s_own), (high,) * 4, 2
     )
-    out, rest = call(
+    out, rest, slots = call(
         late_kernel,
         (own, outer, outer_own, from_outer, s_own, outer_part, from_outer_part, cube_part),
-        (full, high),
+        (full, high, jax.ShapeDtypeStruct((rb, 8, 128), jnp.int32)),
         3,
     )
     (out,) = call(
         head_kernel, (outer, s_outer_head, rest, inner, s_inner_own, inner_part), (full,), 2, into=out
     )
-    (out,) = call(tail_kernel, (outer, s_outer_tail, rest), (full,), 1, into=out)
-    return out
+    return pl.pallas_call(
+        functools.partial(tail_kernel, devices, rb, bs),
+        out_shape=full,
+        in_specs=[VMEM, VMEM, VMEM, VMEM, ANY],
+        out_specs=ANY,
+        scratch_shapes=[pltpu.VMEM((1, rb * bs, bs), BF16), pltpu.SemaphoreType.DMA((rb,))],
+        input_output_aliases={4: 0},
+        compiler_params=pltpu.CompilerParams(vmem_limit_bytes=VMEM_LIMIT),
+        cost_estimate=BRIEF,
+        name="tail_kernel",
+    )(slots, outer, s_outer_tail, rest, out)
 
 
 def solution(mesh):

time: 84 us -> 83.2 us (level)
    pallas_call x6 -> x5, Pallas kernels: 26.8 us -> 25 us  [call(): pl.pallas_call(functools.partial(kernel, devices, rb, bs), out_shape=outs...]
    pallas_call x0 -> x1, Pallas kernels: none -> 1.21 us  [local(): pl.pallas_call(functools.partial(tail_kernel, devices, rb, bs), out_shape...]
where the time goes in v4:
time: 83.2 us; the launch traced here: 83.1 us
  waiting for transfers between devices  47.2 us (57%)
  Pallas kernels  28.2 us (34%)
  starting transfers between devices  7.53 us (9%)
    ppermute x4, waiting for transfers between devices, local(): to_outer = lambda x: lax.ppermute(x, 'grid', over)  47.2 us
    pallas_call x5, Pallas kernels, call(): pl.pallas_call(functools.partial(kernel, devices, rb, bs), out_shape=outs...  25 us
    ppermute x4, starting transfers between devices, local(): to_outer = lambda x: lax.ppermute(x, 'grid', over)  4.58 us
    ppermute x3, starting transfers between devices, local(): to_inner = lambda x: lax.ppermute(x, 'grid', across)  2.95 us
    pallas_call x1, Pallas kernels, pack(): pl.pallas_call(functools.partial(pack_kernel, devices, rb, bs), out_shape...  2.06 us
  transfers between devices with their start and end apart: 7, of which 4 were waited for; matrix products, arithmetic and copies ran while one was open for 0% of the time, Pallas kernels for 30%

profile of v4, /device:TPU:1, one launch (start us, length us, event | category | flops | bytes accessed | tf_op | source)
XLA Modules:
  0.0 83.1 jit_solution(8094418746122457921)
XLA Ops:
  0.0 0.0 copy-start
  0.0 2.1 %pack.1 = (bf16[3,768,256]{2,1,0:T(8,128)(2,1)S(1)}, bf16[3,768,256]{2,1,0:T(8,128)(2,1)S(1)}, bf16[3,768,256]{2,1,0:T(8,128)(2,1)S(1)}) custom-call(s32[8,48]{1,0:T(8,128)} %bitcast.1, bf16[3,8,256,256]{3,2,1,0:T(8,128)(2,1)} %blocks.1), custom_call_target="tpu_custom_call" | custom-call | flops 1 | bytes 1 | tf_op jit(solution)/shard_map/pack/pallas_call | solution.py:76
  2.1 2.7 %collective-permute-start.1 = (bf16[3,768,256]{2,1,0:T(8,128)(2,1)S(1)}, bf16[3,768,256]{2,1,0:T(8,128)(2,1)S(1)}, u32[]{:S(2)}, u32[]{:S(2)}) collective-permute-start(bf16[3,768,256]{2,1,0:T(8,128)(2,1)S(1)} %get-tuple-element.19.outer), channel_id=1, source_target_pairs={{0,15},{1,2},{2,1},{3,4},{4,3},{5,6},{6,5},{7,8},{8,7},{9,10},{10,... | collective-permute-start | bytes 3538952 | tf_op jit(solution)/shard_map/ppermute | solution.py:227
  4.8 2.9 %collective-permute-start.2 = (bf16[3,768,256]{2,1,0:T(8,128)(2,1)S(1)}, bf16[3,768,256]{2,1,0:T(8,128)(2,1)S(1)}, u32[]{:S(2)}, u32[]{:S(2)}) collective-permute-start(bf16[3,768,256]{2,1,0:T(8,128)(2,1)S(1)} %get-tuple-element.20.inner), channel_id=1, source_target_pairs={{0,1},{1,0},{2,3},{3,2},{4,5},{5,4},{6,7},{7,6},{8,9},{9,8},{10,11... | collective-permute-start | bytes 3538952 | tf_op jit(solution)/shard_map/ppermute | solution.py:228
  7.6 0.0 collective-permute-start.3
  7.6 0.0 collective-permute-start
  7.6 36.3 %collective-permute-done.1.from_outer = bf16[3,768,256]{2,1,0:T(8,128)(2,1)S(1)} collective-permute-done((bf16[3,768,256]{2,1,0:T(8,128)(2,1)S(1)}, bf16[3,768,256]{2,1,0:T(8,128)(2,1)S(1)}, u32[]{:S(2)}, u32[]{:S(2)}) %collective-permute-start.1) | collective-permute-done | bytes 1179680 | tf_op jit(solution)/shard_map/ppermute | solution.py:227
  43.9 0.0 copy-done
  43.9 2.0 %outer_kernel.1.own_part = f32[3,768,256]{2,1,0:T(8,128)S(1)} custom-call(s32[8,48]{1,0:T(8,128)S(1)} %bitcast.2, bf16[3,768,256]{2,1,0:T(8,128)(2,1)S(1)} %get-tuple-element.19.outer, bf16[3,768,256]{2,1,0:T(8,128)(2,1)S(1)} %collective-permute-done.1.from_outer), custom_call_target="tpu_custom_call" | custom-call | flops 1 | bytes 1 | tf_op jit(solution)/shard_map/outer_kernel/pallas_call | solution.py:242
  46.0 0.0 collective-permute-done.2.from_inner
  46.0 3.2 %square_kernel.1 = (bf16[3,768,256]{2,1,0:T(8,128)(2,1)S(1)}, bf16[2,768,256]{2,1,0:T(8,128)(2,1)S(1)}, bf16[1,768,256]{2,1,0:T(8,128)(2,1)S(1)}) custom-call(s32[8,48]{1,0:T(8,128)S(1)} %bitcast.3, bf16[3,768,256]{2,1,0:T(8,128)(2,1)S(1)} %get-tuple-element.18.own, bf16[3,768,256]{2,1,0:T(8,128)(2,1)S(1)} %get-tuple-element.20.inner, ...), custom_call_target="tpu_custom_call" | custom-call | flops 1 | bytes 1 | tf_op jit(solution)/shard_map/square_kernel/pallas_call | solution.py:242
  49.1 0.1 collective-permute-start.6
  49.2 1.8 %collective-permute-start.5 = (bf16[2,768,256]{2,1,0:T(8,128)(2,1)S(1)}, bf16[2,768,256]{2,1,0:T(8,128)(2,1)S(1)}, u32[]{:S(2)}, u32[]{:S(2)}) collective-permute-start(bf16[2,768,256]{2,1,0:T(8,128)(2,1)S(1)} %get-tuple-element.28), channel_id=1, source_target_pairs={{0,15},{1,2},{2,1},{3,4},{4,3},{5,6},{6,5},{7,8},{8,7},{9,10},{10,... | collective-permute-start | bytes 2359304 | tf_op jit(solution)/shard_map/ppermute | solution.py:227
  51.0 0.1 collective-permute-start.4
  51.1 0.0 collective-permute-done.3.inner_own
  51.1 10.3 %early_kernel.1 = (f32[3,768,256]{2,1,0:T(8,128)S(1)}, f32[3,768,256]{2,1,0:T(8,128)S(1)}, f32[3,768,256]{2,1,0:T(8,128)S(1)}, f32[3,768,256]{2,1,0:T(8,128)S(1)}) custom-call(s32[8,48]{1,0:T(8,128)S(1)} %bitcast.4, bf16[3,768,256]{2,1,0:T(8,128)(2,1)S(1)} %get-tuple-element.18.own, bf16[3,768,256]{2,1,0:T(8,128)(2,1)S(1)} %get-tuple-element.20.inner, ...), custom_call_target="tpu_custom_call" | custom-call | flops 1 | bytes 1 | tf_op jit(solution)/shard_map/early_kernel/pallas_call | solution.py:242
  61.5 7.8 %collective-permute-done.outer_own = bf16[3,768,256]{2,1,0:T(8,128)(2,1)S(1)} collective-permute-done((bf16[3,768,256]{2,1,0:T(8,128)(2,1)S(1)}, bf16[3,768,256]{2,1,0:T(8,128)(2,1)S(1)}, u32[]{:S(2)}, u32[]{:S(2)}) %collective-permute-start) | collective-permute-done | bytes 1179680 | tf_op jit(solution)/shard_map/ppermute | solution.py:227
  69.2 6.1 %late_kernel.1 = (bf16[3,8,256,256]{3,2,1,0:T(8,128)(2,1)}, f32[3,768,256]{2,1,0:T(8,128)S(1)}, s32[3,8,128]{2,1,0:T(8,128)S(1)}) custom-call(s32[8,48]{1,0:T(8,128)S(1)} %bitcast.5, bf16[3,768,256]{2,1,0:T(8,128)(2,1)S(1)} %get-tuple-element.18.own, bf16[3,768,256]{2,1,0:T(8,128)(2,1)S(1)} %get-tuple-element.19.outer, ...), custom_call_target="tpu_custom_call" | custom-call | flops 1 | bytes 1 | tf_op jit(solution)/shard_map/late_kernel/pallas_call | solution.py:242
  75.3 2.3 %collective-permute-done.5.s_outer_head = bf16[2,768,256]{2,1,0:T(8,128)(2,1)S(1)} collective-permute-done((bf16[2,768,256]{2,1,0:T(8,128)(2,1)S(1)}, bf16[2,768,256]{2,1,0:T(8,128)(2,1)S(1)}, u32[]{:S(2)}, u32[]{:S(2)}) %collective-permute-start.5) | collective-permute-done | bytes 786464 | tf_op jit(solution)/shard_map/ppermute | solution.py:227
  77.6 0.0 collective-permute-done.6.s_inner_own
  77.6 3.3 %head_kernel.1._ = bf16[3,8,256,256]{3,2,1,0:T(8,128)(2,1)} custom-call(s32[8,48]{1,0:T(8,128)S(1)} %bitcast.6, bf16[3,768,256]{2,1,0:T(8,128)(2,1)S(1)} %get-tuple-element.19.outer, bf16[2,768,256]{2,1,0:T(8,128)(2,1)S(1)} %collective-permute-done.5.s_outer_head, f32[3,768,256]{2,1,0:T(8,128)S(1)} %get-tuple-element.27.rest, ...), custom_call_target="tpu_custom_call", output_to_operand_aliasing={{}: (7, {})} | custom-call | flops 1 | bytes 1 | tf_op jit(solution)/shard_map/head_kernel/pallas_call | solution.py:242
  81.0 0.9 %collective-permute-done.4.s_outer_tail = bf16[1,768,256]{2,1,0:T(8,128)(2,1)S(1)} collective-permute-done((bf16[1,768,256]{2,1,0:T(8,128)(2,1)S(1)}, bf16[1,768,256]{2,1,0:T(8,128)(2,1)S(1)}, u32[]{:S(2)}, u32[]{:S(2)}) %collective-permute-start.4) | collective-permute-done | bytes 393248 | tf_op jit(solution)/shard_map/ppermute | solution.py:227
  81.8 1.2 %tail_kernel.1 = bf16[3,8,256,256]{3,2,1,0:T(8,128)(2,1)} custom-call(s32[3,8,128]{2,1,0:T(8,128)S(1)} %get-tuple-element.25.slots, bf16[3,768,256]{2,1,0:T(8,128)(2,1)S(1)} %get-tuple-element.19.outer, bf16[1,768,256]{2,1,0:T(8,128)(2,1)S(1)} %collective-permute-done.4.s_outer_tail, ...), custom_call_target="tpu_custom_call", output_to_operand_aliasing={{}: (4, {})} | custom-call | flops 1 | bytes 1 | tf_op jit(solution)/shard_map/tail_kernel/pallas_call | solution.py:275
Async XLA Ops:
  0.0 43.9 %copy-start = (s32[48,8]{0,1:T(8,128)S(1)}, s32[48,8]{0,1:T(8,128)}, u32[]{:S(2)}) copy-start(s32[48,8]{0,1:T(8,128)} %param.3) | copy-start | bytes 4612
  2.1 41.9 %collective-permute-start.1 = (bf16[3,768,256]{2,1,0:T(8,128)(2,1)S(1)}, bf16[3,768,256]{2,1,0:T(8,128)(2,1)S(1)}, u32[]{:S(2)}, u32[]{:S(2)}) collective-permute-start(bf16[3,768,256]{2,1,0:T(8,128)(2,1)S(1)} %get-tuple-element.19.outer), channel_id=1, source_target_pairs={{0,15},{1,2},{2,1},{3,4},{4,3},{5,6},{6,5},{7,8},{8,7},{9,10},{10,... | collective-permute-start | bytes 3538952 | tf_op jit(solution)/shard_map/ppermute | solution.py:227
  4.8 41.2 %collective-permute-start.2 = (bf16[3,768,256]{2,1,0:T(8,128)(2,1)S(1)}, bf16[3,768,256]{2,1,0:T(8,128)(2,1)S(1)}, u32[]{:S(2)}, u32[]{:S(2)}) collective-permute-start(bf16[3,768,256]{2,1,0:T(8,128)(2,1)S(1)} %get-tuple-element.20.inner), channel_id=1, source_target_pairs={{0,1},{1,0},{2,3},{3,2},{4,5},{5,4},{6,7},{7,6},{8,9},{9,8},{10,11... | collective-permute-start | bytes 3538952 | tf_op jit(solution)/shard_map/ppermute | solution.py:228
  7.6 43.5 %collective-permute-start.3 = (bf16[3,768,256]{2,1,0:T(8,128)(2,1)S(1)}, bf16[3,768,256]{2,1,0:T(8,128)(2,1)S(1)}, u32[]{:S(2)}, u32[]{:S(2)}) collective-permute-start(bf16[3,768,256]{2,1,0:T(8,128)(2,1)S(1)} %get-tuple-element.18.own), channel_id=1, source_target_pairs={{0,1},{1,0},{2,3},{3,2},{4,5},{5,4},{6,7},{7,6},{8,9},{9,8},{10,11... | collective-permute-start | bytes 3538952 | tf_op jit(solution)/shard_map/ppermute | solution.py:228
  7.6 61.6 %collective-permute-start = (bf16[3,768,256]{2,1,0:T(8,128)(2,1)S(1)}, bf16[3,768,256]{2,1,0:T(8,128)(2,1)S(1)}, u32[]{:S(2)}, u32[]{:S(2)}) collective-permute-start(bf16[3,768,256]{2,1,0:T(8,128)(2,1)S(1)} %get-tuple-element.18.own), channel_id=1, source_target_pairs={{0,15},{1,2},{2,1},{3,4},{4,3},{5,6},{6,5},{7,8},{8,7},{9,10},{10,... | collective-permute-start | bytes 3538952 | tf_op jit(solution)/shard_map/ppermute | solution.py:227
  49.1 28.5 %collective-permute-start.6 = (bf16[3,768,256]{2,1,0:T(8,128)(2,1)S(1)}, bf16[3,768,256]{2,1,0:T(8,128)(2,1)S(1)}, u32[]{:S(2)}, u32[]{:S(2)}) collective-permute-start(bf16[3,768,256]{2,1,0:T(8,128)(2,1)S(1)} %get-tuple-element.21.s_own), channel_id=1, source_target_pairs={{0,1},{1,0},{2,3},{3,2},{4,5},{5,4},{6,7},{7,6},{8,9},{9,8},{10,11... | collective-permute-start | bytes 3538952 | tf_op jit(solution)/shard_map/ppermute | solution.py:228
  49.2 28.4 %collective-permute-start.5 = (bf16[2,768,256]{2,1,0:T(8,128)(2,1)S(1)}, bf16[2,768,256]{2,1,0:T(8,128)(2,1)S(1)}, u32[]{:S(2)}, u32[]{:S(2)}) collective-permute-start(bf16[2,768,256]{2,1,0:T(8,128)(2,1)S(1)} %get-tuple-element.28), channel_id=1, source_target_pairs={{0,15},{1,2},{2,1},{3,4},{4,3},{5,6},{6,5},{7,8},{8,7},{9,10},{10,... | collective-permute-start | bytes 2359304 | tf_op jit(solution)/shard_map/ppermute | solution.py:227
  51.0 30.8 %collective-permute-start.4 = (bf16[1,768,256]{2,1,0:T(8,128)(2,1)S(1)}, bf16[1,768,256]{2,1,0:T(8,128)(2,1)S(1)}, u32[]{:S(2)}, u32[]{:S(2)}) collective-permute-start(bf16[1,768,256]{2,1,0:T(8,128)(2,1)S(1)} %get-tuple-element.26), channel_id=1, source_target_pairs={{0,15},{1,2},{2,1},{3,4},{4,3},{5,6},{6,5},{7,8},{8,7},{9,10},{10,... | collective-permute-start | bytes 1179656 | tf_op jit(solution)/shard_map/ppermute | solution.py:227

commit v5 on v4

--- a/solution.py
+++ b/solution.py
@@ -15,6 +15,7 @@
 VMEM = pl.BlockSpec(memory_space=pltpu.VMEM)
 SMEM = pl.BlockSpec(memory_space=pltpu.SMEM)
 BRIEF = pl.CostEstimate(flops=1, bytes_accessed=1, transcendentals=0)
+LONGER = pl.CostEstimate(flops=5 * 10**9, bytes_accessed=1, transcendentals=0)
 VMEM_LIMIT = 24 * 1024 * 1024
 
 
@@ -50,47 +51,77 @@
                 ref[j, pl.ds(r * bs, bs), :] = jnp.zeros((bs, bs), ref.dtype)
 
 
-def pack_kernel(devices, rb, bs, pattern_hbm, blocks, *rest):
+def place(pattern, held, row, owner, columns, cut, first, rb, bs):
+    for j in range(rb):
+        slot = slot_of(pattern, owner * rb + row, columns * rb + j)
+        block = held[jnp.maximum(slot, 0)]
+        cut[j, pl.ds((row - first) * bs, bs), :] = jnp.where(slot >= 0, block, jnp.zeros_like(block))
+
+
+def first_kernel(devices, rb, bs, pattern_hbm, blocks, cut, pattern, held, pattern_sem, sem):
+    fetch = pltpu.make_async_copy(pattern_hbm, pattern, pattern_sem)
+    fetch.start()
+    load = pltpu.make_async_copy(blocks.at[0], held, sem)
+    load.start()
+    me, other, _ = neighbours(devices)
+    fetch.wait()
+    load.wait()
+    place(pattern, held, 0, me, other, cut, 0, rb, bs)
+
+
+def pack_kernel(devices, rb, bs, pattern_hbm, blocks, _, others, *rest):
     cuts, (pattern, held, pattern_sem, sems) = rest[:3], rest[3:]
     fetch = pltpu.make_async_copy(pattern_hbm, pattern, pattern_sem)
     fetch.start()
     loads = [pltpu.make_async_copy(blocks.at[r], held.at[r], sems.at[r]) for r in range(rb)]
     for load in loads:
         load.start()
-    me, other, partner = neighbours(devices)
+    people = neighbours(devices)
+    me, other, partner = people
     fetch.wait()
-    slots = [
-        [[slot_of(pattern, me * rb + r, column_device * rb + j) for j in range(rb)] for r in range(rb)]
-        for column_device in (other, me, partner)
-    ]
     for r in range(rb):
         loads[r].wait()
-        for cut, rows in zip(cuts, slots):
-            for j, slot in enumerate(rows[r]):
-                block = held[r, jnp.maximum(slot, 0)]
-                cut[j, pl.ds(r * bs, bs), :] = jnp.where(slot >= 0, block, jnp.zeros_like(block))
+        for cut, columns in zip(cuts, (other, me, partner)):
+            place(pattern, held.at[r], r, me, columns, cut, 0, rb, bs)
+    others[...] = cuts[0][:, pl.ds(bs, (rb - 1) * bs), :]
 
 
 def pack(devices, pattern, blocks):
-    rb, _, bs, _ = blocks.shape
-    return pl.pallas_call(
+    rb, slots, bs, _ = blocks.shape
+    pattern = pltpu.with_memory_space_constraint(pattern, pltpu.HBM)
+    blocks = pltpu.with_memory_space_constraint(blocks, pltpu.HBM)
+    cut = lambda rows: jax.ShapeDtypeStruct((rb, rows * bs, bs), blocks.dtype)
+    params = pltpu.CompilerParams(vmem_limit_bytes=VMEM_LIMIT)
+    first = pl.pallas_call(
+        functools.partial(first_kernel, devices, rb, bs),
+        out_shape=cut(1),
+        in_specs=[ANY, ANY],
+        out_specs=VMEM,
+        scratch_shapes=[
+            pltpu.SMEM(pattern.shape, pattern.dtype),
+            pltpu.VMEM(blocks.shape[1:], blocks.dtype),
+            pltpu.SemaphoreType.DMA,
+            pltpu.SemaphoreType.DMA,
+        ],
+        compiler_params=params,
+        cost_estimate=BRIEF,
+        name="first",
+    )(pattern, blocks)
+    return first, *pl.pallas_call(
         functools.partial(pack_kernel, devices, rb, bs),
-        out_shape=[jax.ShapeDtypeStruct((rb, rb * bs, bs), blocks.dtype)] * 3,
-        in_specs=[ANY, ANY],
-        out_specs=[VMEM] * 3,
+        out_shape=[cut(rb - 1), cut(rb), cut(rb), cut(rb)],
+        in_specs=[ANY, ANY, ANY],
+        out_specs=[VMEM] * 4,
         scratch_shapes=[
             pltpu.SMEM(pattern.shape, pattern.dtype),
             pltpu.VMEM(blocks.shape, blocks.dtype),
             pltpu.SemaphoreType.DMA,
             pltpu.SemaphoreType.DMA((rb,)),
         ],
-        compiler_params=pltpu.CompilerParams(vmem_limit_bytes=VMEM_LIMIT),
+        compiler_params=params,
         cost_estimate=BRIEF,
         name="pack",
-    )(
-        pltpu.with_memory_space_constraint(pattern, pltpu.HBM),
-        pltpu.with_memory_space_constraint(blocks, pltpu.HBM),
-    )
+    )(pattern, blocks, first)
 
 
 def scatter(out, pattern, me, column_device, panels, j, sems, base, rb, bs):
@@ -110,10 +141,22 @@
         pl.when(slot >= 0)(copy.wait)
 
 
-def outer_kernel(devices, rb, bs, pattern, outer, from_outer, own_part):
-    @pl.loop(0, rb)
-    def _(c):
-        own_part[c] = panel_product(outer, from_outer, c, rb, bs)
+def begin_kernel(devices, rb, bs, outer, from_first, part):
+    @pl.loop(0, rb)
+    def _(c):
+        part[c] = jnp.dot(outer[0], from_first[c], preferred_element_type=F32)
+
+
+def outer_kernel(devices, rb, bs, outer, from_first, from_others, part, from_outer, own_part):
+    from_outer[:, pl.ds(0, bs), :] = from_first[...]
+    from_outer[:, pl.ds(bs, (rb - 1) * bs), :] = from_others[...]
+
+    @pl.loop(0, rb)
+    def _(c):
+        total = part[c]
+        for k in range(1, rb):
+            total += jnp.dot(outer[k], from_others[c, pl.ds((k - 1) * bs, bs), :], preferred_element_type=F32)
+        own_part[c] = total
 
 
 def square_kernel(devices, rb, bs, pattern, own, inner, from_inner, own_part, s_own, s_head, s_tail):
@@ -231,9 +274,11 @@
     high = jax.ShapeDtypeStruct(low.shape, F32)
     full = jax.ShapeDtypeStruct(block_values.shape, BF16)
 
-    def call(kernel, operands, outs, scratch=(), into=None):
-        operands = (pltpu.with_memory_space_constraint(pattern, pltpu.SMEM), *operands)
-        in_specs = [SMEM] + [VMEM] * (len(operands) - 1)
+    def call(kernel, operands, outs, scratch=(), into=None, patterned=True, cost=BRIEF):
+        in_specs = [VMEM] * len(operands)
+        if patterned:
+            operands = (pltpu.with_memory_space_constraint(pattern, pltpu.SMEM), *operands)
+            in_specs = [SMEM] + in_specs
         aliases = {}
         if into is not None:
             aliases = {len(operands): 0}
@@ -247,16 +292,17 @@
             scratch_shapes=scratch,
             input_output_aliases=aliases,
             compiler_params=pltpu.CompilerParams(vmem_limit_bytes=VMEM_LIMIT),
-            cost_estimate=BRIEF,
+            cost_estimate=cost,
             name=kernel.__name__,
         )(*operands)
 
-    outer, own, inner = pack(devices, pattern, block_values)
-    from_outer = to_outer(outer)
+    first, others, outer, own, inner = pack(devices, pattern, block_values)
+    from_first, from_others = to_outer(first), to_outer(others)
     outer_own = to_outer(own)
     from_inner, inner_own = to_inner(inner), to_inner(own)
 
-    (own_part,) = call(outer_kernel, (outer, from_outer), (high,))
+    (part,) = call(begin_kernel, (outer, from_first), (high,), patterned=False, cost=LONGER)
+    from_outer, own_part = call(outer_kernel, (outer, from_first, from_others, part), (low, high), patterned=False, cost=LONGER)
     s_own, s_head, s_tail = call(square_kernel, (own, inner, from_inner, own_part), (low, low_of(rb - 1), low_of(1)))
     s_outer_head, s_outer_tail = to_outer(s_head), to_outer(s_tail)
     s_inner_own = to_inner(s_own)

time: 83.2 us -> 82.5 us (level)
  waiting for transfers between devices: 47.2 us -> 45 us
  Pallas kernels: 28.2 us -> 29.5 us
    ppermute x4 -> x5, waiting for transfers between devices: 47.2 us -> 45 us  [local(): to_outer = lambda x: lax.ppermute(x, 'grid', over)]
    pallas_call x0 -> x1, Pallas kernels: none -> 1.29 us  [pack(): pl.pallas_call(functools.partial(first_kernel, devices, rb, bs), out_shap...]
    pallas_call x5 -> x6, Pallas kernels: 25 us -> 24.9 us  [call(): pl.pallas_call(functools.partial(kernel, devices, rb, bs), out_shape=outs...]
    ppermute x4 -> x5, starting transfers between devices: 4.58 us -> 4.67 us  [local(): to_outer = lambda x: lax.ppermute(x, 'grid', over)]
  transfers between devices with their start and end apart: 7 -> 8, of which waited for: 4 -> 5; matrix products, arithmetic and copies ran while one was open for 0% -> 0% of each run, Pallas kernels for 30% -> 33%
where the time goes in v5:
time: 82.5 us; the launch traced here: 82.3 us
  waiting for transfers between devices  45 us (55%)
  Pallas kernels  29.5 us (36%)
  starting transfers between devices  7.75 us (9%)
    ppermute x5, waiting for transfers between devices, local(): to_outer = lambda x: lax.ppermute(x, 'grid', over)  45 us
    pallas_call x6, Pallas kernels, call(): pl.pallas_call(functools.partial(kernel, devices, rb, bs), out_shape=outs...  24.9 us
    ppermute x5, starting transfers between devices, local(): to_outer = lambda x: lax.ppermute(x, 'grid', over)  4.67 us
    ppermute x3, starting transfers between devices, local(): to_inner = lambda x: lax.ppermute(x, 'grid', across)  3.08 us
    pallas_call x1, Pallas kernels, pack(): pl.pallas_call(functools.partial(pack_kernel, devices, rb, bs), out_shape...  2.08 us
  transfers between devices with their start and end apart: 8, of which 5 were waited for; matrix products, arithmetic and copies ran while one was open for 0% of the time, Pallas kernels for 33%

profile of v5, /device:TPU:1, one launch (start us, length us, event | category | flops | bytes accessed | tf_op | source)
XLA Modules:
  0.0 82.3 jit_solution(16282476739681206806)
XLA Ops:
  0.0 1.3 %first.1._ = bf16[3,256,256]{2,1,0:T(8,128)(2,1)S(1)} custom-call(s32[8,48]{1,0:T(8,128)} %bitcast.1, bf16[3,8,256,256]{3,2,1,0:T(8,128)(2,1)} %blocks.3), custom_call_target="tpu_custom_call" | custom-call | flops 1 | bytes 1 | tf_op jit(solution)/shard_map/first/pallas_call | solution.py:95
  1.3 2.7 %collective-permute-start.1 = (bf16[3,256,256]{2,1,0:T(8,128)(2,1)S(1)}, bf16[3,256,256]{2,1,0:T(8,128)(2,1)S(1)}, u32[]{:S(2)}, u32[]{:S(2)}) collective-permute-start(bf16[3,256,256]{2,1,0:T(8,128)(2,1)S(1)} %first.1._), channel_id=1, source_target_pairs={{0,15},{1,2},{2,1},{3,4},{4,3},{5,6},{6,5},{7,8},{8,7},{9,10},{10,... | collective-permute-start | bytes 1179656 | tf_op jit(solution)/shard_map/ppermute | solution.py:270
  4.0 2.1 %pack.1 = (bf16[3,512,256]{2,1,0:T(8,128)(2,1)S(1)}, bf16[3,768,256]{2,1,0:T(8,128)(2,1)S(1)}, bf16[3,768,256]{2,1,0:T(8,128)(2,1)S(1)}, bf16[3,768,256]{2,1,0:T(8,128)(2,1)S(1)}) custom-call(s32[8,48]{1,0:T(8,128)} %bitcast.2, bf16[3,8,256,256]{3,2,1,0:T(8,128)(2,1)} %blocks.3, bf16[3,256,256]{2,1,0:T(8,128)(2,1)S(1)} %first.1._), custom_call_target="tpu_custom_call" | custom-call | flops 1 | bytes 1 | tf_op jit(solution)/shard_map/pack/pallas_call | solution.py:110
  6.1 0.1 collective-permute-start.2
  6.2 2.9 %collective-permute-start.3 = (bf16[3,768,256]{2,1,0:T(8,128)(2,1)S(1)}, bf16[3,768,256]{2,1,0:T(8,128)(2,1)S(1)}, u32[]{:S(2)}, u32[]{:S(2)}) collective-permute-start(bf16[3,768,256]{2,1,0:T(8,128)(2,1)S(1)} %get-tuple-element.25.inner), channel_id=1, source_target_pairs={{0,1},{1,0},{2,3},{3,2},{4,5},{5,4},{6,7},{7,6},{8,9},{9,8},{10,11... | collective-permute-start | bytes 3538952 | tf_op jit(solution)/shard_map/ppermute | solution.py:271
  9.1 0.1 collective-permute-start.4
  9.2 0.0 collective-permute-start
  9.2 24.8 %collective-permute-done.1.from_first = bf16[3,256,256]{2,1,0:T(8,128)(2,1)S(1)} collective-permute-done((bf16[3,256,256]{2,1,0:T(8,128)(2,1)S(1)}, bf16[3,256,256]{2,1,0:T(8,128)(2,1)S(1)}, u32[]{:S(2)}, u32[]{:S(2)}) %collective-permute-start.1) | collective-permute-done | bytes 393248 | tf_op jit(solution)/shard_map/ppermute | solution.py:270
  34.0 0.8 begin_kernel.1.part
  34.8 0.0 copy-start
  34.8 8.4 %collective-permute-done.2.from_others = bf16[3,512,256]{2,1,0:T(8,128)(2,1)S(1)} collective-permute-done((bf16[3,512,256]{2,1,0:T(8,128)(2,1)S(1)}, bf16[3,512,256]{2,1,0:T(8,128)(2,1)S(1)}, u32[]{:S(2)}, u32[]{:S(2)}) %collective-permute-start.2) | collective-permute-done | bytes 786464 | tf_op jit(solution)/shard_map/ppermute | solution.py:270
  43.2 1.2 %outer_kernel.1 = (bf16[3,768,256]{2,1,0:T(8,128)(2,1)S(1)}, f32[3,768,256]{2,1,0:T(8,128)S(1)}) custom-call(bf16[3,768,256]{2,1,0:T(8,128)(2,1)S(1)} %get-tuple-element.22.outer, bf16[3,256,256]{2,1,0:T(8,128)(2,1)S(1)} %collective-permute-done.1.from_first, bf16[3,512,256]{2,1,0:T(8,128)(2,1)S(1)} %collective-permute-done.2.from_others, ...), custom_call_target="tpu_custom_call" | custom-call | flops 5000000000 | bytes 1 | tf_op jit(solution)/shard_map/outer_kernel/pallas_call | solution.py:287
  44.4 0.0 collective-permute-done.3.from_inner
  44.4 0.0 copy-done
  44.4 3.2 %square_kernel.1 = (bf16[3,768,256]{2,1,0:T(8,128)(2,1)S(1)}, bf16[2,768,256]{2,1,0:T(8,128)(2,1)S(1)}, bf16[1,768,256]{2,1,0:T(8,128)(2,1)S(1)}) custom-call(s32[8,48]{1,0:T(8,128)S(1)} %bitcast.3, bf16[3,768,256]{2,1,0:T(8,128)(2,1)S(1)} %get-tuple-element.21.own, bf16[3,768,256]{2,1,0:T(8,128)(2,1)S(1)} %get-tuple-element.25.inner, ...), custom_call_target="tpu_custom_call" | custom-call | flops 1 | bytes 1 | tf_op jit(solution)/shard_map/square_kernel/pallas_call | solution.py:287
  47.5 0.1 collective-permute-start.7
  47.6 1.8 %collective-permute-start.6 = (bf16[2,768,256]{2,1,0:T(8,128)(2,1)S(1)}, bf16[2,768,256]{2,1,0:T(8,128)(2,1)S(1)}, u32[]{:S(2)}, u32[]{:S(2)}) collective-permute-start(bf16[2,768,256]{2,1,0:T(8,128)(2,1)S(1)} %get-tuple-element.34), channel_id=1, source_target_pairs={{0,15},{1,2},{2,1},{3,4},{4,3},{5,6},{6,5},{7,8},{8,7},{9,10},{10,... | collective-permute-start | bytes 2359304 | tf_op jit(solution)/shard_map/ppermute | solution.py:270
  49.4 0.1 collective-permute-start.5
  49.5 0.0 collective-permute-done.4.inner_own
  49.5 10.3 %early_kernel.1 = (f32[3,768,256]{2,1,0:T(8,128)S(1)}, f32[3,768,256]{2,1,0:T(8,128)S(1)}, f32[3,768,256]{2,1,0:T(8,128)S(1)}, f32[3,768,256]{2,1,0:T(8,128)S(1)}) custom-call(s32[8,48]{1,0:T(8,128)S(1)} %bitcast.4, bf16[3,768,256]{2,1,0:T(8,128)(2,1)S(1)} %get-tuple-element.21.own, bf16[3,768,256]{2,1,0:T(8,128)(2,1)S(1)} %get-tuple-element.25.inner, ...), custom_call_target="tpu_custom_call" | custom-call | flops 1 | bytes 1 | tf_op jit(solution)/shard_map/early_kernel/pallas_call | solution.py:287
  59.9 8.6 %collective-permute-done.outer_own = bf16[3,768,256]{2,1,0:T(8,128)(2,1)S(1)} collective-permute-done((bf16[3,768,256]{2,1,0:T(8,128)(2,1)S(1)}, bf16[3,768,256]{2,1,0:T(8,128)(2,1)S(1)}, u32[]{:S(2)}, u32[]{:S(2)}) %collective-permute-start) | collective-permute-done | bytes 1179680 | tf_op jit(solution)/shard_map/ppermute | solution.py:270
  68.4 6.1 %late_kernel.1 = (bf16[3,8,256,256]{3,2,1,0:T(8,128)(2,1)}, f32[3,768,256]{2,1,0:T(8,128)S(1)}, s32[3,8,128]{2,1,0:T(8,128)S(1)}) custom-call(s32[8,48]{1,0:T(8,128)S(1)} %bitcast.5, bf16[3,768,256]{2,1,0:T(8,128)(2,1)S(1)} %get-tuple-element.21.own, bf16[3,768,256]{2,1,0:T(8,128)(2,1)S(1)} %get-tuple-element.22.outer, ...), custom_call_target="tpu_custom_call" | custom-call | flops 1 | bytes 1 | tf_op jit(solution)/shard_map/late_kernel/pallas_call | solution.py:287
  74.6 2.3 %collective-permute-done.6.s_outer_head = bf16[2,768,256]{2,1,0:T(8,128)(2,1)S(1)} collective-permute-done((bf16[2,768,256]{2,1,0:T(8,128)(2,1)S(1)}, bf16[2,768,256]{2,1,0:T(8,128)(2,1)S(1)}, u32[]{:S(2)}, u32[]{:S(2)}) %collective-permute-start.6) | collective-permute-done | bytes 786464 | tf_op jit(solution)/shard_map/ppermute | solution.py:270
  76.9 0.0 collective-permute-done.7.s_inner_own
  76.9 3.3 %head_kernel.1._ = bf16[3,8,256,256]{3,2,1,0:T(8,128)(2,1)} custom-call(s32[8,48]{1,0:T(8,128)S(1)} %bitcast.6, bf16[3,768,256]{2,1,0:T(8,128)(2,1)S(1)} %get-tuple-element.22.outer, bf16[2,768,256]{2,1,0:T(8,128)(2,1)S(1)} %collective-permute-done.6.s_outer_head, f32[3,768,256]{2,1,0:T(8,128)S(1)} %get-tuple-element.33.rest, ...), custom_call_target="tpu_custom_call", output_to_operand_aliasing={{}: (7, {})} | custom-call | flops 1 | bytes 1 | tf_op jit(solution)/shard_map/head_kernel/pallas_call | solution.py:287
  80.2 0.9 %collective-permute-done.5.s_outer_tail = bf16[1,768,256]{2,1,0:T(8,128)(2,1)S(1)} collective-permute-done((bf16[1,768,256]{2,1,0:T(8,128)(2,1)S(1)}, bf16[1,768,256]{2,1,0:T(8,128)(2,1)S(1)}, u32[]{:S(2)}, u32[]{:S(2)}) %collective-permute-start.5) | collective-permute-done | bytes 393248 | tf_op jit(solution)/shard_map/ppermute | solution.py:270
  81.1 1.2 %tail_kernel.1 = bf16[3,8,256,256]{3,2,1,0:T(8,128)(2,1)} custom-call(s32[3,8,128]{2,1,0:T(8,128)S(1)} %get-tuple-element.31.slots, bf16[3,768,256]{2,1,0:T(8,128)(2,1)S(1)} %get-tuple-element.22.outer, bf16[1,768,256]{2,1,0:T(8,128)(2,1)S(1)} %collective-permute-done.5.s_outer_tail, ...), custom_call_target="tpu_custom_call", output_to_operand_aliasing={{}: (4, {})} | custom-call | flops 1 | bytes 1 | tf_op jit(solution)/shard_map/tail_kernel/pallas_call | solution.py:321
Async XLA Ops:
  1.3 32.7 %collective-permute-start.1 = (bf16[3,256,256]{2,1,0:T(8,128)(2,1)S(1)}, bf16[3,256,256]{2,1,0:T(8,128)(2,1)S(1)}, u32[]{:S(2)}, u32[]{:S(2)}) collective-permute-start(bf16[3,256,256]{2,1,0:T(8,128)(2,1)S(1)} %first.1._), channel_id=1, source_target_pairs={{0,15},{1,2},{2,1},{3,4},{4,3},{5,6},{6,5},{7,8},{8,7},{9,10},{10,... | collective-permute-start | bytes 1179656 | tf_op jit(solution)/shard_map/ppermute | solution.py:270
  6.1 37.1 %collective-permute-start.2 = (bf16[3,512,256]{2,1,0:T(8,128)(2,1)S(1)}, bf16[3,512,256]{2,1,0:T(8,128)(2,1)S(1)}, u32[]{:S(2)}, u32[]{:S(2)}) collective-permute-start(bf16[3,512,256]{2,1,0:T(8,128)(2,1)S(1)} %get-tuple-element.23), channel_id=1, source_target_pairs={{0,15},{1,2},{2,1},{3,4},{4,3},{5,6},{6,5},{7,8},{8,7},{9,10},{10,... | collective-permute-start | bytes 2359304 | tf_op jit(solution)/shard_map/ppermute | solution.py:270
  6.2 38.2 %collective-permute-start.3 = (bf16[3,768,256]{2,1,0:T(8,128)(2,1)S(1)}, bf16[3,768,256]{2,1,0:T(8,128)(2,1)S(1)}, u32[]{:S(2)}, u32[]{:S(2)}) collective-permute-start(bf16[3,768,256]{2,1,0:T(8,128)(2,1)S(1)} %get-tuple-element.25.inner), channel_id=1, source_target_pairs={{0,1},{1,0},{2,3},{3,2},{4,5},{5,4},{6,7},{7,6},{8,9},{9,8},{10,11... | collective-permute-start | bytes 3538952 | tf_op jit(solution)/shard_map/ppermute | solution.py:271
  9.1 40.4 %collective-permute-start.4 = (bf16[3,768,256]{2,1,0:T(8,128)(2,1)S(1)}, bf16[3,768,256]{2,1,0:T(8,128)(2,1)S(1)}, u32[]{:S(2)}, u32[]{:S(2)}) collective-permute-start(bf16[3,768,256]{2,1,0:T(8,128)(2,1)S(1)} %get-tuple-element.21.own), channel_id=1, source_target_pairs={{0,1},{1,0},{2,3},{3,2},{4,5},{5,4},{6,7},{7,6},{8,9},{9,8},{10,11... | collective-permute-start | bytes 3538952 | tf_op jit(solution)/shard_map/ppermute | solution.py:271
  9.2 59.3 %collective-permute-start = (bf16[3,768,256]{2,1,0:T(8,128)(2,1)S(1)}, bf16[3,768,256]{2,1,0:T(8,128)(2,1)S(1)}, u32[]{:S(2)}, u32[]{:S(2)}) collective-permute-start(bf16[3,768,256]{2,1,0:T(8,128)(2,1)S(1)} %get-tuple-element.21.own), channel_id=1, source_target_pairs={{0,15},{1,2},{2,1},{3,4},{4,3},{5,6},{6,5},{7,8},{8,7},{9,10},{10,... | collective-permute-start | bytes 3538952 | tf_op jit(solution)/shard_map/ppermute | solution.py:270
  34.8 9.6 %copy-start = (s32[48,8]{0,1:T(8,128)S(1)}, s32[48,8]{0,1:T(8,128)}, u32[]{:S(2)}) copy-start(s32[48,8]{0,1:T(8,128)} %param.3) | copy-start | bytes 4612
  47.5 29.3 %collective-permute-start.7 = (bf16[3,768,256]{2,1,0:T(8,128)(2,1)S(1)}, bf16[3,768,256]{2,1,0:T(8,128)(2,1)S(1)}, u32[]{:S(2)}, u32[]{:S(2)}) collective-permute-start(bf16[3,768,256]{2,1,0:T(8,128)(2,1)S(1)} %get-tuple-element.27.s_own), channel_id=1, source_target_pairs={{0,1},{1,0},{2,3},{3,2},{4,5},{5,4},{6,7},{7,6},{8,9},{9,8},{10,11... | collective-permute-start | bytes 3538952 | tf_op jit(solution)/shard_map/ppermute | solution.py:271
  47.6 29.3 %collective-permute-start.6 = (bf16[2,768,256]{2,1,0:T(8,128)(2,1)S(1)}, bf16[2,768,256]{2,1,0:T(8,128)(2,1)S(1)}, u32[]{:S(2)}, u32[]{:S(2)}) collective-permute-start(bf16[2,768,256]{2,1,0:T(8,128)(2,1)S(1)} %get-tuple-element.34), channel_id=1, source_target_pairs={{0,15},{1,2},{2,1},{3,4},{4,3},{5,6},{6,5},{7,8},{8,7},{9,10},{10,... | collective-permute-start | bytes 2359304 | tf_op jit(solution)/shard_map/ppermute | solution.py:270
  49.4 31.7 %collective-permute-start.5 = (bf16[1,768,256]{2,1,0:T(8,128)(2,1)S(1)}, bf16[1,768,256]{2,1,0:T(8,128)(2,1)S(1)}, u32[]{:S(2)}, u32[]{:S(2)}) collective-permute-start(bf16[1,768,256]{2,1,0:T(8,128)(2,1)S(1)} %get-tuple-element.32), channel_id=1, source_target_pairs={{0,15},{1,2},{2,1},{3,4},{4,3},{5,6},{6,5},{7,8},{8,7},{9,10},{10,... | collective-permute-start | bytes 1179656 | tf_op jit(solution)/shard_map/ppermute | solution.py:270

commit v6 on v5

--- a/solution.py
+++ b/solution.py
@@ -41,9 +41,9 @@
     return total
 
 
-def drop_absent(ref, pattern, row_device, column_device, rb, bs):
-    for r in range(rb):
-        for j in range(rb):
+def drop_absent(ref, pattern, row_device, column_device, rb, bs, panels=None):
+    for r in range(rb):
+        for j in range(rb if panels is None else panels):
             slot = slot_of(pattern, row_device * rb + r, column_device * rb + j)
 
             @pl.when(slot < 0)
@@ -159,7 +159,7 @@
         own_part[c] = total
 
 
-def square_kernel(devices, rb, bs, pattern, own, inner, from_inner, own_part, s_own, s_head, s_tail):
+def square_kernel(devices, rb, bs, pattern, own, inner, from_inner, own_part, s_own, s_head):
     me, _, _ = neighbours(devices)
 
     @pl.loop(0, rb)
@@ -170,7 +170,6 @@
 
     drop_absent(s_own, pattern, me, me, rb, bs)
     s_head[...] = s_own[pl.ds(0, rb - 1)]
-    s_tail[...] = s_own[pl.ds(rb - 1, 1)]
 
 
 def early_kernel(
@@ -197,66 +196,64 @@
         inner_part[c] = 3.0 * s_inner[c].astype(F32) - 2.0 * panel_product(own, s_inner, c, rb, bs)
 
 
-def late_kernel(
-    devices, rb, bs, pattern, own, outer, outer_own, from_outer, s_own, outer_part, from_outer_part, cube_part,
-    out, rest, slots, s_outer, s_from_outer, out_own, sems,
+def ahead_kernel(
+    devices, rb, bs, pattern, outer_own, from_outer, from_outer_part, s_own, s_from_outer, out_there, slots
 ):
     me, other, _ = neighbours(devices)
-    for r in range(rb):
-        slots[r] = jnp.full(slots.shape[1:], slot_of(pattern, me * rb + r, other * rb + rb - 1))
+    last = rb - 1
+    for r in range(rb):
+        slots[r] = jnp.full(slots.shape[1:], slot_of(pattern, me * rb + r, other * rb + last))
 
     @pl.loop(0, rb)
     def _(c):
         s_from_outer[c] = (from_outer_part[c] + panel_product(outer_own, from_outer, c, rb, bs)).astype(BF16)
-        s_outer[c] = (outer_part[c] + panel_product(outer, outer_own, c, rb, bs)).astype(BF16)
-
-    drop_absent(s_outer, pattern, me, other, rb, bs)
+
     drop_absent(s_from_outer, pattern, other, me, rb, bs)
+    cube = panel_product(outer_own, s_from_outer, last, rb, bs) + panel_product(from_outer, s_own, last, rb, bs)
+    out_there[0] = (3.0 * s_from_outer[last].astype(F32) - 2.0 * cube).astype(BF16)
+
+
+def late_kernel(
+    devices, rb, bs, pattern, own, outer, outer_own, s_from_outer, s_own, outer_part, cube_part, inner,
+    s_inner_own, inner_part, out, rest, s_outer, out_own, out_inner, sems,
+):
+    me, other, partner = neighbours(devices)
     waits = []
+    for c in range(rb):
+        out_inner[c] = (inner_part[c] - 2.0 * panel_product(inner, s_inner_own, c, rb, bs)).astype(BF16)
+        waits += scatter(out, pattern, me, partner, out_inner, c, sems, rb * rb, rb, bs)
     for c in range(rb):
         cube = cube_part[c] + panel_product(outer, s_from_outer, c, rb, bs)
         out_own[c] = (3.0 * s_own[c].astype(F32) - 2.0 * cube).astype(BF16)
         waits += scatter(out, pattern, me, me, out_own, c, sems, 0, rb, bs)
 
-    @pl.loop(0, rb)
+    @pl.loop(0, rb - 1)
+    def _(c):
+        s_outer[c] = (outer_part[c] + panel_product(outer, outer_own, c, rb, bs)).astype(BF16)
+
+    drop_absent(s_outer, pattern, me, other, rb, bs, rb - 1)
+
+    @pl.loop(0, rb - 1)
     def _(c):
         rest[c] = 3.0 * s_outer[c].astype(F32) - 2.0 * panel_product(own, s_outer, c, rb, bs)
 
     settle(waits)
 
 
-def finish(devices, rb, bs, pattern, column_device, first, left, right, part, out, panels, sems, base):
-    me = lax.axis_index("grid")
+def head_kernel(devices, rb, bs, pattern, outer, s_outer_head, rest, _, out, out_outer, sems):
+    me, other, _ = neighbours(devices)
     waits = []
-    for c in range(right.shape[0]):
-        cube = panel_product(left, right, c, rb, bs)
-        panels[first + c] = (part[first + c] - 2.0 * cube).astype(BF16)
-        waits += scatter(out, pattern, me, column_device, panels, first + c, sems, base, rb, bs)
-    return waits
-
-
-def head_kernel(
-    devices, rb, bs, pattern, outer, s_outer_head, rest, inner, s_inner_own, inner_part, _,
-    out, out_outer, out_inner, sems,
-):
-    _, other, partner = neighbours(devices)
-    waits = finish(devices, rb, bs, pattern, other, 0, outer, s_outer_head, rest, out, out_outer, sems, 0)
-    waits += finish(
-        devices, rb, bs, pattern, partner, 0, inner, s_inner_own, inner_part, out, out_inner, sems, rb * rb
-    )
+    for c in range(rb - 1):
+        out_outer[c] = (rest[c] - 2.0 * panel_product(outer, s_outer_head, c, rb, bs)).astype(BF16)
+        waits += scatter(out, pattern, me, other, out_outer, c, sems, 0, rb, bs)
     settle(waits)
 
 
-def tail_kernel(devices, rb, bs, slots, outer, s_outer_tail, rest, _, out, panels, sems):
+def tail_kernel(rb, bs, slots, panel, _, out, sems):
     waits = []
     for r in range(rb):
-        rows = pl.ds(r * bs, bs)
         slot = jnp.max(slots[r])
-        cube = jnp.dot(outer[0, rows, :], s_outer_tail[0, pl.ds(0, bs), :], preferred_element_type=F32)
-        for k in range(1, rb):
-            cube += jnp.dot(outer[k, rows, :], s_outer_tail[0, pl.ds(k * bs, bs), :], preferred_element_type=F32)
-        panels[0, rows, :] = (rest[rb - 1, rows, :] - 2.0 * cube).astype(BF16)
-        copy = pltpu.make_async_copy(panels.at[0, rows, :], out.at[r, jnp.maximum(slot, 0)], sems.at[r])
+        copy = pltpu.make_async_copy(panel.at[0, pl.ds(r * bs, bs), :], out.at[r, jnp.maximum(slot, 0)], sems.at[r])
         pl.when(slot >= 0)(copy.start)
         waits.append((slot, copy))
     settle(waits)
@@ -303,32 +300,38 @@
 
     (part,) = call(begin_kernel, (outer, from_first), (high,), patterned=False, cost=LONGER)
     from_outer, own_part = call(outer_kernel, (outer, from_first, from_others, part), (low, high), patterned=False, cost=LONGER)
-    s_own, s_head, s_tail = call(square_kernel, (own, inner, from_inner, own_part), (low, low_of(rb - 1), low_of(1)))
-    s_outer_head, s_outer_tail = to_outer(s_head), to_outer(s_tail)
+    s_own, s_head = call(square_kernel, (own, inner, from_inner, own_part), (low, low_of(rb - 1)))
+    s_outer_head = to_outer(s_head)
     s_inner_own = to_inner(s_own)
     cube_part, inner_part, from_outer_part, outer_part = call(
         early_kernel, (own, inner, outer, from_inner, inner_own, from_outer, s_own), (high,) * 4, 2
     )
-    out, rest, slots = call(
+    s_from_outer, out_there, slots = call(
+        ahead_kernel,
+        (outer_own, from_outer, from_outer_part, s_own),
+        (low, low_of(1), jax.ShapeDtypeStruct((rb, 8, 128), jnp.int32)),
+        cost=BRIEF,
+    )
+    out_here = to_outer(out_there)
+    out, rest = call(
         late_kernel,
-        (own, outer, outer_own, from_outer, s_own, outer_part, from_outer_part, cube_part),
-        (full, high, jax.ShapeDtypeStruct((rb, 8, 128), jnp.int32)),
+        (own, outer, outer_own, s_from_outer, s_own, outer_part, cube_part, inner, s_inner_own, inner_part),
+        (full, high),
         3,
+        cost=BRIEF,
     )
-    (out,) = call(
-        head_kernel, (outer, s_outer_head, rest, inner, s_inner_own, inner_part), (full,), 2, into=out
-    )
+    (out,) = call(head_kernel, (outer, s_outer_head, rest), (full,), 1, into=out, cost=BRIEF)
     return pl.pallas_call(
-        functools.partial(tail_kernel, devices, rb, bs),
+        functools.partial(tail_kernel, rb, bs),
         out_shape=full,
-        in_specs=[VMEM, VMEM, VMEM, VMEM, ANY],
+        in_specs=[VMEM, VMEM, ANY],
         out_specs=ANY,
-        scratch_shapes=[pltpu.VMEM((1, rb * bs, bs), BF16), pltpu.SemaphoreType.DMA((rb,))],
-        input_output_aliases={4: 0},
+        scratch_shapes=[pltpu.SemaphoreType.DMA((rb,))],
+        input_output_aliases={2: 0},
         compiler_params=pltpu.CompilerParams(vmem_limit_bytes=VMEM_LIMIT),
         cost_estimate=BRIEF,
         name="tail_kernel",
-    )(slots, outer, s_outer_tail, rest, out)
+    )(slots, out_here, out)
 
 
 def solution(mesh):

time: 82.5 us -> 82.2 us (level)
  waiting for transfers between devices: 45 us -> 38.1 us
  starting transfers between devices: 7.75 us -> 13.7 us
    ppermute x5, waiting for transfers between devices: 45 us -> 38.1 us  [local(): to_outer = lambda x: lax.ppermute(x, 'grid', over)]
    ppermute x3, starting transfers between devices: 3.08 us -> 7.37 us  [local(): to_inner = lambda x: lax.ppermute(x, 'grid', across)]
    ppermute x5, starting transfers between devices: 4.67 us -> 6.38 us  [local(): to_outer = lambda x: lax.ppermute(x, 'grid', over)]
    pallas_call x6 -> x7, Pallas kernels: 24.9 us -> 25.8 us  [call(): pl.pallas_call(functools.partial(kernel, devices, rb, bs), out_shape=outs...]
  transfers between devices with their start and end apart: 8 -> 8, of which waited for: 5 -> 5; matrix products, arithmetic and copies ran while one was open for 0% -> 0% of each run, Pallas kernels for 33% -> 34%
where the time goes in v6:
time: 82.2 us; the launch traced here: 82 us
  waiting for transfers between devices  38.1 us (46%)
  Pallas kernels  30.1 us (37%)
  starting transfers between devices  13.7 us (17%)
    ppermute x5, waiting for transfers between devices, local(): to_outer = lambda x: lax.ppermute(x, 'grid', over)  38.1 us
    pallas_call x7, Pallas kernels, call(): pl.pallas_call(functools.partial(kernel, devices, rb, bs), out_shape=outs...  25.8 us
    ppermute x3, starting transfers between devices, local(): to_inner = lambda x: lax.ppermute(x, 'grid', across)  7.37 us
    ppermute x5, starting transfers between devices, local(): to_outer = lambda x: lax.ppermute(x, 'grid', over)  6.38 us
    pallas_call x1, Pallas kernels, pack(): pl.pallas_call(functools.partial(pack_kernel, devices, rb, bs), out_shape...  2.09 us
  transfers between devices with their start and end apart: 8, of which 5 were waited for; matrix products, arithmetic and copies ran while one was open for 0% of the time, Pallas kernels for 34%

profile of v6, /device:TPU:1, one launch (start us, length us, event | category | flops | bytes accessed | tf_op | source)
XLA Modules:
  0.0 82.0 jit_solution(9388689673132787951)
XLA Ops:
  0.0 1.3 %first.1._ = bf16[3,256,256]{2,1,0:T(8,128)(2,1)S(1)} custom-call(s32[8,48]{1,0:T(8,128)} %bitcast.1, bf16[3,8,256,256]{3,2,1,0:T(8,128)(2,1)} %blocks.3), custom_call_target="tpu_custom_call" | custom-call | flops 1 | bytes 1 | tf_op jit(solution)/shard_map/first/pallas_call | solution.py:95
  1.3 2.7 %collective-permute-start.1 = (bf16[3,256,256]{2,1,0:T(8,128)(2,1)S(1)}, bf16[3,256,256]{2,1,0:T(8,128)(2,1)S(1)}, u32[]{:S(2)}, u32[]{:S(2)}) collective-permute-start(bf16[3,256,256]{2,1,0:T(8,128)(2,1)S(1)} %first.1._), channel_id=1, source_target_pairs={{0,15},{1,2},{2,1},{3,4},{4,3},{5,6},{6,5},{7,8},{8,7},{9,10},{10,... | collective-permute-start | bytes 1179656 | tf_op jit(solution)/shard_map/ppermute | solution.py:267
  4.0 2.1 %pack.1 = (bf16[3,512,256]{2,1,0:T(8,128)(2,1)S(1)}, bf16[3,768,256]{2,1,0:T(8,128)(2,1)S(1)}, bf16[3,768,256]{2,1,0:T(8,128)(2,1)S(1)}, bf16[3,768,256]{2,1,0:T(8,128)(2,1)S(1)}) custom-call(s32[8,48]{1,0:T(8,128)} %bitcast.2, bf16[3,8,256,256]{3,2,1,0:T(8,128)(2,1)} %blocks.3, bf16[3,256,256]{2,1,0:T(8,128)(2,1)S(1)} %first.1._), custom_call_target="tpu_custom_call" | custom-call | flops 1 | bytes 1 | tf_op jit(solution)/shard_map/pack/pallas_call | solution.py:110
  6.1 0.1 collective-permute-start.2
  6.2 2.9 %collective-permute-start.3 = (bf16[3,768,256]{2,1,0:T(8,128)(2,1)S(1)}, bf16[3,768,256]{2,1,0:T(8,128)(2,1)S(1)}, u32[]{:S(2)}, u32[]{:S(2)}) collective-permute-start(bf16[3,768,256]{2,1,0:T(8,128)(2,1)S(1)} %get-tuple-element.26.inner), channel_id=1, source_target_pairs={{0,1},{1,0},{2,3},{3,2},{4,5},{5,4},{6,7},{7,6},{8,9},{9,8},{10,11... | collective-permute-start | bytes 3538952 | tf_op jit(solution)/shard_map/ppermute | solution.py:268
  9.1 0.0 collective-permute-start
  9.1 4.4 %collective-permute-start.4 = (bf16[3,768,256]{2,1,0:T(8,128)(2,1)S(1)}, bf16[3,768,256]{2,1,0:T(8,128)(2,1)S(1)}, u32[]{:S(2)}, u32[]{:S(2)}) collective-permute-start(bf16[3,768,256]{2,1,0:T(8,128)(2,1)S(1)} %get-tuple-element.22.own), channel_id=1, source_target_pairs={{0,1},{1,0},{2,3},{3,2},{4,5},{5,4},{6,7},{7,6},{8,9},{9,8},{10,11... | collective-permute-start | bytes 3538952 | tf_op jit(solution)/shard_map/ppermute | solution.py:268
  13.5 20.5 %collective-permute-done.1.from_first = bf16[3,256,256]{2,1,0:T(8,128)(2,1)S(1)} collective-permute-done((bf16[3,256,256]{2,1,0:T(8,128)(2,1)S(1)}, bf16[3,256,256]{2,1,0:T(8,128)(2,1)S(1)}, u32[]{:S(2)}, u32[]{:S(2)}) %collective-permute-start.1) | collective-permute-done | bytes 393248 | tf_op jit(solution)/shard_map/ppermute | solution.py:267
  34.0 0.8 begin_kernel.1.part
  34.8 0.0 copy-start
  34.8 8.4 %collective-permute-done.2.from_others = bf16[3,512,256]{2,1,0:T(8,128)(2,1)S(1)} collective-permute-done((bf16[3,512,256]{2,1,0:T(8,128)(2,1)S(1)}, bf16[3,512,256]{2,1,0:T(8,128)(2,1)S(1)}, u32[]{:S(2)}, u32[]{:S(2)}) %collective-permute-start.2) | collective-permute-done | bytes 786464 | tf_op jit(solution)/shard_map/ppermute | solution.py:267
  43.2 1.2 %outer_kernel.1 = (bf16[3,768,256]{2,1,0:T(8,128)(2,1)S(1)}, f32[3,768,256]{2,1,0:T(8,128)S(1)}) custom-call(bf16[3,768,256]{2,1,0:T(8,128)(2,1)S(1)} %get-tuple-element.23.outer, bf16[3,256,256]{2,1,0:T(8,128)(2,1)S(1)} %collective-permute-done.1.from_first, bf16[3,512,256]{2,1,0:T(8,128)(2,1)S(1)} %collective-permute-done.2.from_others, ...), custom_call_target="tpu_custom_call" | custom-call | flops 5000000000 | bytes 1 | tf_op jit(solution)/shard_map/outer_kernel/pallas_call | solution.py:284
  44.4 0.0 collective-permute-done.3.from_inner
  44.4 0.0 copy-done
  44.4 3.1 %square_kernel.1 = (bf16[3,768,256]{2,1,0:T(8,128)(2,1)S(1)}, bf16[2,768,256]{2,1,0:T(8,128)(2,1)S(1)}) custom-call(s32[8,48]{1,0:T(8,128)S(1)} %bitcast.3, bf16[3,768,256]{2,1,0:T(8,128)(2,1)S(1)} %get-tuple-element.22.own, bf16[3,768,256]{2,1,0:T(8,128)(2,1)S(1)} %get-tuple-element.26.inner, bf16[3,768,256]{2,1,0:T(8,128)(2,1)S(1)} %collective-permute-done.3.from_inner, ...), custom_call_target="tpu_custom_call" | custom-call | flops 1 | bytes 1 | tf_op jit(solution)/shard_map/square_kernel/pallas_call | solution.py:284
  47.5 0.1 collective-permute-start.7
  47.6 1.8 %collective-permute-start.6 = (bf16[2,768,256]{2,1,0:T(8,128)(2,1)S(1)}, bf16[2,768,256]{2,1,0:T(8,128)(2,1)S(1)}, u32[]{:S(2)}, u32[]{:S(2)}) collective-permute-start(bf16[2,768,256]{2,1,0:T(8,128)(2,1)S(1)} %get-tuple-element.32), channel_id=1, source_target_pairs={{0,15},{1,2},{2,1},{3,4},{4,3},{5,6},{6,5},{7,8},{8,7},{9,10},{10,... | collective-permute-start | bytes 2359304 | tf_op jit(solution)/shard_map/ppermute | solution.py:267
  49.4 0.0 collective-permute-done.4.inner_own
  49.4 10.3 %early_kernel.1 = (f32[3,768,256]{2,1,0:T(8,128)S(1)}, f32[3,768,256]{2,1,0:T(8,128)S(1)}, f32[3,768,256]{2,1,0:T(8,128)S(1)}, f32[3,768,256]{2,1,0:T(8,128)S(1)}) custom-call(s32[8,48]{1,0:T(8,128)S(1)} %bitcast.4, bf16[3,768,256]{2,1,0:T(8,128)(2,1)S(1)} %get-tuple-element.22.own, bf16[3,768,256]{2,1,0:T(8,128)(2,1)S(1)} %get-tuple-element.26.inner, ...), custom_call_target="tpu_custom_call" | custom-call | flops 1 | bytes 1 | tf_op jit(solution)/shard_map/early_kernel/pallas_call | solution.py:284
  59.7 4.5 %collective-permute-done.outer_own = bf16[3,768,256]{2,1,0:T(8,128)(2,1)S(1)} collective-permute-done((bf16[3,768,256]{2,1,0:T(8,128)(2,1)S(1)}, bf16[3,768,256]{2,1,0:T(8,128)(2,1)S(1)}, u32[]{:S(2)}, u32[]{:S(2)}) %collective-permute-start) | collective-permute-done | bytes 1179680 | tf_op jit(solution)/shard_map/ppermute | solution.py:267
  64.2 3.0 %ahead_kernel.1 = (bf16[3,768,256]{2,1,0:T(8,128)(2,1)S(1)}, bf16[1,768,256]{2,1,0:T(8,128)(2,1)S(1)}, s32[3,8,128]{2,1,0:T(8,128)S(1)}) custom-call(s32[8,48]{1,0:T(8,128)S(1)} %bitcast.5, bf16[3,768,256]{2,1,0:T(8,128)(2,1)S(1)} %collective-permute-done.outer_own, bf16[3,768,256]{2,1,0:T(8,128)(2,1)S(1)} %get-tuple-element.25.from_outer, ...), custom_call_target="tpu_custom_call" | custom-call | flops 1 | bytes 1 | tf_op jit(solution)/shard_map/ahead_kernel/pallas_call | solution.py:284
  67.3 1.8 %collective-permute-start.5 = (bf16[1,768,256]{2,1,0:T(8,128)(2,1)S(1)}, bf16[1,768,256]{2,1,0:T(8,128)(2,1)S(1)}, u32[]{:S(2)}, u32[]{:S(2)}) collective-permute-start(bf16[1,768,256]{2,1,0:T(8,128)(2,1)S(1)} %get-tuple-element.31), channel_id=1, source_target_pairs={{0,15},{1,2},{2,1},{3,4},{4,3},{5,6},{6,5},{7,8},{8,7},{9,10},{10,... | collective-permute-start | bytes 1179656 | tf_op jit(solution)/shard_map/ppermute | solution.py:267
  69.1 0.0 collective-permute-done.7.s_inner_own
  69.1 4.9 %late_kernel.1 = (bf16[3,8,256,256]{3,2,1,0:T(8,128)(2,1)}, f32[3,768,256]{2,1,0:T(8,128)S(1)}) custom-call(s32[8,48]{1,0:T(8,128)S(1)} %bitcast.6, bf16[3,768,256]{2,1,0:T(8,128)(2,1)S(1)} %get-tuple-element.22.own, bf16[3,768,256]{2,1,0:T(8,128)(2,1)S(1)} %get-tuple-element.23.outer, bf16[3,768,256]{2,1,0:T(8,128)(2,1)S(1)} %collective-permute-done.outer_own, ...), custom_call_target="tpu_custom_call" | custom-call | flops 1 | bytes 1 | tf_op jit(solution)/shard_map/late_kernel/pallas_call | solution.py:284
  74.0 2.9 %collective-permute-done.6.s_outer_head = bf16[2,768,256]{2,1,0:T(8,128)(2,1)S(1)} collective-permute-done((bf16[2,768,256]{2,1,0:T(8,128)(2,1)S(1)}, bf16[2,768,256]{2,1,0:T(8,128)(2,1)S(1)}, u32[]{:S(2)}, u32[]{:S(2)}) %collective-permute-start.6) | collective-permute-done | bytes 786464 | tf_op jit(solution)/shard_map/ppermute | solution.py:267
  76.9 2.4 %head_kernel.1._ = bf16[3,8,256,256]{3,2,1,0:T(8,128)(2,1)} custom-call(s32[8,48]{1,0:T(8,128)S(1)} %bitcast.7, bf16[3,768,256]{2,1,0:T(8,128)(2,1)S(1)} %get-tuple-element.23.outer, bf16[2,768,256]{2,1,0:T(8,128)(2,1)S(1)} %collective-permute-done.6.s_outer_head, f32[3,768,256]{2,1,0:T(8,128)S(1)} %get-tuple-element.37.rest, ...), custom_call_target="tpu_custom_call", output_to_operand_aliasing={{}: (4, {})} | custom-call | flops 1 | bytes 1 | tf_op jit(solution)/shard_map/head_kernel/pallas_call | solution.py:284
  79.2 1.8 %collective-permute-done.5.panel = bf16[1,768,256]{2,1,0:T(8,128)(2,1)S(1)} collective-permute-done((bf16[1,768,256]{2,1,0:T(8,128)(2,1)S(1)}, bf16[1,768,256]{2,1,0:T(8,128)(2,1)S(1)}, u32[]{:S(2)}, u32[]{:S(2)}) %collective-permute-start.5) | collective-permute-done | bytes 393248 | tf_op jit(solution)/shard_map/ppermute | solution.py:267
  81.1 1.0 %tail_kernel.1 = bf16[3,8,256,256]{3,2,1,0:T(8,128)(2,1)} custom-call(s32[3,8,128]{2,1,0:T(8,128)S(1)} %get-tuple-element.30.slots, bf16[1,768,256]{2,1,0:T(8,128)(2,1)S(1)} %collective-permute-done.5.panel, bf16[3,8,256,256]{3,2,1,0:T(8,128)(2,1)} %head_kernel.1._), custom_call_target="tpu_custom_call", output_to_operand_aliasing={{}: (2, {})} | custom-call | flops 1 | bytes 1 | tf_op jit(solution)/shard_map/tail_kernel/pallas_call | solution.py:324
Async XLA Ops:
  1.3 32.7 %collective-permute-start.1 = (bf16[3,256,256]{2,1,0:T(8,128)(2,1)S(1)}, bf16[3,256,256]{2,1,0:T(8,128)(2,1)S(1)}, u32[]{:S(2)}, u32[]{:S(2)}) collective-permute-start(bf16[3,256,256]{2,1,0:T(8,128)(2,1)S(1)} %first.1._), channel_id=1, source_target_pairs={{0,15},{1,2},{2,1},{3,4},{4,3},{5,6},{6,5},{7,8},{8,7},{9,10},{10,... | collective-permute-start | bytes 1179656 | tf_op jit(solution)/shard_map/ppermute | solution.py:267
  6.1 37.1 %collective-permute-start.2 = (bf16[3,512,256]{2,1,0:T(8,128)(2,1)S(1)}, bf16[3,512,256]{2,1,0:T(8,128)(2,1)S(1)}, u32[]{:S(2)}, u32[]{:S(2)}) collective-permute-start(bf16[3,512,256]{2,1,0:T(8,128)(2,1)S(1)} %get-tuple-element.24), channel_id=1, source_target_pairs={{0,15},{1,2},{2,1},{3,4},{4,3},{5,6},{6,5},{7,8},{8,7},{9,10},{10,... | collective-permute-start | bytes 2359304 | tf_op jit(solution)/shard_map/ppermute | solution.py:267
  6.2 38.2 %collective-permute-start.3 = (bf16[3,768,256]{2,1,0:T(8,128)(2,1)S(1)}, bf16[3,768,256]{2,1,0:T(8,128)(2,1)S(1)}, u32[]{:S(2)}, u32[]{:S(2)}) collective-permute-start(bf16[3,768,256]{2,1,0:T(8,128)(2,1)S(1)} %get-tuple-element.26.inner), channel_id=1, source_target_pairs={{0,1},{1,0},{2,3},{3,2},{4,5},{5,4},{6,7},{7,6},{8,9},{9,8},{10,11... | collective-permute-start | bytes 3538952 | tf_op jit(solution)/shard_map/ppermute | solution.py:268
  9.1 55.1 %collective-permute-start = (bf16[3,768,256]{2,1,0:T(8,128)(2,1)S(1)}, bf16[3,768,256]{2,1,0:T(8,128)(2,1)S(1)}, u32[]{:S(2)}, u32[]{:S(2)}) collective-permute-start(bf16[3,768,256]{2,1,0:T(8,128)(2,1)S(1)} %get-tuple-element.22.own), channel_id=1, source_target_pairs={{0,15},{1,2},{2,1},{3,4},{4,3},{5,6},{6,5},{7,8},{8,7},{9,10},{10,... | collective-permute-start | bytes 3538952 | tf_op jit(solution)/shard_map/ppermute | solution.py:267
  9.1 40.3 %collective-permute-start.4 = (bf16[3,768,256]{2,1,0:T(8,128)(2,1)S(1)}, bf16[3,768,256]{2,1,0:T(8,128)(2,1)S(1)}, u32[]{:S(2)}, u32[]{:S(2)}) collective-permute-start(bf16[3,768,256]{2,1,0:T(8,128)(2,1)S(1)} %get-tuple-element.22.own), channel_id=1, source_target_pairs={{0,1},{1,0},{2,3},{3,2},{4,5},{5,4},{6,7},{7,6},{8,9},{9,8},{10,11... | collective-permute-start | bytes 3538952 | tf_op jit(solution)/shard_map/ppermute | solution.py:268
  34.8 9.6 %copy-start = (s32[48,8]{0,1:T(8,128)S(1)}, s32[48,8]{0,1:T(8,128)}, u32[]{:S(2)}) copy-start(s32[48,8]{0,1:T(8,128)} %param.3) | copy-start | bytes 4612
  47.5 21.5 %collective-permute-start.7 = (bf16[3,768,256]{2,1,0:T(8,128)(2,1)S(1)}, bf16[3,768,256]{2,1,0:T(8,128)(2,1)S(1)}, u32[]{:S(2)}, u32[]{:S(2)}) collective-permute-start(bf16[3,768,256]{2,1,0:T(8,128)(2,1)S(1)} %get-tuple-element.28.s_own), channel_id=1, source_target_pairs={{0,1},{1,0},{2,3},{3,2},{4,5},{5,4},{6,7},{7,6},{8,9},{9,8},{10,11... | collective-permute-start | bytes 3538952 | tf_op jit(solution)/shard_map/ppermute | solution.py:268
  47.6 29.3 %collective-permute-start.6 = (bf16[2,768,256]{2,1,0:T(8,128)(2,1)S(1)}, bf16[2,768,256]{2,1,0:T(8,128)(2,1)S(1)}, u32[]{:S(2)}, u32[]{:S(2)}) collective-permute-start(bf16[2,768,256]{2,1,0:T(8,128)(2,1)S(1)} %get-tuple-element.32), channel_id=1, source_target_pairs={{0,15},{1,2},{2,1},{3,4},{4,3},{5,6},{6,5},{7,8},{8,7},{9,10},{10,... | collective-permute-start | bytes 2359304 | tf_op jit(solution)/shard_map/ppermute | solution.py:267
  67.3 13.8 %collective-permute-start.5 = (bf16[1,768,256]{2,1,0:T(8,128)(2,1)S(1)}, bf16[1,768,256]{2,1,0:T(8,128)(2,1)S(1)}, u32[]{:S(2)}, u32[]{:S(2)}) collective-permute-start(bf16[1,768,256]{2,1,0:T(8,128)(2,1)S(1)} %get-tuple-element.31), channel_id=1, source_target_pairs={{0,15},{1,2},{2,1},{3,4},{4,3},{5,6},{6,5},{7,8},{8,7},{9,10},{10,... | collective-permute-start | bytes 1179656 | tf_op jit(solution)/shard_map/ppermute | solution.py:267

commit v7 on v6

--- a/solution.py
+++ b/solution.py
@@ -252,7 +252,7 @@
 def tail_kernel(rb, bs, slots, panel, _, out, sems):
     waits = []
     for r in range(rb):
-        slot = jnp.max(slots[r])
+        slot = slots[r, 0, 0]
         copy = pltpu.make_async_copy(panel.at[0, pl.ds(r * bs, bs), :], out.at[r, jnp.maximum(slot, 0)], sems.at[r])
         pl.when(slot >= 0)(copy.start)
         waits.append((slot, copy))

time: 82.2 us -> 82.1 us (level)
  no operation moved by 1% of the time
where the time goes in v7:
time: 82.1 us; the launch traced here: 81.9 us
  waiting for transfers between devices  38.1 us (46%)
  Pallas kernels  29.9 us (36%)
  starting transfers between devices  13.8 us (17%)
    ppermute x5, waiting for transfers between devices, local(): to_outer = lambda x: lax.ppermute(x, 'grid', over)  38.1 us
    pallas_call x7, Pallas kernels, call(): pl.pallas_call(functools.partial(kernel, devices, rb, bs), out_shape=outs...  25.7 us
    ppermute x3, starting transfers between devices, local(): to_inner = lambda x: lax.ppermute(x, 'grid', across)  7.37 us
    ppermute x5, starting transfers between devices, local(): to_outer = lambda x: lax.ppermute(x, 'grid', over)  6.39 us
    pallas_call x1, Pallas kernels, pack(): pl.pallas_call(functools.partial(pack_kernel, devices, rb, bs), out_shape...  2.09 us
  transfers between devices with their start and end apart: 8, of which 5 were waited for; matrix products, arithmetic and copies ran while one was open for 0% of the time, Pallas kernels for 34%

profile of v7, /device:TPU:1, one launch (start us, length us, event | category | flops | bytes accessed | tf_op | source)
XLA Modules:
  0.0 81.9 jit_solution(3182601605644390397)
XLA Ops:
  0.0 1.3 %first.1._ = bf16[3,256,256]{2,1,0:T(8,128)(2,1)S(1)} custom-call(s32[8,48]{1,0:T(8,128)} %bitcast.1, bf16[3,8,256,256]{3,2,1,0:T(8,128)(2,1)} %blocks.3), custom_call_target="tpu_custom_call" | custom-call | flops 1 | bytes 1 | tf_op jit(solution)/shard_map/first/pallas_call | solution.py:95
  1.3 2.7 %collective-permute-start.1 = (bf16[3,256,256]{2,1,0:T(8,128)(2,1)S(1)}, bf16[3,256,256]{2,1,0:T(8,128)(2,1)S(1)}, u32[]{:S(2)}, u32[]{:S(2)}) collective-permute-start(bf16[3,256,256]{2,1,0:T(8,128)(2,1)S(1)} %first.1._), channel_id=1, source_target_pairs={{0,15},{1,2},{2,1},{3,4},{4,3},{5,6},{6,5},{7,8},{8,7},{9,10},{10,... | collective-permute-start | bytes 1179656 | tf_op jit(solution)/shard_map/ppermute | solution.py:267
  4.0 2.1 %pack.1 = (bf16[3,512,256]{2,1,0:T(8,128)(2,1)S(1)}, bf16[3,768,256]{2,1,0:T(8,128)(2,1)S(1)}, bf16[3,768,256]{2,1,0:T(8,128)(2,1)S(1)}, bf16[3,768,256]{2,1,0:T(8,128)(2,1)S(1)}) custom-call(s32[8,48]{1,0:T(8,128)} %bitcast.2, bf16[3,8,256,256]{3,2,1,0:T(8,128)(2,1)} %blocks.3, bf16[3,256,256]{2,1,0:T(8,128)(2,1)S(1)} %first.1._), custom_call_target="tpu_custom_call" | custom-call | flops 1 | bytes 1 | tf_op jit(solution)/shard_map/pack/pallas_call | solution.py:110
  6.1 0.1 collective-permute-start.2
  6.2 2.9 %collective-permute-start.3 = (bf16[3,768,256]{2,1,0:T(8,128)(2,1)S(1)}, bf16[3,768,256]{2,1,0:T(8,128)(2,1)S(1)}, u32[]{:S(2)}, u32[]{:S(2)}) collective-permute-start(bf16[3,768,256]{2,1,0:T(8,128)(2,1)S(1)} %get-tuple-element.26.inner), channel_id=1, source_target_pairs={{0,1},{1,0},{2,3},{3,2},{4,5},{5,4},{6,7},{7,6},{8,9},{9,8},{10,11... | collective-permute-start | bytes 3538952 | tf_op jit(solution)/shard_map/ppermute | solution.py:268
  9.1 0.0 collective-permute-start
  9.1 4.4 %collective-permute-start.4 = (bf16[3,768,256]{2,1,0:T(8,128)(2,1)S(1)}, bf16[3,768,256]{2,1,0:T(8,128)(2,1)S(1)}, u32[]{:S(2)}, u32[]{:S(2)}) collective-permute-start(bf16[3,768,256]{2,1,0:T(8,128)(2,1)S(1)} %get-tuple-element.22.own), channel_id=1, source_target_pairs={{0,1},{1,0},{2,3},{3,2},{4,5},{5,4},{6,7},{7,6},{8,9},{9,8},{10,11... | collective-permute-start | bytes 3538952 | tf_op jit(solution)/shard_map/ppermute | solution.py:268
  13.5 20.5 %collective-permute-done.1.from_first = bf16[3,256,256]{2,1,0:T(8,128)(2,1)S(1)} collective-permute-done((bf16[3,256,256]{2,1,0:T(8,128)(2,1)S(1)}, bf16[3,256,256]{2,1,0:T(8,128)(2,1)S(1)}, u32[]{:S(2)}, u32[]{:S(2)}) %collective-permute-start.1) | collective-permute-done | bytes 393248 | tf_op jit(solution)/shard_map/ppermute | solution.py:267
  34.0 0.8 begin_kernel.1.part
  34.8 0.0 copy-start
  34.8 8.4 %collective-permute-done.2.from_others = bf16[3,512,256]{2,1,0:T(8,128)(2,1)S(1)} collective-permute-done((bf16[3,512,256]{2,1,0:T(8,128)(2,1)S(1)}, bf16[3,512,256]{2,1,0:T(8,128)(2,1)S(1)}, u32[]{:S(2)}, u32[]{:S(2)}) %collective-permute-start.2) | collective-permute-done | bytes 786464 | tf_op jit(solution)/shard_map/ppermute | solution.py:267
  43.2 1.2 %outer_kernel.1 = (bf16[3,768,256]{2,1,0:T(8,128)(2,1)S(1)}, f32[3,768,256]{2,1,0:T(8,128)S(1)}) custom-call(bf16[3,768,256]{2,1,0:T(8,128)(2,1)S(1)} %get-tuple-element.23.outer, bf16[3,256,256]{2,1,0:T(8,128)(2,1)S(1)} %collective-permute-done.1.from_first, bf16[3,512,256]{2,1,0:T(8,128)(2,1)S(1)} %collective-permute-done.2.from_others, ...), custom_call_target="tpu_custom_call" | custom-call | flops 5000000000 | bytes 1 | tf_op jit(solution)/shard_map/outer_kernel/pallas_call | solution.py:284
  44.4 0.0 collective-permute-done.3.from_inner
  44.4 0.0 copy-done
  44.4 3.1 %square_kernel.1 = (bf16[3,768,256]{2,1,0:T(8,128)(2,1)S(1)}, bf16[2,768,256]{2,1,0:T(8,128)(2,1)S(1)}) custom-call(s32[8,48]{1,0:T(8,128)S(1)} %bitcast.3, bf16[3,768,256]{2,1,0:T(8,128)(2,1)S(1)} %get-tuple-element.22.own, bf16[3,768,256]{2,1,0:T(8,128)(2,1)S(1)} %get-tuple-element.26.inner, bf16[3,768,256]{2,1,0:T(8,128)(2,1)S(1)} %collective-permute-done.3.from_inner, ...), custom_call_target="tpu_custom_call" | custom-call | flops 1 | bytes 1 | tf_op jit(solution)/shard_map/square_kernel/pallas_call | solution.py:284
  47.5 0.1 collective-permute-start.7
  47.6 1.8 %collective-permute-start.6 = (bf16[2,768,256]{2,1,0:T(8,128)(2,1)S(1)}, bf16[2,768,256]{2,1,0:T(8,128)(2,1)S(1)}, u32[]{:S(2)}, u32[]{:S(2)}) collective-permute-start(bf16[2,768,256]{2,1,0:T(8,128)(2,1)S(1)} %get-tuple-element.32), channel_id=1, source_target_pairs={{0,15},{1,2},{2,1},{3,4},{4,3},{5,6},{6,5},{7,8},{8,7},{9,10},{10,... | collective-permute-start | bytes 2359304 | tf_op jit(solution)/shard_map/ppermute | solution.py:267
  49.4 0.0 collective-permute-done.4.inner_own
  49.4 10.3 %early_kernel.1 = (f32[3,768,256]{2,1,0:T(8,128)S(1)}, f32[3,768,256]{2,1,0:T(8,128)S(1)}, f32[3,768,256]{2,1,0:T(8,128)S(1)}, f32[3,768,256]{2,1,0:T(8,128)S(1)}) custom-call(s32[8,48]{1,0:T(8,128)S(1)} %bitcast.4, bf16[3,768,256]{2,1,0:T(8,128)(2,1)S(1)} %get-tuple-element.22.own, bf16[3,768,256]{2,1,0:T(8,128)(2,1)S(1)} %get-tuple-element.26.inner, ...), custom_call_target="tpu_custom_call" | custom-call | flops 1 | bytes 1 | tf_op jit(solution)/shard_map/early_kernel/pallas_call | solution.py:284
  59.7 4.5 %collective-permute-done.outer_own = bf16[3,768,256]{2,1,0:T(8,128)(2,1)S(1)} collective-permute-done((bf16[3,768,256]{2,1,0:T(8,128)(2,1)S(1)}, bf16[3,768,256]{2,1,0:T(8,128)(2,1)S(1)}, u32[]{:S(2)}, u32[]{:S(2)}) %collective-permute-start) | collective-permute-done | bytes 1179680 | tf_op jit(solution)/shard_map/ppermute | solution.py:267
  64.2 3.0 %ahead_kernel.1 = (bf16[3,768,256]{2,1,0:T(8,128)(2,1)S(1)}, bf16[1,768,256]{2,1,0:T(8,128)(2,1)S(1)}, s32[3,8,128]{2,1,0:T(8,128)S(1)}) custom-call(s32[8,48]{1,0:T(8,128)S(1)} %bitcast.5, bf16[3,768,256]{2,1,0:T(8,128)(2,1)S(1)} %collective-permute-done.outer_own, bf16[3,768,256]{2,1,0:T(8,128)(2,1)S(1)} %get-tuple-element.25.from_outer, ...), custom_call_target="tpu_custom_call" | custom-call | flops 1 | bytes 1 | tf_op jit(solution)/shard_map/ahead_kernel/pallas_call | solution.py:284
  67.3 1.8 %collective-permute-start.5 = (bf16[1,768,256]{2,1,0:T(8,128)(2,1)S(1)}, bf16[1,768,256]{2,1,0:T(8,128)(2,1)S(1)}, u32[]{:S(2)}, u32[]{:S(2)}) collective-permute-start(bf16[1,768,256]{2,1,0:T(8,128)(2,1)S(1)} %get-tuple-element.31), channel_id=1, source_target_pairs={{0,15},{1,2},{2,1},{3,4},{4,3},{5,6},{6,5},{7,8},{8,7},{9,10},{10,... | collective-permute-start | bytes 1179656 | tf_op jit(solution)/shard_map/ppermute | solution.py:267
  69.1 0.0 collective-permute-done.7.s_inner_own
  69.1 4.9 %late_kernel.1 = (bf16[3,8,256,256]{3,2,1,0:T(8,128)(2,1)}, f32[3,768,256]{2,1,0:T(8,128)S(1)}) custom-call(s32[8,48]{1,0:T(8,128)S(1)} %bitcast.6, bf16[3,768,256]{2,1,0:T(8,128)(2,1)S(1)} %get-tuple-element.22.own, bf16[3,768,256]{2,1,0:T(8,128)(2,1)S(1)} %get-tuple-element.23.outer, bf16[3,768,256]{2,1,0:T(8,128)(2,1)S(1)} %collective-permute-done.outer_own, ...), custom_call_target="tpu_custom_call" | custom-call | flops 1 | bytes 1 | tf_op jit(solution)/shard_map/late_kernel/pallas_call | solution.py:284
  74.0 2.9 %collective-permute-done.6.s_outer_head = bf16[2,768,256]{2,1,0:T(8,128)(2,1)S(1)} collective-permute-done((bf16[2,768,256]{2,1,0:T(8,128)(2,1)S(1)}, bf16[2,768,256]{2,1,0:T(8,128)(2,1)S(1)}, u32[]{:S(2)}, u32[]{:S(2)}) %collective-permute-start.6) | collective-permute-done | bytes 786464 | tf_op jit(solution)/shard_map/ppermute | solution.py:267
  76.9 2.4 %head_kernel.1._ = bf16[3,8,256,256]{3,2,1,0:T(8,128)(2,1)} custom-call(s32[8,48]{1,0:T(8,128)S(1)} %bitcast.7, bf16[3,768,256]{2,1,0:T(8,128)(2,1)S(1)} %get-tuple-element.23.outer, bf16[2,768,256]{2,1,0:T(8,128)(2,1)S(1)} %collective-permute-done.6.s_outer_head, f32[3,768,256]{2,1,0:T(8,128)S(1)} %get-tuple-element.37.rest, ...), custom_call_target="tpu_custom_call", output_to_operand_aliasing={{}: (4, {})} | custom-call | flops 1 | bytes 1 | tf_op jit(solution)/shard_map/head_kernel/pallas_call | solution.py:284
  79.2 1.8 %collective-permute-done.5.panel = bf16[1,768,256]{2,1,0:T(8,128)(2,1)S(1)} collective-permute-done((bf16[1,768,256]{2,1,0:T(8,128)(2,1)S(1)}, bf16[1,768,256]{2,1,0:T(8,128)(2,1)S(1)}, u32[]{:S(2)}, u32[]{:S(2)}) %collective-permute-start.5) | collective-permute-done | bytes 393248 | tf_op jit(solution)/shard_map/ppermute | solution.py:267
  81.1 0.8 tail_kernel.1
Async XLA Ops:
  1.3 32.7 %collective-permute-start.1 = (bf16[3,256,256]{2,1,0:T(8,128)(2,1)S(1)}, bf16[3,256,256]{2,1,0:T(8,128)(2,1)S(1)}, u32[]{:S(2)}, u32[]{:S(2)}) collective-permute-start(bf16[3,256,256]{2,1,0:T(8,128)(2,1)S(1)} %first.1._), channel_id=1, source_target_pairs={{0,15},{1,2},{2,1},{3,4},{4,3},{5,6},{6,5},{7,8},{8,7},{9,10},{10,... | collective-permute-start | bytes 1179656 | tf_op jit(solution)/shard_map/ppermute | solution.py:267
  6.1 37.1 %collective-permute-start.2 = (bf16[3,512,256]{2,1,0:T(8,128)(2,1)S(1)}, bf16[3,512,256]{2,1,0:T(8,128)(2,1)S(1)}, u32[]{:S(2)}, u32[]{:S(2)}) collective-permute-start(bf16[3,512,256]{2,1,0:T(8,128)(2,1)S(1)} %get-tuple-element.24), channel_id=1, source_target_pairs={{0,15},{1,2},{2,1},{3,4},{4,3},{5,6},{6,5},{7,8},{8,7},{9,10},{10,... | collective-permute-start | bytes 2359304 | tf_op jit(solution)/shard_map/ppermute | solution.py:267
  6.2 38.2 %collective-permute-start.3 = (bf16[3,768,256]{2,1,0:T(8,128)(2,1)S(1)}, bf16[3,768,256]{2,1,0:T(8,128)(2,1)S(1)}, u32[]{:S(2)}, u32[]{:S(2)}) collective-permute-start(bf16[3,768,256]{2,1,0:T(8,128)(2,1)S(1)} %get-tuple-element.26.inner), channel_id=1, source_target_pairs={{0,1},{1,0},{2,3},{3,2},{4,5},{5,4},{6,7},{7,6},{8,9},{9,8},{10,11... | collective-permute-start | bytes 3538952 | tf_op jit(solution)/shard_map/ppermute | solution.py:268
  9.1 55.1 %collective-permute-start = (bf16[3,768,256]{2,1,0:T(8,128)(2,1)S(1)}, bf16[3,768,256]{2,1,0:T(8,128)(2,1)S(1)}, u32[]{:S(2)}, u32[]{:S(2)}) collective-permute-start(bf16[3,768,256]{2,1,0:T(8,128)(2,1)S(1)} %get-tuple-element.22.own), channel_id=1, source_target_pairs={{0,15},{1,2},{2,1},{3,4},{4,3},{5,6},{6,5},{7,8},{8,7},{9,10},{10,... | collective-permute-start | bytes 3538952 | tf_op jit(solution)/shard_map/ppermute | solution.py:267
  9.1 40.3 %collective-permute-start.4 = (bf16[3,768,256]{2,1,0:T(8,128)(2,1)S(1)}, bf16[3,768,256]{2,1,0:T(8,128)(2,1)S(1)}, u32[]{:S(2)}, u32[]{:S(2)}) collective-permute-start(bf16[3,768,256]{2,1,0:T(8,128)(2,1)S(1)} %get-tuple-element.22.own), channel_id=1, source_target_pairs={{0,1},{1,0},{2,3},{3,2},{4,5},{5,4},{6,7},{7,6},{8,9},{9,8},{10,11... | collective-permute-start | bytes 3538952 | tf_op jit(solution)/shard_map/ppermute | solution.py:268
  34.8 9.6 %copy-start = (s32[48,8]{0,1:T(8,128)S(1)}, s32[48,8]{0,1:T(8,128)}, u32[]{:S(2)}) copy-start(s32[48,8]{0,1:T(8,128)} %param.3) | copy-start | bytes 4612
  47.5 21.5 %collective-permute-start.7 = (bf16[3,768,256]{2,1,0:T(8,128)(2,1)S(1)}, bf16[3,768,256]{2,1,0:T(8,128)(2,1)S(1)}, u32[]{:S(2)}, u32[]{:S(2)}) collective-permute-start(bf16[3,768,256]{2,1,0:T(8,128)(2,1)S(1)} %get-tuple-element.28.s_own), channel_id=1, source_target_pairs={{0,1},{1,0},{2,3},{3,2},{4,5},{5,4},{6,7},{7,6},{8,9},{9,8},{10,11... | collective-permute-start | bytes 3538952 | tf_op jit(solution)/shard_map/ppermute | solution.py:268
  47.6 29.3 %collective-permute-start.6 = (bf16[2,768,256]{2,1,0:T(8,128)(2,1)S(1)}, bf16[2,768,256]{2,1,0:T(8,128)(2,1)S(1)}, u32[]{:S(2)}, u32[]{:S(2)}) collective-permute-start(bf16[2,768,256]{2,1,0:T(8,128)(2,1)S(1)} %get-tuple-element.32), channel_id=1, source_target_pairs={{0,15},{1,2},{2,1},{3,4},{4,3},{5,6},{6,5},{7,8},{8,7},{9,10},{10,... | collective-permute-start | bytes 2359304 | tf_op jit(solution)/shard_map/ppermute | solution.py:267
  67.3 13.8 %collective-permute-start.5 = (bf16[1,768,256]{2,1,0:T(8,128)(2,1)S(1)}, bf16[1,768,256]{2,1,0:T(8,128)(2,1)S(1)}, u32[]{:S(2)}, u32[]{:S(2)}) collective-permute-start(bf16[1,768,256]{2,1,0:T(8,128)(2,1)S(1)} %get-tuple-element.31), channel_id=1, source_target_pairs={{0,15},{1,2},{2,1},{3,4},{4,3},{5,6},{6,5},{7,8},{8,7},{9,10},{10,... | collective-permute-start | bytes 1179656 | tf_op jit(solution)/shard_map/ppermute | solution.py:267

commit v8 on v7

--- a/solution.py
+++ b/solution.py
@@ -16,6 +16,7 @@
 SMEM = pl.BlockSpec(memory_space=pltpu.SMEM)
 BRIEF = pl.CostEstimate(flops=1, bytes_accessed=1, transcendentals=0)
 LONGER = pl.CostEstimate(flops=5 * 10**9, bytes_accessed=1, transcendentals=0)
+LONGEST = pl.CostEstimate(flops=10**10, bytes_accessed=1, transcendentals=0)
 VMEM_LIMIT = 24 * 1024 * 1024
 
 
@@ -51,22 +52,22 @@
                 ref[j, pl.ds(r * bs, bs), :] = jnp.zeros((bs, bs), ref.dtype)
 
 
-def place(pattern, held, row, owner, columns, cut, first, rb, bs):
-    for j in range(rb):
-        slot = slot_of(pattern, owner * rb + row, columns * rb + j)
+def place(slots, held, cut, start, size):
+    for j, slot in enumerate(slots):
         block = held[jnp.maximum(slot, 0)]
-        cut[j, pl.ds((row - first) * bs, bs), :] = jnp.where(slot >= 0, block, jnp.zeros_like(block))
+        cut[j, pl.ds(start, size), :] = jnp.where(slot >= 0, block, jnp.zeros_like(block))
 
 
 def first_kernel(devices, rb, bs, pattern_hbm, blocks, cut, pattern, held, pattern_sem, sem):
     fetch = pltpu.make_async_copy(pattern_hbm, pattern, pattern_sem)
     fetch.start()
-    load = pltpu.make_async_copy(blocks.at[0], held, sem)
+    load = pltpu.make_async_copy(blocks.at[0, :, pl.ds(0, bs // 2), :], held, sem)
     load.start()
     me, other, _ = neighbours(devices)
     fetch.wait()
+    slots = [slot_of(pattern, me * rb, other * rb + j) for j in range(rb)]
     load.wait()
-    place(pattern, held, 0, me, other, cut, 0, rb, bs)
+    place(slots, held, cut, 0, bs // 2)
 
 
 def pack_kernel(devices, rb, bs, pattern_hbm, blocks, _, others, *rest):
@@ -82,24 +83,25 @@
     for r in range(rb):
         loads[r].wait()
         for cut, columns in zip(cuts, (other, me, partner)):
-            place(pattern, held.at[r], r, me, columns, cut, 0, rb, bs)
-    others[...] = cuts[0][:, pl.ds(bs, (rb - 1) * bs), :]
+            slots = [slot_of(pattern, me * rb + r, columns * rb + j) for j in range(rb)]
+            place(slots, held.at[r], cut, r * bs, bs)
+    others[...] = cuts[0][:, pl.ds(bs // 2, rb * bs - bs // 2), :]
 
 
 def pack(devices, pattern, blocks):
     rb, slots, bs, _ = blocks.shape
     pattern = pltpu.with_memory_space_constraint(pattern, pltpu.HBM)
     blocks = pltpu.with_memory_space_constraint(blocks, pltpu.HBM)
-    cut = lambda rows: jax.ShapeDtypeStruct((rb, rows * bs, bs), blocks.dtype)
+    cut = lambda rows: jax.ShapeDtypeStruct((rb, rows, bs), blocks.dtype)
     params = pltpu.CompilerParams(vmem_limit_bytes=VMEM_LIMIT)
     first = pl.pallas_call(
         functools.partial(first_kernel, devices, rb, bs),
-        out_shape=cut(1),
+        out_shape=cut(bs // 2),
         in_specs=[ANY, ANY],
         out_specs=VMEM,
         scratch_shapes=[
             pltpu.SMEM(pattern.shape, pattern.dtype),
-            pltpu.VMEM(blocks.shape[1:], blocks.dtype),
+            pltpu.VMEM((slots, bs // 2, bs), blocks.dtype),
             pltpu.SemaphoreType.DMA,
             pltpu.SemaphoreType.DMA,
         ],
@@ -109,7 +111,7 @@
     )(pattern, blocks)
     return first, *pl.pallas_call(
         functools.partial(pack_kernel, devices, rb, bs),
-        out_shape=[cut(rb - 1), cut(rb), cut(rb), cut(rb)],
+        out_shape=[cut(rb * bs - bs // 2)] + [cut(rb * bs)] * 3,
         in_specs=[ANY, ANY, ANY],
         out_specs=[VMEM] * 4,
         scratch_shapes=[
@@ -144,18 +146,22 @@
 def begin_kernel(devices, rb, bs, outer, from_first, part):
     @pl.loop(0, rb)
     def _(c):
-        part[c] = jnp.dot(outer[0], from_first[c], preferred_element_type=F32)
+        part[c] = jnp.dot(outer[0, :, pl.ds(0, bs // 2)], from_first[c], preferred_element_type=F32)
 
 
 def outer_kernel(devices, rb, bs, outer, from_first, from_others, part, from_outer, own_part):
-    from_outer[:, pl.ds(0, bs), :] = from_first[...]
-    from_outer[:, pl.ds(bs, (rb - 1) * bs), :] = from_others[...]
-
-    @pl.loop(0, rb)
-    def _(c):
-        total = part[c]
+    half = bs // 2
+    from_outer[:, pl.ds(0, half), :] = from_first[...]
+    from_outer[:, pl.ds(half, rb * bs - half), :] = from_others[...]
+
+    @pl.loop(0, rb)
+    def _(c):
+        total = part[c] + jnp.dot(
+            outer[0, :, pl.ds(half, half)], from_others[c, pl.ds(0, half), :], preferred_element_type=F32
+        )
         for k in range(1, rb):
-            total += jnp.dot(outer[k], from_others[c, pl.ds((k - 1) * bs, bs), :], preferred_element_type=F32)
+            rows = pl.ds(k * bs - half, bs)
+            total += jnp.dot(outer[k], from_others[c, rows, :], preferred_element_type=F32)
         own_part[c] = total
 
 
@@ -197,7 +203,7 @@
 
 
 def ahead_kernel(
-    devices, rb, bs, pattern, outer_own, from_outer, from_outer_part, s_own, s_from_outer, out_there, slots
+    devices, rb, bs, pattern, outer_own, from_outer, from_outer_part, s_own, s_from_outer, out_most, out_last, slots
 ):
     me, other, _ = neighbours(devices)
     last = rb - 1
@@ -210,7 +216,9 @@
 
     drop_absent(s_from_outer, pattern, other, me, rb, bs)
     cube = panel_product(outer_own, s_from_outer, last, rb, bs) + panel_product(from_outer, s_own, last, rb, bs)
-    out_there[0] = (3.0 * s_from_outer[last].astype(F32) - 2.0 * cube).astype(BF16)
+    out_there = (3.0 * s_from_outer[last].astype(F32) - 2.0 * cube).astype(BF16)
+    out_most[...] = out_there[: last * bs]
+    out_last[...] = out_there[last * bs :]
 
 
 def late_kernel(
@@ -249,11 +257,13 @@
     settle(waits)
 
 
-def tail_kernel(rb, bs, slots, panel, _, out, sems):
+def tail_kernel(first, bs, slots, blocks, _, out, sems):
     waits = []
-    for r in range(rb):
-        slot = slots[r, 0, 0]
-        copy = pltpu.make_async_copy(panel.at[0, pl.ds(r * bs, bs), :], out.at[r, jnp.maximum(slot, 0)], sems.at[r])
+    for r in range(blocks.shape[0] // bs):
+        slot = slots[first + r, 0, 0]
+        copy = pltpu.make_async_copy(
+            blocks.at[pl.ds(r * bs, bs), :], out.at[first + r, jnp.maximum(slot, 0)], sems.at[r]
+        )
         pl.when(slot >= 0)(copy.start)
         waits.append((slot, copy))
     settle(waits)
@@ -298,7 +308,7 @@
     outer_own = to_outer(own)
     from_inner, inner_own = to_inner(inner), to_inner(own)
 
-    (part,) = call(begin_kernel, (outer, from_first), (high,), patterned=False, cost=LONGER)
+    (part,) = call(begin_kernel, (outer, from_first), (high,), patterned=False, cost=LONGEST)
     from_outer, own_part = call(outer_kernel, (outer, from_first, from_others, part), (low, high), patterned=False, cost=LONGER)
     s_own, s_head = call(square_kernel, (own, inner, from_inner, own_part), (low, low_of(rb - 1)))
     s_outer_head = to_outer(s_head)
@@ -306,13 +316,18 @@
     cube_part, inner_part, from_outer_part, outer_part = call(
         early_kernel, (own, inner, outer, from_inner, inner_own, from_outer, s_own), (high,) * 4, 2
     )
-    s_from_outer, out_there, slots = call(
+    s_from_outer, out_most, out_last, slots = call(
         ahead_kernel,
         (outer_own, from_outer, from_outer_part, s_own),
-        (low, low_of(1), jax.ShapeDtypeStruct((rb, 8, 128), jnp.int32)),
+        (
+            low,
+            jax.ShapeDtypeStruct(((rb - 1) * bs, bs), BF16),
+            jax.ShapeDtypeStruct((bs, bs), BF16),
+            jax.ShapeDtypeStruct((rb, 8, 128), jnp.int32),
+        ),
         cost=BRIEF,
     )
-    out_here = to_outer(out_there)
+    arrivals = to_outer(out_most), to_outer(out_last)
     out, rest = call(
         late_kernel,
         (own, outer, outer_own, s_from_outer, s_own, outer_part, cube_part, inner, s_inner_own, inner_part),
@@ -321,17 +336,19 @@
         cost=BRIEF,
     )
     (out,) = call(head_kernel, (outer, s_outer_head, rest), (full,), 1, into=out, cost=BRIEF)
-    return pl.pallas_call(
-        functools.partial(tail_kernel, rb, bs),
-        out_shape=full,
-        in_specs=[VMEM, VMEM, ANY],
-        out_specs=ANY,
-        scratch_shapes=[pltpu.SemaphoreType.DMA((rb,))],
-        input_output_aliases={2: 0},
-        compiler_params=pltpu.CompilerParams(vmem_limit_bytes=VMEM_LIMIT),
-        cost_estimate=BRIEF,
-        name="tail_kernel",
-    )(slots, out_here, out)
+    for first, blocks in zip((0, rb - 1), arrivals):
+        out = pl.pallas_call(
+            functools.partial(tail_kernel, first, bs),
+            out_shape=full,
+            in_specs=[VMEM, VMEM, ANY],
+            out_specs=ANY,
+            scratch_shapes=[pltpu.SemaphoreType.DMA((blocks.shape[0] // bs,))],
+            input_output_aliases={2: 0},
+            compiler_params=pltpu.CompilerParams(vmem_limit_bytes=VMEM_LIMIT),
+            cost_estimate=BRIEF,
+            name="tail_kernel",
+        )(slots, blocks, out)
+    return out
 
 
 def solution(mesh):

time: 82.1 us -> 81.8 us (level)
  waiting for transfers between devices: 38.1 us -> 37.1 us
    ppermute x3, starting transfers between devices: 7.37 us -> 5.64 us  [local(): to_inner = lambda x: lax.ppermute(x, 'grid', across)]
    ppermute x5 -> x6, starting transfers between devices: 6.39 us -> 8.06 us  [local(): to_outer = lambda x: lax.ppermute(x, 'grid', over)]
    ppermute x5 -> x6, waiting for transfers between devices: 38.1 us -> 37.1 us  [local(): to_outer = lambda x: lax.ppermute(x, 'grid', over)]
  transfers between devices with their start and end apart: 8 -> 9, of which waited for: 5 -> 5; matrix products, arithmetic and copies ran while one was open for 0% -> 0% of each run, Pallas kernels for 34% -> 35%
where the time goes in v8:
time: 81.8 us; the launch traced here: 81.7 us
  waiting for transfers between devices  37.1 us (45%)
  Pallas kernels  30.7 us (38%)
  starting transfers between devices  13.7 us (17%)
    ppermute x6, waiting for transfers between devices, local(): to_outer = lambda x: lax.ppermute(x, 'grid', over)  37.1 us
    pallas_call x7, Pallas kernels, call(): pl.pallas_call(functools.partial(kernel, devices, rb, bs), out_shape=outs...  26 us
    ppermute x6, starting transfers between devices, local(): to_outer = lambda x: lax.ppermute(x, 'grid', over)  8.06 us
    ppermute x3, starting transfers between devices, local(): to_inner = lambda x: lax.ppermute(x, 'grid', across)  5.64 us
    pallas_call x1, Pallas kernels, pack(): pl.pallas_call(functools.partial(pack_kernel, devices, rb, bs), out_shape...  2.12 us
  transfers between devices with their start and end apart: 9, of which 5 were waited for; matrix products, arithmetic and copies ran while one was open for 0% of the time, Pallas kernels for 35%

profile of v8, /device:TPU:1, one launch (start us, length us, event | category | flops | bytes accessed | tf_op | source)
XLA Modules:
  0.0 81.7 jit_solution(12680382264900748758)
XLA Ops:
  0.0 1.1 %first.1._ = bf16[3,128,256]{2,1,0:T(8,128)(2,1)S(1)} custom-call(s32[8,48]{1,0:T(8,128)} %bitcast.1, bf16[3,8,256,256]{3,2,1,0:T(8,128)(2,1)} %blocks.3), custom_call_target="tpu_custom_call" | custom-call | flops 1 | bytes 1 | tf_op jit(solution)/shard_map/first/pallas_call | solution.py:97
  1.1 2.7 %collective-permute-start.1 = (bf16[3,128,256]{2,1,0:T(8,128)(2,1)S(1)}, bf16[3,128,256]{2,1,0:T(8,128)(2,1)S(1)}, u32[]{:S(2)}, u32[]{:S(2)}) collective-permute-start(bf16[3,128,256]{2,1,0:T(8,128)(2,1)S(1)} %first.1._), channel_id=1, source_target_pairs={{0,15},{1,2},{2,1},{3,4},{4,3},{5,6},{6,5},{7,8},{8,7},{9,10},{10,... | collective-permute-start | bytes 589832 | tf_op jit(solution)/shard_map/ppermute | solution.py:277
  3.8 2.1 %pack.1 = (bf16[3,640,256]{2,1,0:T(8,128)(2,1)S(1)}, bf16[3,768,256]{2,1,0:T(8,128)(2,1)S(1)}, bf16[3,768,256]{2,1,0:T(8,128)(2,1)S(1)}, bf16[3,768,256]{2,1,0:T(8,128)(2,1)S(1)}) custom-call(s32[8,48]{1,0:T(8,128)} %bitcast.2, bf16[3,8,256,256]{3,2,1,0:T(8,128)(2,1)} %blocks.3, bf16[3,128,256]{2,1,0:T(8,128)(2,1)S(1)} %first.1._), custom_call_target="tpu_custom_call" | custom-call | flops 1 | bytes 1 | tf_op jit(solution)/shard_map/pack/pallas_call | solution.py:112
  5.9 0.1 collective-permute-start.2
  6.0 1.7 %collective-permute-start = (bf16[3,768,256]{2,1,0:T(8,128)(2,1)S(1)}, bf16[3,768,256]{2,1,0:T(8,128)(2,1)S(1)}, u32[]{:S(2)}, u32[]{:S(2)}) collective-permute-start(bf16[3,768,256]{2,1,0:T(8,128)(2,1)S(1)} %get-tuple-element.23.own), channel_id=1, source_target_pairs={{0,15},{1,2},{2,1},{3,4},{4,3},{5,6},{6,5},{7,8},{8,7},{9,10},{10,... | collective-permute-start | bytes 3538952 | tf_op jit(solution)/shard_map/ppermute | solution.py:277
  7.7 5.6 %collective-permute-start.4 = (bf16[3,768,256]{2,1,0:T(8,128)(2,1)S(1)}, bf16[3,768,256]{2,1,0:T(8,128)(2,1)S(1)}, u32[]{:S(2)}, u32[]{:S(2)}) collective-permute-start(bf16[3,768,256]{2,1,0:T(8,128)(2,1)S(1)} %get-tuple-element.23.own), channel_id=1, source_target_pairs={{0,1},{1,0},{2,3},{3,2},{4,5},{5,4},{6,7},{7,6},{8,9},{9,8},{10,11... | collective-permute-start | bytes 3538952 | tf_op jit(solution)/shard_map/ppermute | solution.py:278
  13.3 0.0 collective-permute-start.3
  13.3 0.0 collective-permute-done.1.from_first
  13.3 0.7 begin_kernel.1.part
  14.0 0.0 copy-start
  14.1 29.0 %collective-permute-done.2.from_others = bf16[3,640,256]{2,1,0:T(8,128)(2,1)S(1)} collective-permute-done((bf16[3,640,256]{2,1,0:T(8,128)(2,1)S(1)}, bf16[3,640,256]{2,1,0:T(8,128)(2,1)S(1)}, u32[]{:S(2)}, u32[]{:S(2)}) %collective-permute-start.2) | collective-permute-done | bytes 983072 | tf_op jit(solution)/shard_map/ppermute | solution.py:277
  43.0 1.5 %outer_kernel.1 = (bf16[3,768,256]{2,1,0:T(8,128)(2,1)S(1)}, f32[3,768,256]{2,1,0:T(8,128)S(1)}) custom-call(bf16[3,768,256]{2,1,0:T(8,128)(2,1)S(1)} %get-tuple-element.24.outer, bf16[3,128,256]{2,1,0:T(8,128)(2,1)S(1)} %collective-permute-done.1.from_first, bf16[3,640,256]{2,1,0:T(8,128)(2,1)S(1)} %collective-permute-done.2.from_others, ...), custom_call_target="tpu_custom_call" | custom-call | flops 5000000000 | bytes 1 | tf_op jit(solution)/shard_map/outer_kernel/pallas_call | solution.py:294
  44.6 0.0 collective-permute-done.3.from_inner
  44.6 0.0 copy-done
  44.6 3.1 %square_kernel.1 = (bf16[3,768,256]{2,1,0:T(8,128)(2,1)S(1)}, bf16[2,768,256]{2,1,0:T(8,128)(2,1)S(1)}) custom-call(s32[8,48]{1,0:T(8,128)S(1)} %bitcast.3, bf16[3,768,256]{2,1,0:T(8,128)(2,1)S(1)} %get-tuple-element.23.own, bf16[3,768,256]{2,1,0:T(8,128)(2,1)S(1)} %get-tuple-element.27.inner, bf16[3,768,256]{2,1,0:T(8,128)(2,1)S(1)} %collective-permute-done.3.from_inner, ...), custom_call_target="tpu_custom_call" | custom-call | flops 1 | bytes 1 | tf_op jit(solution)/shard_map/square_kernel/pallas_call | solution.py:294
  47.7 0.1 collective-permute-start.8
  47.8 1.7 %collective-permute-start.7 = (bf16[2,768,256]{2,1,0:T(8,128)(2,1)S(1)}, bf16[2,768,256]{2,1,0:T(8,128)(2,1)S(1)}, u32[]{:S(2)}, u32[]{:S(2)}) collective-permute-start(bf16[2,768,256]{2,1,0:T(8,128)(2,1)S(1)} %get-tuple-element.34), channel_id=1, source_target_pairs={{0,15},{1,2},{2,1},{3,4},{4,3},{5,6},{6,5},{7,8},{8,7},{9,10},{10,... | collective-permute-start | bytes 2359304 | tf_op jit(solution)/shard_map/ppermute | solution.py:277
  49.5 0.0 collective-permute-done.4.inner_own
  49.5 10.3 %early_kernel.1 = (f32[3,768,256]{2,1,0:T(8,128)S(1)}, f32[3,768,256]{2,1,0:T(8,128)S(1)}, f32[3,768,256]{2,1,0:T(8,128)S(1)}, f32[3,768,256]{2,1,0:T(8,128)S(1)}) custom-call(s32[8,48]{1,0:T(8,128)S(1)} %bitcast.4, bf16[3,768,256]{2,1,0:T(8,128)(2,1)S(1)} %get-tuple-element.23.own, bf16[3,768,256]{2,1,0:T(8,128)(2,1)S(1)} %get-tuple-element.27.inner, ...), custom_call_target="tpu_custom_call" | custom-call | flops 1 | bytes 1 | tf_op jit(solution)/shard_map/early_kernel/pallas_call | solution.py:294
  59.9 4.2 %collective-permute-done.outer_own = bf16[3,768,256]{2,1,0:T(8,128)(2,1)S(1)} collective-permute-done((bf16[3,768,256]{2,1,0:T(8,128)(2,1)S(1)}, bf16[3,768,256]{2,1,0:T(8,128)(2,1)S(1)}, u32[]{:S(2)}, u32[]{:S(2)}) %collective-permute-start) | collective-permute-done | bytes 1179680 | tf_op jit(solution)/shard_map/ppermute | solution.py:277
  64.1 3.0 %ahead_kernel.1 = (bf16[3,768,256]{2,1,0:T(8,128)(2,1)S(1)}, bf16[512,256]{1,0:T(8,128)(2,1)S(1)}, bf16[256,256]{1,0:T(8,128)(2,1)S(1)}, s32[3,8,128]{2,1,0:T(8,128)S(1)}) custom-call(s32[8,48]{1,0:T(8,128)S(1)} %bitcast.5, bf16[3,768,256]{2,1,0:T(8,128)(2,1)S(1)} %collective-permute-done.outer_own, bf16[3,768,256]{2,1,0:T(8,128)(2,1)S(1)} %get-tuple-element.26.from_outer, ...), custom_call_target="tpu_custom_call" | custom-call | flops 1 | bytes 1 | tf_op jit(solution)/shard_map/ahead_kernel/pallas_call | solution.py:294
  67.1 1.7 %collective-permute-start.6 = (bf16[512,256]{1,0:T(8,128)(2,1)S(1)}, bf16[512,256]{1,0:T(8,128)(2,1)S(1)}, u32[]{:S(2)}, u32[]{:S(2)}) collective-permute-start(bf16[512,256]{1,0:T(8,128)(2,1)S(1)} %get-tuple-element.33), channel_id=1, source_target_pairs={{0,15},{1,2},{2,1},{3,4},{4,3},{5,6},{6,5},{7,8},{8,7},{9,10},{10,... | collective-permute-start | bytes 786440 | tf_op jit(solution)/shard_map/ppermute | solution.py:277
  68.8 0.1 collective-permute-start.5
  68.9 0.0 collective-permute-done.8.s_inner_own
  68.9 4.9 %late_kernel.1 = (bf16[3,8,256,256]{3,2,1,0:T(8,128)(2,1)}, f32[3,768,256]{2,1,0:T(8,128)S(1)}) custom-call(s32[8,48]{1,0:T(8,128)S(1)} %bitcast.6, bf16[3,768,256]{2,1,0:T(8,128)(2,1)S(1)} %get-tuple-element.23.own, bf16[3,768,256]{2,1,0:T(8,128)(2,1)S(1)} %get-tuple-element.24.outer, bf16[3,768,256]{2,1,0:T(8,128)(2,1)S(1)} %collective-permute-done.outer_own, ...), custom_call_target="tpu_custom_call" | custom-call | flops 1 | bytes 1 | tf_op jit(solution)/shard_map/late_kernel/pallas_call | solution.py:294
  73.9 2.9 %collective-permute-done.7.s_outer_head = bf16[2,768,256]{2,1,0:T(8,128)(2,1)S(1)} collective-permute-done((bf16[2,768,256]{2,1,0:T(8,128)(2,1)S(1)}, bf16[2,768,256]{2,1,0:T(8,128)(2,1)S(1)}, u32[]{:S(2)}, u32[]{:S(2)}) %collective-permute-start.7) | collective-permute-done | bytes 786464 | tf_op jit(solution)/shard_map/ppermute | solution.py:277
  76.7 2.4 %head_kernel.1._ = bf16[3,8,256,256]{3,2,1,0:T(8,128)(2,1)} custom-call(s32[8,48]{1,0:T(8,128)S(1)} %bitcast.7, bf16[3,768,256]{2,1,0:T(8,128)(2,1)S(1)} %get-tuple-element.24.outer, bf16[2,768,256]{2,1,0:T(8,128)(2,1)S(1)} %collective-permute-done.7.s_outer_head, f32[3,768,256]{2,1,0:T(8,128)S(1)} %get-tuple-element.39.rest, ...), custom_call_target="tpu_custom_call", output_to_operand_aliasing={{}: (4, {})} | custom-call | flops 1 | bytes 1 | tf_op jit(solution)/shard_map/head_kernel/pallas_call | solution.py:294
  79.1 0.4 collective-permute-done.6.blocks
  79.5 0.8 tail_kernel.2._
  80.3 0.6 collective-permute-done.5.blocks
  81.0 0.7 tail_kernel.3
Async XLA Ops:
  1.1 12.2 %collective-permute-start.1 = (bf16[3,128,256]{2,1,0:T(8,128)(2,1)S(1)}, bf16[3,128,256]{2,1,0:T(8,128)(2,1)S(1)}, u32[]{:S(2)}, u32[]{:S(2)}) collective-permute-start(bf16[3,128,256]{2,1,0:T(8,128)(2,1)S(1)} %first.1._), channel_id=1, source_target_pairs={{0,15},{1,2},{2,1},{3,4},{4,3},{5,6},{6,5},{7,8},{8,7},{9,10},{10,... | collective-permute-start | bytes 589832 | tf_op jit(solution)/shard_map/ppermute | solution.py:277
  5.9 37.1 %collective-permute-start.2 = (bf16[3,640,256]{2,1,0:T(8,128)(2,1)S(1)}, bf16[3,640,256]{2,1,0:T(8,128)(2,1)S(1)}, u32[]{:S(2)}, u32[]{:S(2)}) collective-permute-start(bf16[3,640,256]{2,1,0:T(8,128)(2,1)S(1)} %get-tuple-element.25), channel_id=1, source_target_pairs={{0,15},{1,2},{2,1},{3,4},{4,3},{5,6},{6,5},{7,8},{8,7},{9,10},{10,... | collective-permute-start | bytes 2949128 | tf_op jit(solution)/shard_map/ppermute | solution.py:277
  6.0 58.1 %collective-permute-start = (bf16[3,768,256]{2,1,0:T(8,128)(2,1)S(1)}, bf16[3,768,256]{2,1,0:T(8,128)(2,1)S(1)}, u32[]{:S(2)}, u32[]{:S(2)}) collective-permute-start(bf16[3,768,256]{2,1,0:T(8,128)(2,1)S(1)} %get-tuple-element.23.own), channel_id=1, source_target_pairs={{0,15},{1,2},{2,1},{3,4},{4,3},{5,6},{6,5},{7,8},{8,7},{9,10},{10,... | collective-permute-start | bytes 3538952 | tf_op jit(solution)/shard_map/ppermute | solution.py:277
  7.7 41.8 %collective-permute-start.4 = (bf16[3,768,256]{2,1,0:T(8,128)(2,1)S(1)}, bf16[3,768,256]{2,1,0:T(8,128)(2,1)S(1)}, u32[]{:S(2)}, u32[]{:S(2)}) collective-permute-start(bf16[3,768,256]{2,1,0:T(8,128)(2,1)S(1)} %get-tuple-element.23.own), channel_id=1, source_target_pairs={{0,1},{1,0},{2,3},{3,2},{4,5},{5,4},{6,7},{7,6},{8,9},{9,8},{10,11... | collective-permute-start | bytes 3538952 | tf_op jit(solution)/shard_map/ppermute | solution.py:278
  13.3 31.3 %collective-permute-start.3 = (bf16[3,768,256]{2,1,0:T(8,128)(2,1)S(1)}, bf16[3,768,256]{2,1,0:T(8,128)(2,1)S(1)}, u32[]{:S(2)}, u32[]{:S(2)}) collective-permute-start(bf16[3,768,256]{2,1,0:T(8,128)(2,1)S(1)} %get-tuple-element.27.inner), channel_id=1, source_target_pairs={{0,1},{1,0},{2,3},{3,2},{4,5},{5,4},{6,7},{7,6},{8,9},{9,8},{10,11... | collective-permute-start | bytes 3538952 | tf_op jit(solution)/shard_map/ppermute | solution.py:278
  14.0 30.5 %copy-start = (s32[48,8]{0,1:T(8,128)S(1)}, s32[48,8]{0,1:T(8,128)}, u32[]{:S(2)}) copy-start(s32[48,8]{0,1:T(8,128)} %param.3) | copy-start | bytes 4612
  47.7 21.2 %collective-permute-start.8 = (bf16[3,768,256]{2,1,0:T(8,128)(2,1)S(1)}, bf16[3,768,256]{2,1,0:T(8,128)(2,1)S(1)}, u32[]{:S(2)}, u32[]{:S(2)}) collective-permute-start(bf16[3,768,256]{2,1,0:T(8,128)(2,1)S(1)} %get-tuple-element.29.s_own), channel_id=1, source_target_pairs={{0,1},{1,0},{2,3},{3,2},{4,5},{5,4},{6,7},{7,6},{8,9},{9,8},{10,11... | collective-permute-start | bytes 3538952 | tf_op jit(solution)/shard_map/ppermute | solution.py:278
  47.8 28.9 %collective-permute-start.7 = (bf16[2,768,256]{2,1,0:T(8,128)(2,1)S(1)}, bf16[2,768,256]{2,1,0:T(8,128)(2,1)S(1)}, u32[]{:S(2)}, u32[]{:S(2)}) collective-permute-start(bf16[2,768,256]{2,1,0:T(8,128)(2,1)S(1)} %get-tuple-element.34), channel_id=1, source_target_pairs={{0,15},{1,2},{2,1},{3,4},{4,3},{5,6},{6,5},{7,8},{8,7},{9,10},{10,... | collective-permute-start | bytes 2359304 | tf_op jit(solution)/shard_map/ppermute | solution.py:277
  67.1 12.4 %collective-permute-start.6 = (bf16[512,256]{1,0:T(8,128)(2,1)S(1)}, bf16[512,256]{1,0:T(8,128)(2,1)S(1)}, u32[]{:S(2)}, u32[]{:S(2)}) collective-permute-start(bf16[512,256]{1,0:T(8,128)(2,1)S(1)} %get-tuple-element.33), channel_id=1, source_target_pairs={{0,15},{1,2},{2,1},{3,4},{4,3},{5,6},{6,5},{7,8},{8,7},{9,10},{10,... | collective-permute-start | bytes 786440 | tf_op jit(solution)/shard_map/ppermute | solution.py:277
  68.8 12.1 %collective-permute-start.5 = (bf16[256,256]{1,0:T(8,128)(2,1)S(1)}, bf16[256,256]{1,0:T(8,128)(2,1)S(1)}, u32[]{:S(2)}, u32[]{:S(2)}) collective-permute-start(bf16[256,256]{1,0:T(8,128)(2,1)S(1)} %get-tuple-element.32), channel_id=1, source_target_pairs={{0,15},{1,2},{2,1},{3,4},{4,3},{5,6},{6,5},{7,8},{8,7},{9,10},{10,... | collective-permute-start | bytes 393224 | tf_op jit(solution)/shard_map/ppermute | solution.py:277

commit v9 on v8

--- a/solution.py
+++ b/solution.py
@@ -16,7 +16,7 @@
 SMEM = pl.BlockSpec(memory_space=pltpu.SMEM)
 BRIEF = pl.CostEstimate(flops=1, bytes_accessed=1, transcendentals=0)
 LONGER = pl.CostEstimate(flops=5 * 10**9, bytes_accessed=1, transcendentals=0)
-LONGEST = pl.CostEstimate(flops=10**10, bytes_accessed=1, transcendentals=0)
+LONGEST = pl.CostEstimate(flops=8 * 10**9, bytes_accessed=1, transcendentals=0)
 VMEM_LIMIT = 24 * 1024 * 1024
 
 
@@ -61,13 +61,13 @@
 def first_kernel(devices, rb, bs, pattern_hbm, blocks, cut, pattern, held, pattern_sem, sem):
     fetch = pltpu.make_async_copy(pattern_hbm, pattern, pattern_sem)
     fetch.start()
-    load = pltpu.make_async_copy(blocks.at[0, :, pl.ds(0, bs // 2), :], held, sem)
+    load = pltpu.make_async_copy(blocks.at[0, :, pl.ds(0, bs * 5 // 8), :], held, sem)
     load.start()
     me, other, _ = neighbours(devices)
     fetch.wait()
     slots = [slot_of(pattern, me * rb, other * rb + j) for j in range(rb)]
     load.wait()
-    place(slots, held, cut, 0, bs // 2)
+    place(slots, held, cut, 0, bs * 5 // 8)
 
 
 def pack_kernel(devices, rb, bs, pattern_hbm, blocks, _, others, *rest):
@@ -85,7 +85,7 @@
         for cut, columns in zip(cuts, (other, me, partner)):
             slots = [slot_of(pattern, me * rb + r, columns * rb + j) for j in range(rb)]
             place(slots, held.at[r], cut, r * bs, bs)
-    others[...] = cuts[0][:, pl.ds(bs // 2, rb * bs - bs // 2), :]
+    others[...] = cuts[0][:, pl.ds(bs * 5 // 8, rb * bs - bs * 5 // 8), :]
 
 
 def pack(devices, pattern, blocks):
@@ -96,12 +96,12 @@
     params = pltpu.CompilerParams(vmem_limit_bytes=VMEM_LIMIT)
     first = pl.pallas_call(
         functools.partial(first_kernel, devices, rb, bs),
-        out_shape=cut(bs // 2),
+        out_shape=cut(bs * 5 // 8),
         in_specs=[ANY, ANY],
         out_specs=VMEM,
         scratch_shapes=[
             pltpu.SMEM(pattern.shape, pattern.dtype),
-            pltpu.VMEM((slots, bs // 2, bs), blocks.dtype),
+            pltpu.VMEM((slots, bs * 5 // 8, bs), blocks.dtype),
             pltpu.SemaphoreType.DMA,
             pltpu.SemaphoreType.DMA,
         ],
@@ -111,7 +111,7 @@
     )(pattern, blocks)
     return first, *pl.pallas_call(
         functools.partial(pack_kernel, devices, rb, bs),
-        out_shape=[cut(rb * bs - bs // 2)] + [cut(rb * bs)] * 3,
+        out_shape=[cut(rb * bs - bs * 5 // 8)] + [cut(rb * bs)] * 3,
         in_specs=[ANY, ANY, ANY],
         out_specs=[VMEM] * 4,
         scratch_shapes=[
@@ -143,26 +143,18 @@
         pl.when(slot >= 0)(copy.wait)
 
 
-def begin_kernel(devices, rb, bs, outer, from_first, part):
-    @pl.loop(0, rb)
-    def _(c):
-        part[c] = jnp.dot(outer[0, :, pl.ds(0, bs // 2)], from_first[c], preferred_element_type=F32)
-
-
-def outer_kernel(devices, rb, bs, outer, from_first, from_others, part, from_outer, own_part):
-    half = bs // 2
-    from_outer[:, pl.ds(0, half), :] = from_first[...]
-    from_outer[:, pl.ds(half, rb * bs - half), :] = from_others[...]
-
-    @pl.loop(0, rb)
-    def _(c):
-        total = part[c] + jnp.dot(
-            outer[0, :, pl.ds(half, half)], from_others[c, pl.ds(0, half), :], preferred_element_type=F32
-        )
-        for k in range(1, rb):
-            rows = pl.ds(k * bs - half, bs)
-            total += jnp.dot(outer[k], from_others[c, rows, :], preferred_element_type=F32)
-        own_part[c] = total
+def begin_kernel(devices, rb, bs, from_first, held):
+    held[...] = from_first[...]
+
+
+def outer_kernel(devices, rb, bs, outer, held, from_others, from_outer, own_part):
+    size = held.shape[1]
+    from_outer[:, pl.ds(0, size), :] = held[...]
+    from_outer[:, pl.ds(size, rb * bs - size), :] = from_others[...]
+
+    @pl.loop(0, rb)
+    def _(c):
+        own_part[c] = panel_product(outer, from_outer, c, rb, bs)
 
 
 def square_kernel(devices, rb, bs, pattern, own, inner, from_inner, own_part, s_own, s_head):
@@ -308,8 +300,10 @@
     outer_own = to_outer(own)
     from_inner, inner_own = to_inner(inner), to_inner(own)
 
-    (part,) = call(begin_kernel, (outer, from_first), (high,), patterned=False, cost=LONGEST)
-    from_outer, own_part = call(outer_kernel, (outer, from_first, from_others, part), (low, high), patterned=False, cost=LONGER)
+    (held,) = call(
+        begin_kernel, (from_first,), (jax.ShapeDtypeStruct(first.shape, BF16),), patterned=False, cost=LONGEST
+    )
+    from_outer, own_part = call(outer_kernel, (outer, held, from_others), (low, high), patterned=False, cost=LONGER)
     s_own, s_head = call(square_kernel, (own, inner, from_inner, own_part), (low, low_of(rb - 1)))
     s_outer_head = to_outer(s_head)
     s_inner_own = to_inner(s_own)

time: 81.8 us -> 81.8 us (level)
  transfers between devices with their start and end apart: 9 -> 9, of which waited for: 5 -> 6; matrix products, arithmetic and copies ran while one was open for 0% -> 0% of each run, Pallas kernels for 35% -> 34%
where the time goes in v9:
time: 81.8 us; the launch traced here: 81.6 us
  waiting for transfers between devices  37.7 us (46%)
  Pallas kernels  29.9 us (37%)
  starting transfers between devices  13.8 us (17%)
    ppermute x6, waiting for transfers between devices, local(): to_outer = lambda x: lax.ppermute(x, 'grid', over)  37.7 us
    pallas_call x7, Pallas kernels, call(): pl.pallas_call(functools.partial(kernel, devices, rb, bs), out_shape=outs...  25.3 us
    ppermute x6, starting transfers between devices, local(): to_outer = lambda x: lax.ppermute(x, 'grid', over)  8.2 us
    ppermute x3, starting transfers between devices, local(): to_inner = lambda x: lax.ppermute(x, 'grid', across)  5.65 us
    pallas_call x1, Pallas kernels, pack(): pl.pallas_call(functools.partial(pack_kernel, devices, rb, bs), out_shape...  2.11 us
  transfers between devices with their start and end apart: 9, of which 6 were waited for; matrix products, arithmetic and copies ran while one was open for 0% of the time, Pallas kernels for 34%

profile of v9, /device:TPU:1, one launch (start us, length us, event | category | flops | bytes accessed | tf_op | source)
XLA Modules:
  0.0 81.6 jit_solution(2923695125952070779)
XLA Ops:
  0.0 1.1 %first.1._ = bf16[3,160,256]{2,1,0:T(8,128)(2,1)S(1)} custom-call(s32[8,48]{1,0:T(8,128)} %bitcast.1, bf16[3,8,256,256]{3,2,1,0:T(8,128)(2,1)} %blocks.3), custom_call_target="tpu_custom_call" | custom-call | flops 1 | bytes 1 | tf_op jit(solution)/shard_map/first/pallas_call | solution.py:97
  1.1 2.7 %collective-permute-start.1 = (bf16[3,160,256]{2,1,0:T(8,128)(2,1)S(1)}, bf16[3,160,256]{2,1,0:T(8,128)(2,1)S(1)}, u32[]{:S(2)}, u32[]{:S(2)}) collective-permute-start(bf16[3,160,256]{2,1,0:T(8,128)(2,1)S(1)} %first.1._), channel_id=1, source_target_pairs={{0,15},{1,2},{2,1},{3,4},{4,3},{5,6},{6,5},{7,8},{8,7},{9,10},{10,... | collective-permute-start | bytes 737288 | tf_op jit(solution)/shard_map/ppermute | solution.py:269
  3.8 2.1 %pack.1 = (bf16[3,608,256]{2,1,0:T(8,128)(2,1)S(1)}, bf16[3,768,256]{2,1,0:T(8,128)(2,1)S(1)}, bf16[3,768,256]{2,1,0:T(8,128)(2,1)S(1)}, bf16[3,768,256]{2,1,0:T(8,128)(2,1)S(1)}) custom-call(s32[8,48]{1,0:T(8,128)} %bitcast.2, bf16[3,8,256,256]{3,2,1,0:T(8,128)(2,1)} %blocks.3, bf16[3,160,256]{2,1,0:T(8,128)(2,1)S(1)} %first.1._), custom_call_target="tpu_custom_call" | custom-call | flops 1 | bytes 1 | tf_op jit(solution)/shard_map/pack/pallas_call | solution.py:112
  6.0 0.1 collective-permute-start.2
  6.0 1.7 %collective-permute-start = (bf16[3,768,256]{2,1,0:T(8,128)(2,1)S(1)}, bf16[3,768,256]{2,1,0:T(8,128)(2,1)S(1)}, u32[]{:S(2)}, u32[]{:S(2)}) collective-permute-start(bf16[3,768,256]{2,1,0:T(8,128)(2,1)S(1)} %get-tuple-element.23.own), channel_id=1, source_target_pairs={{0,15},{1,2},{2,1},{3,4},{4,3},{5,6},{6,5},{7,8},{8,7},{9,10},{10,... | collective-permute-start | bytes 3538952 | tf_op jit(solution)/shard_map/ppermute | solution.py:269
  7.8 5.6 %collective-permute-start.4 = (bf16[3,768,256]{2,1,0:T(8,128)(2,1)S(1)}, bf16[3,768,256]{2,1,0:T(8,128)(2,1)S(1)}, u32[]{:S(2)}, u32[]{:S(2)}) collective-permute-start(bf16[3,768,256]{2,1,0:T(8,128)(2,1)S(1)} %get-tuple-element.23.own), channel_id=1, source_target_pairs={{0,1},{1,0},{2,3},{3,2},{4,5},{5,4},{6,7},{7,6},{8,9},{9,8},{10,11... | collective-permute-start | bytes 3538952 | tf_op jit(solution)/shard_map/ppermute | solution.py:270
  13.3 0.0 collective-permute-start.3
  13.3 18.9 %collective-permute-done.1.from_first = bf16[3,160,256]{2,1,0:T(8,128)(2,1)S(1)} collective-permute-done((bf16[3,160,256]{2,1,0:T(8,128)(2,1)S(1)}, bf16[3,160,256]{2,1,0:T(8,128)(2,1)S(1)}, u32[]{:S(2)}, u32[]{:S(2)}) %collective-permute-start.1) | collective-permute-done | bytes 245792 | tf_op jit(solution)/shard_map/ppermute | solution.py:269
  32.3 10.7 %collective-permute-done.2.from_others = bf16[3,608,256]{2,1,0:T(8,128)(2,1)S(1)} collective-permute-done((bf16[3,608,256]{2,1,0:T(8,128)(2,1)S(1)}, bf16[3,608,256]{2,1,0:T(8,128)(2,1)S(1)}, u32[]{:S(2)}, u32[]{:S(2)}) %collective-permute-start.2) | collective-permute-done | bytes 933920 | tf_op jit(solution)/shard_map/ppermute | solution.py:269
  43.0 0.0 copy-start
  43.0 1.5 %outer_kernel.1 = (bf16[3,768,256]{2,1,0:T(8,128)(2,1)S(1)}, f32[3,768,256]{2,1,0:T(8,128)S(1)}) custom-call(bf16[3,768,256]{2,1,0:T(8,128)(2,1)S(1)} %get-tuple-element.24.outer, bf16[3,160,256]{2,1,0:T(8,128)(2,1)S(1)} %begin_kernel.1.held, bf16[3,608,256]{2,1,0:T(8,128)(2,1)S(1)} %collective-permute-done.2.from_others), custom_call_target="tpu_custom_call" | custom-call | flops 5000000000 | bytes 1 | tf_op jit(solution)/shard_map/outer_kernel/pallas_call | solution.py:286
  44.5 0.0 collective-permute-done.3.from_inner
  44.5 0.0 copy-done
  44.5 3.1 %square_kernel.1 = (bf16[3,768,256]{2,1,0:T(8,128)(2,1)S(1)}, bf16[2,768,256]{2,1,0:T(8,128)(2,1)S(1)}) custom-call(s32[8,48]{1,0:T(8,128)S(1)} %bitcast.3, bf16[3,768,256]{2,1,0:T(8,128)(2,1)S(1)} %get-tuple-element.23.own, bf16[3,768,256]{2,1,0:T(8,128)(2,1)S(1)} %get-tuple-element.27.inner, bf16[3,768,256]{2,1,0:T(8,128)(2,1)S(1)} %collective-permute-done.3.from_inner, ...), custom_call_target="tpu_custom_call" | custom-call | flops 1 | bytes 1 | tf_op jit(solution)/shard_map/square_kernel/pallas_call | solution.py:286
  47.7 0.1 collective-permute-start.8
  47.8 1.8 %collective-permute-start.7 = (bf16[2,768,256]{2,1,0:T(8,128)(2,1)S(1)}, bf16[2,768,256]{2,1,0:T(8,128)(2,1)S(1)}, u32[]{:S(2)}, u32[]{:S(2)}) collective-permute-start(bf16[2,768,256]{2,1,0:T(8,128)(2,1)S(1)} %get-tuple-element.34), channel_id=1, source_target_pairs={{0,15},{1,2},{2,1},{3,4},{4,3},{5,6},{6,5},{7,8},{8,7},{9,10},{10,... | collective-permute-start | bytes 2359304 | tf_op jit(solution)/shard_map/ppermute | solution.py:269
  49.6 0.0 collective-permute-done.4.inner_own
  49.6 10.3 %early_kernel.1 = (f32[3,768,256]{2,1,0:T(8,128)S(1)}, f32[3,768,256]{2,1,0:T(8,128)S(1)}, f32[3,768,256]{2,1,0:T(8,128)S(1)}, f32[3,768,256]{2,1,0:T(8,128)S(1)}) custom-call(s32[8,48]{1,0:T(8,128)S(1)} %bitcast.4, bf16[3,768,256]{2,1,0:T(8,128)(2,1)S(1)} %get-tuple-element.23.own, bf16[3,768,256]{2,1,0:T(8,128)(2,1)S(1)} %get-tuple-element.27.inner, ...), custom_call_target="tpu_custom_call" | custom-call | flops 1 | bytes 1 | tf_op jit(solution)/shard_map/early_kernel/pallas_call | solution.py:286
  59.9 4.2 %collective-permute-done.outer_own = bf16[3,768,256]{2,1,0:T(8,128)(2,1)S(1)} collective-permute-done((bf16[3,768,256]{2,1,0:T(8,128)(2,1)S(1)}, bf16[3,768,256]{2,1,0:T(8,128)(2,1)S(1)}, u32[]{:S(2)}, u32[]{:S(2)}) %collective-permute-start) | collective-permute-done | bytes 1179680 | tf_op jit(solution)/shard_map/ppermute | solution.py:269
  64.1 3.0 %ahead_kernel.1 = (bf16[3,768,256]{2,1,0:T(8,128)(2,1)S(1)}, bf16[512,256]{1,0:T(8,128)(2,1)S(1)}, bf16[256,256]{1,0:T(8,128)(2,1)S(1)}, s32[3,8,128]{2,1,0:T(8,128)S(1)}) custom-call(s32[8,48]{1,0:T(8,128)S(1)} %bitcast.5, bf16[3,768,256]{2,1,0:T(8,128)(2,1)S(1)} %collective-permute-done.outer_own, bf16[3,768,256]{2,1,0:T(8,128)(2,1)S(1)} %get-tuple-element.26.from_outer, ...), custom_call_target="tpu_custom_call" | custom-call | flops 1 | bytes 1 | tf_op jit(solution)/shard_map/ahead_kernel/pallas_call | solution.py:286
  67.1 1.8 %collective-permute-start.6 = (bf16[512,256]{1,0:T(8,128)(2,1)S(1)}, bf16[512,256]{1,0:T(8,128)(2,1)S(1)}, u32[]{:S(2)}, u32[]{:S(2)}) collective-permute-start(bf16[512,256]{1,0:T(8,128)(2,1)S(1)} %get-tuple-element.33), channel_id=1, source_target_pairs={{0,15},{1,2},{2,1},{3,4},{4,3},{5,6},{6,5},{7,8},{8,7},{9,10},{10,... | collective-permute-start | bytes 786440 | tf_op jit(solution)/shard_map/ppermute | solution.py:269
  68.9 0.1 collective-permute-start.5
  69.0 0.0 collective-permute-done.8.s_inner_own
  69.0 4.9 %late_kernel.1 = (bf16[3,8,256,256]{3,2,1,0:T(8,128)(2,1)}, f32[3,768,256]{2,1,0:T(8,128)S(1)}) custom-call(s32[8,48]{1,0:T(8,128)S(1)} %bitcast.6, bf16[3,768,256]{2,1,0:T(8,128)(2,1)S(1)} %get-tuple-element.23.own, bf16[3,768,256]{2,1,0:T(8,128)(2,1)S(1)} %get-tuple-element.24.outer, bf16[3,768,256]{2,1,0:T(8,128)(2,1)S(1)} %collective-permute-done.outer_own, ...), custom_call_target="tpu_custom_call" | custom-call | flops 1 | bytes 1 | tf_op jit(solution)/shard_map/late_kernel/pallas_call | solution.py:286
  73.9 2.8 %collective-permute-done.7.s_outer_head = bf16[2,768,256]{2,1,0:T(8,128)(2,1)S(1)} collective-permute-done((bf16[2,768,256]{2,1,0:T(8,128)(2,1)S(1)}, bf16[2,768,256]{2,1,0:T(8,128)(2,1)S(1)}, u32[]{:S(2)}, u32[]{:S(2)}) %collective-permute-start.7) | collective-permute-done | bytes 786464 | tf_op jit(solution)/shard_map/ppermute | solution.py:269
  76.7 2.4 %head_kernel.1._ = bf16[3,8,256,256]{3,2,1,0:T(8,128)(2,1)} custom-call(s32[8,48]{1,0:T(8,128)S(1)} %bitcast.7, bf16[3,768,256]{2,1,0:T(8,128)(2,1)S(1)} %get-tuple-element.24.outer, bf16[2,768,256]{2,1,0:T(8,128)(2,1)S(1)} %collective-permute-done.7.s_outer_head, f32[3,768,256]{2,1,0:T(8,128)S(1)} %get-tuple-element.39.rest, ...), custom_call_target="tpu_custom_call", output_to_operand_aliasing={{}: (4, {})} | custom-call | flops 1 | bytes 1 | tf_op jit(solution)/shard_map/head_kernel/pallas_call | solution.py:286
  79.1 0.4 collective-permute-done.6.blocks
  79.5 0.7 tail_kernel.2._
  80.2 0.7 collective-permute-done.5.blocks
  80.9 0.7 tail_kernel.3
  (1 shorter events, 0.0 us)
Async XLA Ops:
  1.1 31.1 %collective-permute-start.1 = (bf16[3,160,256]{2,1,0:T(8,128)(2,1)S(1)}, bf16[3,160,256]{2,1,0:T(8,128)(2,1)S(1)}, u32[]{:S(2)}, u32[]{:S(2)}) collective-permute-start(bf16[3,160,256]{2,1,0:T(8,128)(2,1)S(1)} %first.1._), channel_id=1, source_target_pairs={{0,15},{1,2},{2,1},{3,4},{4,3},{5,6},{6,5},{7,8},{8,7},{9,10},{10,... | collective-permute-start | bytes 737288 | tf_op jit(solution)/shard_map/ppermute | solution.py:269
  6.0 37.1 %collective-permute-start.2 = (bf16[3,608,256]{2,1,0:T(8,128)(2,1)S(1)}, bf16[3,608,256]{2,1,0:T(8,128)(2,1)S(1)}, u32[]{:S(2)}, u32[]{:S(2)}) collective-permute-start(bf16[3,608,256]{2,1,0:T(8,128)(2,1)S(1)} %get-tuple-element.25), channel_id=1, source_target_pairs={{0,15},{1,2},{2,1},{3,4},{4,3},{5,6},{6,5},{7,8},{8,7},{9,10},{10,... | collective-permute-start | bytes 2801672 | tf_op jit(solution)/shard_map/ppermute | solution.py:269
  6.0 58.0 %collective-permute-start = (bf16[3,768,256]{2,1,0:T(8,128)(2,1)S(1)}, bf16[3,768,256]{2,1,0:T(8,128)(2,1)S(1)}, u32[]{:S(2)}, u32[]{:S(2)}) collective-permute-start(bf16[3,768,256]{2,1,0:T(8,128)(2,1)S(1)} %get-tuple-element.23.own), channel_id=1, source_target_pairs={{0,15},{1,2},{2,1},{3,4},{4,3},{5,6},{6,5},{7,8},{8,7},{9,10},{10,... | collective-permute-start | bytes 3538952 | tf_op jit(solution)/shard_map/ppermute | solution.py:269
  7.8 41.8 %collective-permute-start.4 = (bf16[3,768,256]{2,1,0:T(8,128)(2,1)S(1)}, bf16[3,768,256]{2,1,0:T(8,128)(2,1)S(1)}, u32[]{:S(2)}, u32[]{:S(2)}) collective-permute-start(bf16[3,768,256]{2,1,0:T(8,128)(2,1)S(1)} %get-tuple-element.23.own), channel_id=1, source_target_pairs={{0,1},{1,0},{2,3},{3,2},{4,5},{5,4},{6,7},{7,6},{8,9},{9,8},{10,11... | collective-permute-start | bytes 3538952 | tf_op jit(solution)/shard_map/ppermute | solution.py:270
  13.3 31.2 %collective-permute-start.3 = (bf16[3,768,256]{2,1,0:T(8,128)(2,1)S(1)}, bf16[3,768,256]{2,1,0:T(8,128)(2,1)S(1)}, u32[]{:S(2)}, u32[]{:S(2)}) collective-permute-start(bf16[3,768,256]{2,1,0:T(8,128)(2,1)S(1)} %get-tuple-element.27.inner), channel_id=1, source_target_pairs={{0,1},{1,0},{2,3},{3,2},{4,5},{5,4},{6,7},{7,6},{8,9},{9,8},{10,11... | collective-permute-start | bytes 3538952 | tf_op jit(solution)/shard_map/ppermute | solution.py:270
  43.0 1.5 %copy-start = (s32[48,8]{0,1:T(8,128)S(1)}, s32[48,8]{0,1:T(8,128)}, u32[]{:S(2)}) copy-start(s32[48,8]{0,1:T(8,128)} %param.3) | copy-start | bytes 4612
  47.7 21.3 %collective-permute-start.8 = (bf16[3,768,256]{2,1,0:T(8,128)(2,1)S(1)}, bf16[3,768,256]{2,1,0:T(8,128)(2,1)S(1)}, u32[]{:S(2)}, u32[]{:S(2)}) collective-permute-start(bf16[3,768,256]{2,1,0:T(8,128)(2,1)S(1)} %get-tuple-element.29.s_own), channel_id=1, source_target_pairs={{0,1},{1,0},{2,3},{3,2},{4,5},{5,4},{6,7},{7,6},{8,9},{9,8},{10,11... | collective-permute-start | bytes 3538952 | tf_op jit(solution)/shard_map/ppermute | solution.py:270
  47.8 28.9 %collective-permute-start.7 = (bf16[2,768,256]{2,1,0:T(8,128)(2,1)S(1)}, bf16[2,768,256]{2,1,0:T(8,128)(2,1)S(1)}, u32[]{:S(2)}, u32[]{:S(2)}) collective-permute-start(bf16[2,768,256]{2,1,0:T(8,128)(2,1)S(1)} %get-tuple-element.34), channel_id=1, source_target_pairs={{0,15},{1,2},{2,1},{3,4},{4,3},{5,6},{6,5},{7,8},{8,7},{9,10},{10,... | collective-permute-start | bytes 2359304 | tf_op jit(solution)/shard_map/ppermute | solution.py:269
  67.1 12.4 %collective-permute-start.6 = (bf16[512,256]{1,0:T(8,128)(2,1)S(1)}, bf16[512,256]{1,0:T(8,128)(2,1)S(1)}, u32[]{:S(2)}, u32[]{:S(2)}) collective-permute-start(bf16[512,256]{1,0:T(8,128)(2,1)S(1)} %get-tuple-element.33), channel_id=1, source_target_pairs={{0,15},{1,2},{2,1},{3,4},{4,3},{5,6},{6,5},{7,8},{8,7},{9,10},{10,... | collective-permute-start | bytes 786440 | tf_op jit(solution)/shard_map/ppermute | solution.py:269
  68.9 12.0 %collective-permute-start.5 = (bf16[256,256]{1,0:T(8,128)(2,1)S(1)}, bf16[256,256]{1,0:T(8,128)(2,1)S(1)}, u32[]{:S(2)}, u32[]{:S(2)}) collective-permute-start(bf16[256,256]{1,0:T(8,128)(2,1)S(1)} %get-tuple-element.32), channel_id=1, source_target_pairs={{0,15},{1,2},{2,1},{3,4},{4,3},{5,6},{6,5},{7,8},{8,7},{9,10},{10,... | collective-permute-start | bytes 393224 | tf_op jit(solution)/shard_map/ppermute | solution.py:269

commit v10 on v8

--- a/solution.py
+++ b/solution.py
@@ -65,7 +65,10 @@
     load.start()
     me, other, _ = neighbours(devices)
     fetch.wait()
-    slots = [slot_of(pattern, me * rb, other * rb + j) for j in range(rb)]
+    table = pattern[...]
+    slot_ids = lax.broadcasted_iota(jnp.int32, table.shape, 0)
+    at_row = lax.broadcasted_iota(jnp.int32, table.shape, 1) == me * rb
+    slots = [jnp.max(jnp.where(at_row & (table == other * rb + j), slot_ids, -1)) for j in range(rb)]
     load.wait()
     place(slots, held, cut, 0, bs // 2)
 
@@ -100,7 +103,7 @@
         in_specs=[ANY, ANY],
         out_specs=VMEM,
         scratch_shapes=[
-            pltpu.SMEM(pattern.shape, pattern.dtype),
+            pltpu.VMEM(pattern.shape, pattern.dtype),
             pltpu.VMEM((slots, bs // 2, bs), blocks.dtype),
             pltpu.SemaphoreType.DMA,
             pltpu.SemaphoreType.DMA,

time: 81.8 us -> 81.8 us (level)
  no operation moved by 1% of the time
where the time goes in v10:
time: 81.8 us; the launch traced here: 81.7 us
  waiting for transfers between devices  37.2 us (45%)
  Pallas kernels  30.6 us (37%)
  starting transfers between devices  13.7 us (17%)
    ppermute x6, waiting for transfers between devices, local(): to_outer = lambda x: lax.ppermute(x, 'grid', over)  37.2 us
    pallas_call x7, Pallas kernels, call(): pl.pallas_call(functools.partial(kernel, devices, rb, bs), out_shape=outs...  26 us
    ppermute x6, starting transfers between devices, local(): to_outer = lambda x: lax.ppermute(x, 'grid', over)  8.06 us
    ppermute x3, starting transfers between devices, local(): to_inner = lambda x: lax.ppermute(x, 'grid', across)  5.64 us
    pallas_call x1, Pallas kernels, pack(): pl.pallas_call(functools.partial(pack_kernel, devices, rb, bs), out_shape...  2.12 us
  transfers between devices with their start and end apart: 9, of which 5 were waited for; matrix products, arithmetic and copies ran while one was open for 0% of the time, Pallas kernels for 35%

profile of v10, /device:TPU:1, one launch (start us, length us, event | category | flops | bytes accessed | tf_op | source)
XLA Modules:
  0.0 81.7 jit_solution(16063840081796479342)
XLA Ops:
  0.0 1.1 %first.1._ = bf16[3,128,256]{2,1,0:T(8,128)(2,1)S(1)} custom-call(s32[8,48]{1,0:T(8,128)} %bitcast.1, bf16[3,8,256,256]{3,2,1,0:T(8,128)(2,1)} %blocks.3), custom_call_target="tpu_custom_call" | custom-call | flops 1 | bytes 1 | tf_op jit(solution)/shard_map/first/pallas_call | solution.py:100
  1.1 2.7 %collective-permute-start.1 = (bf16[3,128,256]{2,1,0:T(8,128)(2,1)S(1)}, bf16[3,128,256]{2,1,0:T(8,128)(2,1)S(1)}, u32[]{:S(2)}, u32[]{:S(2)}) collective-permute-start(bf16[3,128,256]{2,1,0:T(8,128)(2,1)S(1)} %first.1._), channel_id=1, source_target_pairs={{0,15},{1,2},{2,1},{3,4},{4,3},{5,6},{6,5},{7,8},{8,7},{9,10},{10,... | collective-permute-start | bytes 589832 | tf_op jit(solution)/shard_map/ppermute | solution.py:280
  3.8 2.1 %pack.1 = (bf16[3,640,256]{2,1,0:T(8,128)(2,1)S(1)}, bf16[3,768,256]{2,1,0:T(8,128)(2,1)S(1)}, bf16[3,768,256]{2,1,0:T(8,128)(2,1)S(1)}, bf16[3,768,256]{2,1,0:T(8,128)(2,1)S(1)}) custom-call(s32[8,48]{1,0:T(8,128)} %bitcast.2, bf16[3,8,256,256]{3,2,1,0:T(8,128)(2,1)} %blocks.3, bf16[3,128,256]{2,1,0:T(8,128)(2,1)S(1)} %first.1._), custom_call_target="tpu_custom_call" | custom-call | flops 1 | bytes 1 | tf_op jit(solution)/shard_map/pack/pallas_call | solution.py:115
  5.9 0.1 collective-permute-start.2
  6.0 1.7 %collective-permute-start = (bf16[3,768,256]{2,1,0:T(8,128)(2,1)S(1)}, bf16[3,768,256]{2,1,0:T(8,128)(2,1)S(1)}, u32[]{:S(2)}, u32[]{:S(2)}) collective-permute-start(bf16[3,768,256]{2,1,0:T(8,128)(2,1)S(1)} %get-tuple-element.23.own), channel_id=1, source_target_pairs={{0,15},{1,2},{2,1},{3,4},{4,3},{5,6},{6,5},{7,8},{8,7},{9,10},{10,... | collective-permute-start | bytes 3538952 | tf_op jit(solution)/shard_map/ppermute | solution.py:280
  7.7 5.6 %collective-permute-start.4 = (bf16[3,768,256]{2,1,0:T(8,128)(2,1)S(1)}, bf16[3,768,256]{2,1,0:T(8,128)(2,1)S(1)}, u32[]{:S(2)}, u32[]{:S(2)}) collective-permute-start(bf16[3,768,256]{2,1,0:T(8,128)(2,1)S(1)} %get-tuple-element.23.own), channel_id=1, source_target_pairs={{0,1},{1,0},{2,3},{3,2},{4,5},{5,4},{6,7},{7,6},{8,9},{9,8},{10,11... | collective-permute-start | bytes 3538952 | tf_op jit(solution)/shard_map/ppermute | solution.py:281
  13.3 0.0 collective-permute-start.3
  13.3 0.0 collective-permute-done.1.from_first
  13.3 0.7 begin_kernel.1.part
  14.1 0.0 copy-start
  14.1 29.0 %collective-permute-done.2.from_others = bf16[3,640,256]{2,1,0:T(8,128)(2,1)S(1)} collective-permute-done((bf16[3,640,256]{2,1,0:T(8,128)(2,1)S(1)}, bf16[3,640,256]{2,1,0:T(8,128)(2,1)S(1)}, u32[]{:S(2)}, u32[]{:S(2)}) %collective-permute-start.2) | collective-permute-done | bytes 983072 | tf_op jit(solution)/shard_map/ppermute | solution.py:280
  43.0 1.5 %outer_kernel.1 = (bf16[3,768,256]{2,1,0:T(8,128)(2,1)S(1)}, f32[3,768,256]{2,1,0:T(8,128)S(1)}) custom-call(bf16[3,768,256]{2,1,0:T(8,128)(2,1)S(1)} %get-tuple-element.24.outer, bf16[3,128,256]{2,1,0:T(8,128)(2,1)S(1)} %collective-permute-done.1.from_first, bf16[3,640,256]{2,1,0:T(8,128)(2,1)S(1)} %collective-permute-done.2.from_others, ...), custom_call_target="tpu_custom_call" | custom-call | flops 5000000000 | bytes 1 | tf_op jit(solution)/shard_map/outer_kernel/pallas_call | solution.py:297
  44.6 0.0 collective-permute-done.3.from_inner
  44.6 0.0 copy-done
  44.6 3.1 %square_kernel.1 = (bf16[3,768,256]{2,1,0:T(8,128)(2,1)S(1)}, bf16[2,768,256]{2,1,0:T(8,128)(2,1)S(1)}) custom-call(s32[8,48]{1,0:T(8,128)S(1)} %bitcast.3, bf16[3,768,256]{2,1,0:T(8,128)(2,1)S(1)} %get-tuple-element.23.own, bf16[3,768,256]{2,1,0:T(8,128)(2,1)S(1)} %get-tuple-element.27.inner, bf16[3,768,256]{2,1,0:T(8,128)(2,1)S(1)} %collective-permute-done.3.from_inner, ...), custom_call_target="tpu_custom_call" | custom-call | flops 1 | bytes 1 | tf_op jit(solution)/shard_map/square_kernel/pallas_call | solution.py:297
  47.7 0.1 collective-permute-start.8
  47.8 1.7 %collective-permute-start.7 = (bf16[2,768,256]{2,1,0:T(8,128)(2,1)S(1)}, bf16[2,768,256]{2,1,0:T(8,128)(2,1)S(1)}, u32[]{:S(2)}, u32[]{:S(2)}) collective-permute-start(bf16[2,768,256]{2,1,0:T(8,128)(2,1)S(1)} %get-tuple-element.34), channel_id=1, source_target_pairs={{0,15},{1,2},{2,1},{3,4},{4,3},{5,6},{6,5},{7,8},{8,7},{9,10},{10,... | collective-permute-start | bytes 2359304 | tf_op jit(solution)/shard_map/ppermute | solution.py:280
  49.5 0.0 collective-permute-done.4.inner_own
  49.5 10.3 %early_kernel.1 = (f32[3,768,256]{2,1,0:T(8,128)S(1)}, f32[3,768,256]{2,1,0:T(8,128)S(1)}, f32[3,768,256]{2,1,0:T(8,128)S(1)}, f32[3,768,256]{2,1,0:T(8,128)S(1)}) custom-call(s32[8,48]{1,0:T(8,128)S(1)} %bitcast.4, bf16[3,768,256]{2,1,0:T(8,128)(2,1)S(1)} %get-tuple-element.23.own, bf16[3,768,256]{2,1,0:T(8,128)(2,1)S(1)} %get-tuple-element.27.inner, ...), custom_call_target="tpu_custom_call" | custom-call | flops 1 | bytes 1 | tf_op jit(solution)/shard_map/early_kernel/pallas_call | solution.py:297
  59.9 4.2 %collective-permute-done.outer_own = bf16[3,768,256]{2,1,0:T(8,128)(2,1)S(1)} collective-permute-done((bf16[3,768,256]{2,1,0:T(8,128)(2,1)S(1)}, bf16[3,768,256]{2,1,0:T(8,128)(2,1)S(1)}, u32[]{:S(2)}, u32[]{:S(2)}) %collective-permute-start) | collective-permute-done | bytes 1179680 | tf_op jit(solution)/shard_map/ppermute | solution.py:280
  64.1 3.0 %ahead_kernel.1 = (bf16[3,768,256]{2,1,0:T(8,128)(2,1)S(1)}, bf16[512,256]{1,0:T(8,128)(2,1)S(1)}, bf16[256,256]{1,0:T(8,128)(2,1)S(1)}, s32[3,8,128]{2,1,0:T(8,128)S(1)}) custom-call(s32[8,48]{1,0:T(8,128)S(1)} %bitcast.5, bf16[3,768,256]{2,1,0:T(8,128)(2,1)S(1)} %collective-permute-done.outer_own, bf16[3,768,256]{2,1,0:T(8,128)(2,1)S(1)} %get-tuple-element.26.from_outer, ...), custom_call_target="tpu_custom_call" | custom-call | flops 1 | bytes 1 | tf_op jit(solution)/shard_map/ahead_kernel/pallas_call | solution.py:297
  67.1 1.7 %collective-permute-start.6 = (bf16[512,256]{1,0:T(8,128)(2,1)S(1)}, bf16[512,256]{1,0:T(8,128)(2,1)S(1)}, u32[]{:S(2)}, u32[]{:S(2)}) collective-permute-start(bf16[512,256]{1,0:T(8,128)(2,1)S(1)} %get-tuple-element.33), channel_id=1, source_target_pairs={{0,15},{1,2},{2,1},{3,4},{4,3},{5,6},{6,5},{7,8},{8,7},{9,10},{10,... | collective-permute-start | bytes 786440 | tf_op jit(solution)/shard_map/ppermute | solution.py:280
  68.9 0.1 collective-permute-start.5
  68.9 0.0 collective-permute-done.8.s_inner_own
  69.0 4.9 %late_kernel.1 = (bf16[3,8,256,256]{3,2,1,0:T(8,128)(2,1)}, f32[3,768,256]{2,1,0:T(8,128)S(1)}) custom-call(s32[8,48]{1,0:T(8,128)S(1)} %bitcast.6, bf16[3,768,256]{2,1,0:T(8,128)(2,1)S(1)} %get-tuple-element.23.own, bf16[3,768,256]{2,1,0:T(8,128)(2,1)S(1)} %get-tuple-element.24.outer, bf16[3,768,256]{2,1,0:T(8,128)(2,1)S(1)} %collective-permute-done.outer_own, ...), custom_call_target="tpu_custom_call" | custom-call | flops 1 | bytes 1 | tf_op jit(solution)/shard_map/late_kernel/pallas_call | solution.py:297
  73.9 2.9 %collective-permute-done.7.s_outer_head = bf16[2,768,256]{2,1,0:T(8,128)(2,1)S(1)} collective-permute-done((bf16[2,768,256]{2,1,0:T(8,128)(2,1)S(1)}, bf16[2,768,256]{2,1,0:T(8,128)(2,1)S(1)}, u32[]{:S(2)}, u32[]{:S(2)}) %collective-permute-start.7) | collective-permute-done | bytes 786464 | tf_op jit(solution)/shard_map/ppermute | solution.py:280
  76.8 2.3 %head_kernel.1._ = bf16[3,8,256,256]{3,2,1,0:T(8,128)(2,1)} custom-call(s32[8,48]{1,0:T(8,128)S(1)} %bitcast.7, bf16[3,768,256]{2,1,0:T(8,128)(2,1)S(1)} %get-tuple-element.24.outer, bf16[2,768,256]{2,1,0:T(8,128)(2,1)S(1)} %collective-permute-done.7.s_outer_head, f32[3,768,256]{2,1,0:T(8,128)S(1)} %get-tuple-element.39.rest, ...), custom_call_target="tpu_custom_call", output_to_operand_aliasing={{}: (4, {})} | custom-call | flops 1 | bytes 1 | tf_op jit(solution)/shard_map/head_kernel/pallas_call | solution.py:297
  79.1 0.5 collective-permute-done.6.blocks
  79.6 0.8 tail_kernel.2._
  80.3 0.6 collective-permute-done.5.blocks
  81.0 0.7 tail_kernel.3
Async XLA Ops:
  1.1 12.2 %collective-permute-start.1 = (bf16[3,128,256]{2,1,0:T(8,128)(2,1)S(1)}, bf16[3,128,256]{2,1,0:T(8,128)(2,1)S(1)}, u32[]{:S(2)}, u32[]{:S(2)}) collective-permute-start(bf16[3,128,256]{2,1,0:T(8,128)(2,1)S(1)} %first.1._), channel_id=1, source_target_pairs={{0,15},{1,2},{2,1},{3,4},{4,3},{5,6},{6,5},{7,8},{8,7},{9,10},{10,... | collective-permute-start | bytes 589832 | tf_op jit(solution)/shard_map/ppermute | solution.py:280
  5.9 37.1 %collective-permute-start.2 = (bf16[3,640,256]{2,1,0:T(8,128)(2,1)S(1)}, bf16[3,640,256]{2,1,0:T(8,128)(2,1)S(1)}, u32[]{:S(2)}, u32[]{:S(2)}) collective-permute-start(bf16[3,640,256]{2,1,0:T(8,128)(2,1)S(1)} %get-tuple-element.25), channel_id=1, source_target_pairs={{0,15},{1,2},{2,1},{3,4},{4,3},{5,6},{6,5},{7,8},{8,7},{9,10},{10,... | collective-permute-start | bytes 2949128 | tf_op jit(solution)/shard_map/ppermute | solution.py:280
  6.0 58.1 %collective-permute-start = (bf16[3,768,256]{2,1,0:T(8,128)(2,1)S(1)}, bf16[3,768,256]{2,1,0:T(8,128)(2,1)S(1)}, u32[]{:S(2)}, u32[]{:S(2)}) collective-permute-start(bf16[3,768,256]{2,1,0:T(8,128)(2,1)S(1)} %get-tuple-element.23.own), channel_id=1, source_target_pairs={{0,15},{1,2},{2,1},{3,4},{4,3},{5,6},{6,5},{7,8},{8,7},{9,10},{10,... | collective-permute-start | bytes 3538952 | tf_op jit(solution)/shard_map/ppermute | solution.py:280
  7.7 41.8 %collective-permute-start.4 = (bf16[3,768,256]{2,1,0:T(8,128)(2,1)S(1)}, bf16[3,768,256]{2,1,0:T(8,128)(2,1)S(1)}, u32[]{:S(2)}, u32[]{:S(2)}) collective-permute-start(bf16[3,768,256]{2,1,0:T(8,128)(2,1)S(1)} %get-tuple-element.23.own), channel_id=1, source_target_pairs={{0,1},{1,0},{2,3},{3,2},{4,5},{5,4},{6,7},{7,6},{8,9},{9,8},{10,11... | collective-permute-start | bytes 3538952 | tf_op jit(solution)/shard_map/ppermute | solution.py:281
  13.3 31.3 %collective-permute-start.3 = (bf16[3,768,256]{2,1,0:T(8,128)(2,1)S(1)}, bf16[3,768,256]{2,1,0:T(8,128)(2,1)S(1)}, u32[]{:S(2)}, u32[]{:S(2)}) collective-permute-start(bf16[3,768,256]{2,1,0:T(8,128)(2,1)S(1)} %get-tuple-element.27.inner), channel_id=1, source_target_pairs={{0,1},{1,0},{2,3},{3,2},{4,5},{5,4},{6,7},{7,6},{8,9},{9,8},{10,11... | collective-permute-start | bytes 3538952 | tf_op jit(solution)/shard_map/ppermute | solution.py:281
  14.1 30.5 %copy-start = (s32[48,8]{0,1:T(8,128)S(1)}, s32[48,8]{0,1:T(8,128)}, u32[]{:S(2)}) copy-start(s32[48,8]{0,1:T(8,128)} %param.3) | copy-start | bytes 4612
  47.7 21.2 %collective-permute-start.8 = (bf16[3,768,256]{2,1,0:T(8,128)(2,1)S(1)}, bf16[3,768,256]{2,1,0:T(8,128)(2,1)S(1)}, u32[]{:S(2)}, u32[]{:S(2)}) collective-permute-start(bf16[3,768,256]{2,1,0:T(8,128)(2,1)S(1)} %get-tuple-element.29.s_own), channel_id=1, source_target_pairs={{0,1},{1,0},{2,3},{3,2},{4,5},{5,4},{6,7},{7,6},{8,9},{9,8},{10,11... | collective-permute-start | bytes 3538952 | tf_op jit(solution)/shard_map/ppermute | solution.py:281
  47.8 28.9 %collective-permute-start.7 = (bf16[2,768,256]{2,1,0:T(8,128)(2,1)S(1)}, bf16[2,768,256]{2,1,0:T(8,128)(2,1)S(1)}, u32[]{:S(2)}, u32[]{:S(2)}) collective-permute-start(bf16[2,768,256]{2,1,0:T(8,128)(2,1)S(1)} %get-tuple-element.34), channel_id=1, source_target_pairs={{0,15},{1,2},{2,1},{3,4},{4,3},{5,6},{6,5},{7,8},{8,7},{9,10},{10,... | collective-permute-start | bytes 2359304 | tf_op jit(solution)/shard_map/ppermute | solution.py:280
  67.1 12.4 %collective-permute-start.6 = (bf16[512,256]{1,0:T(8,128)(2,1)S(1)}, bf16[512,256]{1,0:T(8,128)(2,1)S(1)}, u32[]{:S(2)}, u32[]{:S(2)}) collective-permute-start(bf16[512,256]{1,0:T(8,128)(2,1)S(1)} %get-tuple-element.33), channel_id=1, source_target_pairs={{0,15},{1,2},{2,1},{3,4},{4,3},{5,6},{6,5},{7,8},{8,7},{9,10},{10,... | collective-permute-start | bytes 786440 | tf_op jit(solution)/shard_map/ppermute | solution.py:280
  68.9 12.1 %collective-permute-start.5 = (bf16[256,256]{1,0:T(8,128)(2,1)S(1)}, bf16[256,256]{1,0:T(8,128)(2,1)S(1)}, u32[]{:S(2)}, u32[]{:S(2)}) collective-permute-start(bf16[256,256]{1,0:T(8,128)(2,1)S(1)} %get-tuple-element.32), channel_id=1, source_target_pairs={{0,15},{1,2},{2,1},{3,4},{4,3},{5,6},{6,5},{7,8},{8,7},{9,10},{10,... | collective-permute-start | bytes 393224 | tf_op jit(solution)/shard_map/ppermute | solution.py:280

commit v11 on v8

--- a/solution.py
+++ b/solution.py
@@ -65,7 +65,10 @@
     load.start()
     me, other, _ = neighbours(devices)
     fetch.wait()
-    slots = [slot_of(pattern, me * rb, other * rb + j) for j in range(rb)]
+    columns = [pattern[s, me * rb] - other * rb for s in range(pattern.shape[0])]
+    slots = [jnp.int32(-1)] * rb
+    for s, column in enumerate(columns):
+        slots = [jnp.where(column == j, s, slot) for j, slot in enumerate(slots)]
     load.wait()
     place(slots, held, cut, 0, bs // 2)
 

time: 81.8 us -> 81.8 us (level)
  no operation moved by 1% of the time
where the time goes in v11:
time: 81.8 us; the launch traced here: 81.7 us
  waiting for transfers between devices  37.2 us (45%)
  Pallas kernels  30.7 us (38%)
  starting transfers between devices  13.7 us (17%)
    ppermute x6, waiting for transfers between devices, local(): to_outer = lambda x: lax.ppermute(x, 'grid', over)  37.2 us
    pallas_call x7, Pallas kernels, call(): pl.pallas_call(functools.partial(kernel, devices, rb, bs), out_shape=outs...  26 us
    ppermute x6, starting transfers between devices, local(): to_outer = lambda x: lax.ppermute(x, 'grid', over)  8.05 us
    ppermute x3, starting transfers between devices, local(): to_inner = lambda x: lax.ppermute(x, 'grid', across)  5.64 us
    pallas_call x1, Pallas kernels, pack(): pl.pallas_call(functools.partial(pack_kernel, devices, rb, bs), out_shape...  2.12 us
  transfers between devices with their start and end apart: 9, of which 5 were waited for; matrix products, arithmetic and copies ran while one was open for 0% of the time, Pallas kernels for 35%

profile of v11, /device:TPU:1, one launch (start us, length us, event | category | flops | bytes accessed | tf_op | source)
XLA Modules:
  0.0 81.7 jit_solution(5145934956292505425)
XLA Ops:
  0.0 1.1 %first.1._ = bf16[3,128,256]{2,1,0:T(8,128)(2,1)S(1)} custom-call(s32[8,48]{1,0:T(8,128)} %bitcast.1, bf16[3,8,256,256]{3,2,1,0:T(8,128)(2,1)} %blocks.3), custom_call_target="tpu_custom_call" | custom-call | flops 1 | bytes 1 | tf_op jit(solution)/shard_map/first/pallas_call | solution.py:100
  1.1 2.7 %collective-permute-start.1 = (bf16[3,128,256]{2,1,0:T(8,128)(2,1)S(1)}, bf16[3,128,256]{2,1,0:T(8,128)(2,1)S(1)}, u32[]{:S(2)}, u32[]{:S(2)}) collective-permute-start(bf16[3,128,256]{2,1,0:T(8,128)(2,1)S(1)} %first.1._), channel_id=1, source_target_pairs={{0,15},{1,2},{2,1},{3,4},{4,3},{5,6},{6,5},{7,8},{8,7},{9,10},{10,... | collective-permute-start | bytes 589832 | tf_op jit(solution)/shard_map/ppermute | solution.py:280
  3.8 2.1 %pack.1 = (bf16[3,640,256]{2,1,0:T(8,128)(2,1)S(1)}, bf16[3,768,256]{2,1,0:T(8,128)(2,1)S(1)}, bf16[3,768,256]{2,1,0:T(8,128)(2,1)S(1)}, bf16[3,768,256]{2,1,0:T(8,128)(2,1)S(1)}) custom-call(s32[8,48]{1,0:T(8,128)} %bitcast.2, bf16[3,8,256,256]{3,2,1,0:T(8,128)(2,1)} %blocks.3, bf16[3,128,256]{2,1,0:T(8,128)(2,1)S(1)} %first.1._), custom_call_target="tpu_custom_call" | custom-call | flops 1 | bytes 1 | tf_op jit(solution)/shard_map/pack/pallas_call | solution.py:115
  5.9 0.1 collective-permute-start.2
  6.0 1.7 %collective-permute-start = (bf16[3,768,256]{2,1,0:T(8,128)(2,1)S(1)}, bf16[3,768,256]{2,1,0:T(8,128)(2,1)S(1)}, u32[]{:S(2)}, u32[]{:S(2)}) collective-permute-start(bf16[3,768,256]{2,1,0:T(8,128)(2,1)S(1)} %get-tuple-element.23.own), channel_id=1, source_target_pairs={{0,15},{1,2},{2,1},{3,4},{4,3},{5,6},{6,5},{7,8},{8,7},{9,10},{10,... | collective-permute-start | bytes 3538952 | tf_op jit(solution)/shard_map/ppermute | solution.py:280
  7.7 5.6 %collective-permute-start.4 = (bf16[3,768,256]{2,1,0:T(8,128)(2,1)S(1)}, bf16[3,768,256]{2,1,0:T(8,128)(2,1)S(1)}, u32[]{:S(2)}, u32[]{:S(2)}) collective-permute-start(bf16[3,768,256]{2,1,0:T(8,128)(2,1)S(1)} %get-tuple-element.23.own), channel_id=1, source_target_pairs={{0,1},{1,0},{2,3},{3,2},{4,5},{5,4},{6,7},{7,6},{8,9},{9,8},{10,11... | collective-permute-start | bytes 3538952 | tf_op jit(solution)/shard_map/ppermute | solution.py:281
  13.3 0.0 collective-permute-start.3
  13.3 0.0 collective-permute-done.1.from_first
  13.3 0.7 begin_kernel.1.part
  14.0 0.0 copy-start
  14.1 29.0 %collective-permute-done.2.from_others = bf16[3,640,256]{2,1,0:T(8,128)(2,1)S(1)} collective-permute-done((bf16[3,640,256]{2,1,0:T(8,128)(2,1)S(1)}, bf16[3,640,256]{2,1,0:T(8,128)(2,1)S(1)}, u32[]{:S(2)}, u32[]{:S(2)}) %collective-permute-start.2) | collective-permute-done | bytes 983072 | tf_op jit(solution)/shard_map/ppermute | solution.py:280
  43.0 1.5 %outer_kernel.1 = (bf16[3,768,256]{2,1,0:T(8,128)(2,1)S(1)}, f32[3,768,256]{2,1,0:T(8,128)S(1)}) custom-call(bf16[3,768,256]{2,1,0:T(8,128)(2,1)S(1)} %get-tuple-element.24.outer, bf16[3,128,256]{2,1,0:T(8,128)(2,1)S(1)} %collective-permute-done.1.from_first, bf16[3,640,256]{2,1,0:T(8,128)(2,1)S(1)} %collective-permute-done.2.from_others, ...), custom_call_target="tpu_custom_call" | custom-call | flops 5000000000 | bytes 1 | tf_op jit(solution)/shard_map/outer_kernel/pallas_call | solution.py:297
  44.6 0.0 collective-permute-done.3.from_inner
  44.6 0.0 copy-done
  44.6 3.1 %square_kernel.1 = (bf16[3,768,256]{2,1,0:T(8,128)(2,1)S(1)}, bf16[2,768,256]{2,1,0:T(8,128)(2,1)S(1)}) custom-call(s32[8,48]{1,0:T(8,128)S(1)} %bitcast.3, bf16[3,768,256]{2,1,0:T(8,128)(2,1)S(1)} %get-tuple-element.23.own, bf16[3,768,256]{2,1,0:T(8,128)(2,1)S(1)} %get-tuple-element.27.inner, bf16[3,768,256]{2,1,0:T(8,128)(2,1)S(1)} %collective-permute-done.3.from_inner, ...), custom_call_target="tpu_custom_call" | custom-call | flops 1 | bytes 1 | tf_op jit(solution)/shard_map/square_kernel/pallas_call | solution.py:297
  47.7 0.1 collective-permute-start.8
  47.8 1.7 %collective-permute-start.7 = (bf16[2,768,256]{2,1,0:T(8,128)(2,1)S(1)}, bf16[2,768,256]{2,1,0:T(8,128)(2,1)S(1)}, u32[]{:S(2)}, u32[]{:S(2)}) collective-permute-start(bf16[2,768,256]{2,1,0:T(8,128)(2,1)S(1)} %get-tuple-element.34), channel_id=1, source_target_pairs={{0,15},{1,2},{2,1},{3,4},{4,3},{5,6},{6,5},{7,8},{8,7},{9,10},{10,... | collective-permute-start | bytes 2359304 | tf_op jit(solution)/shard_map/ppermute | solution.py:280
  49.5 0.0 collective-permute-done.4.inner_own
  49.5 10.3 %early_kernel.1 = (f32[3,768,256]{2,1,0:T(8,128)S(1)}, f32[3,768,256]{2,1,0:T(8,128)S(1)}, f32[3,768,256]{2,1,0:T(8,128)S(1)}, f32[3,768,256]{2,1,0:T(8,128)S(1)}) custom-call(s32[8,48]{1,0:T(8,128)S(1)} %bitcast.4, bf16[3,768,256]{2,1,0:T(8,128)(2,1)S(1)} %get-tuple-element.23.own, bf16[3,768,256]{2,1,0:T(8,128)(2,1)S(1)} %get-tuple-element.27.inner, ...), custom_call_target="tpu_custom_call" | custom-call | flops 1 | bytes 1 | tf_op jit(solution)/shard_map/early_kernel/pallas_call | solution.py:297
  59.9 4.2 %collective-permute-done.outer_own = bf16[3,768,256]{2,1,0:T(8,128)(2,1)S(1)} collective-permute-done((bf16[3,768,256]{2,1,0:T(8,128)(2,1)S(1)}, bf16[3,768,256]{2,1,0:T(8,128)(2,1)S(1)}, u32[]{:S(2)}, u32[]{:S(2)}) %collective-permute-start) | collective-permute-done | bytes 1179680 | tf_op jit(solution)/shard_map/ppermute | solution.py:280
  64.1 3.0 %ahead_kernel.1 = (bf16[3,768,256]{2,1,0:T(8,128)(2,1)S(1)}, bf16[512,256]{1,0:T(8,128)(2,1)S(1)}, bf16[256,256]{1,0:T(8,128)(2,1)S(1)}, s32[3,8,128]{2,1,0:T(8,128)S(1)}) custom-call(s32[8,48]{1,0:T(8,128)S(1)} %bitcast.5, bf16[3,768,256]{2,1,0:T(8,128)(2,1)S(1)} %collective-permute-done.outer_own, bf16[3,768,256]{2,1,0:T(8,128)(2,1)S(1)} %get-tuple-element.26.from_outer, ...), custom_call_target="tpu_custom_call" | custom-call | flops 1 | bytes 1 | tf_op jit(solution)/shard_map/ahead_kernel/pallas_call | solution.py:297
  67.1 1.7 %collective-permute-start.6 = (bf16[512,256]{1,0:T(8,128)(2,1)S(1)}, bf16[512,256]{1,0:T(8,128)(2,1)S(1)}, u32[]{:S(2)}, u32[]{:S(2)}) collective-permute-start(bf16[512,256]{1,0:T(8,128)(2,1)S(1)} %get-tuple-element.33), channel_id=1, source_target_pairs={{0,15},{1,2},{2,1},{3,4},{4,3},{5,6},{6,5},{7,8},{8,7},{9,10},{10,... | collective-permute-start | bytes 786440 | tf_op jit(solution)/shard_map/ppermute | solution.py:280
  68.9 0.1 collective-permute-start.5
  68.9 0.0 collective-permute-done.8.s_inner_own
  68.9 4.9 %late_kernel.1 = (bf16[3,8,256,256]{3,2,1,0:T(8,128)(2,1)}, f32[3,768,256]{2,1,0:T(8,128)S(1)}) custom-call(s32[8,48]{1,0:T(8,128)S(1)} %bitcast.6, bf16[3,768,256]{2,1,0:T(8,128)(2,1)S(1)} %get-tuple-element.23.own, bf16[3,768,256]{2,1,0:T(8,128)(2,1)S(1)} %get-tuple-element.24.outer, bf16[3,768,256]{2,1,0:T(8,128)(2,1)S(1)} %collective-permute-done.outer_own, ...), custom_call_target="tpu_custom_call" | custom-call | flops 1 | bytes 1 | tf_op jit(solution)/shard_map/late_kernel/pallas_call | solution.py:297
  73.9 2.8 %collective-permute-done.7.s_outer_head = bf16[2,768,256]{2,1,0:T(8,128)(2,1)S(1)} collective-permute-done((bf16[2,768,256]{2,1,0:T(8,128)(2,1)S(1)}, bf16[2,768,256]{2,1,0:T(8,128)(2,1)S(1)}, u32[]{:S(2)}, u32[]{:S(2)}) %collective-permute-start.7) | collective-permute-done | bytes 786464 | tf_op jit(solution)/shard_map/ppermute | solution.py:280
  76.7 2.3 %head_kernel.1._ = bf16[3,8,256,256]{3,2,1,0:T(8,128)(2,1)} custom-call(s32[8,48]{1,0:T(8,128)S(1)} %bitcast.7, bf16[3,768,256]{2,1,0:T(8,128)(2,1)S(1)} %get-tuple-element.24.outer, bf16[2,768,256]{2,1,0:T(8,128)(2,1)S(1)} %collective-permute-done.7.s_outer_head, f32[3,768,256]{2,1,0:T(8,128)S(1)} %get-tuple-element.39.rest, ...), custom_call_target="tpu_custom_call", output_to_operand_aliasing={{}: (4, {})} | custom-call | flops 1 | bytes 1 | tf_op jit(solution)/shard_map/head_kernel/pallas_call | solution.py:297
  79.1 0.5 collective-permute-done.6.blocks
  79.5 0.8 tail_kernel.2._
  80.3 0.6 collective-permute-done.5.blocks
  81.0 0.7 tail_kernel.3
Async XLA Ops:
  1.1 12.2 %collective-permute-start.1 = (bf16[3,128,256]{2,1,0:T(8,128)(2,1)S(1)}, bf16[3,128,256]{2,1,0:T(8,128)(2,1)S(1)}, u32[]{:S(2)}, u32[]{:S(2)}) collective-permute-start(bf16[3,128,256]{2,1,0:T(8,128)(2,1)S(1)} %first.1._), channel_id=1, source_target_pairs={{0,15},{1,2},{2,1},{3,4},{4,3},{5,6},{6,5},{7,8},{8,7},{9,10},{10,... | collective-permute-start | bytes 589832 | tf_op jit(solution)/shard_map/ppermute | solution.py:280
  5.9 37.1 %collective-permute-start.2 = (bf16[3,640,256]{2,1,0:T(8,128)(2,1)S(1)}, bf16[3,640,256]{2,1,0:T(8,128)(2,1)S(1)}, u32[]{:S(2)}, u32[]{:S(2)}) collective-permute-start(bf16[3,640,256]{2,1,0:T(8,128)(2,1)S(1)} %get-tuple-element.25), channel_id=1, source_target_pairs={{0,15},{1,2},{2,1},{3,4},{4,3},{5,6},{6,5},{7,8},{8,7},{9,10},{10,... | collective-permute-start | bytes 2949128 | tf_op jit(solution)/shard_map/ppermute | solution.py:280
  6.0 58.1 %collective-permute-start = (bf16[3,768,256]{2,1,0:T(8,128)(2,1)S(1)}, bf16[3,768,256]{2,1,0:T(8,128)(2,1)S(1)}, u32[]{:S(2)}, u32[]{:S(2)}) collective-permute-start(bf16[3,768,256]{2,1,0:T(8,128)(2,1)S(1)} %get-tuple-element.23.own), channel_id=1, source_target_pairs={{0,15},{1,2},{2,1},{3,4},{4,3},{5,6},{6,5},{7,8},{8,7},{9,10},{10,... | collective-permute-start | bytes 3538952 | tf_op jit(solution)/shard_map/ppermute | solution.py:280
  7.7 41.8 %collective-permute-start.4 = (bf16[3,768,256]{2,1,0:T(8,128)(2,1)S(1)}, bf16[3,768,256]{2,1,0:T(8,128)(2,1)S(1)}, u32[]{:S(2)}, u32[]{:S(2)}) collective-permute-start(bf16[3,768,256]{2,1,0:T(8,128)(2,1)S(1)} %get-tuple-element.23.own), channel_id=1, source_target_pairs={{0,1},{1,0},{2,3},{3,2},{4,5},{5,4},{6,7},{7,6},{8,9},{9,8},{10,11... | collective-permute-start | bytes 3538952 | tf_op jit(solution)/shard_map/ppermute | solution.py:281
  13.3 31.3 %collective-permute-start.3 = (bf16[3,768,256]{2,1,0:T(8,128)(2,1)S(1)}, bf16[3,768,256]{2,1,0:T(8,128)(2,1)S(1)}, u32[]{:S(2)}, u32[]{:S(2)}) collective-permute-start(bf16[3,768,256]{2,1,0:T(8,128)(2,1)S(1)} %get-tuple-element.27.inner), channel_id=1, source_target_pairs={{0,1},{1,0},{2,3},{3,2},{4,5},{5,4},{6,7},{7,6},{8,9},{9,8},{10,11... | collective-permute-start | bytes 3538952 | tf_op jit(solution)/shard_map/ppermute | solution.py:281
  14.0 30.5 %copy-start = (s32[48,8]{0,1:T(8,128)S(1)}, s32[48,8]{0,1:T(8,128)}, u32[]{:S(2)}) copy-start(s32[48,8]{0,1:T(8,128)} %param.3) | copy-start | bytes 4612
  47.7 21.2 %collective-permute-start.8 = (bf16[3,768,256]{2,1,0:T(8,128)(2,1)S(1)}, bf16[3,768,256]{2,1,0:T(8,128)(2,1)S(1)}, u32[]{:S(2)}, u32[]{:S(2)}) collective-permute-start(bf16[3,768,256]{2,1,0:T(8,128)(2,1)S(1)} %get-tuple-element.29.s_own), channel_id=1, source_target_pairs={{0,1},{1,0},{2,3},{3,2},{4,5},{5,4},{6,7},{7,6},{8,9},{9,8},{10,11... | collective-permute-start | bytes 3538952 | tf_op jit(solution)/shard_map/ppermute | solution.py:281
  47.8 28.9 %collective-permute-start.7 = (bf16[2,768,256]{2,1,0:T(8,128)(2,1)S(1)}, bf16[2,768,256]{2,1,0:T(8,128)(2,1)S(1)}, u32[]{:S(2)}, u32[]{:S(2)}) collective-permute-start(bf16[2,768,256]{2,1,0:T(8,128)(2,1)S(1)} %get-tuple-element.34), channel_id=1, source_target_pairs={{0,15},{1,2},{2,1},{3,4},{4,3},{5,6},{6,5},{7,8},{8,7},{9,10},{10,... | collective-permute-start | bytes 2359304 | tf_op jit(solution)/shard_map/ppermute | solution.py:280
  67.1 12.4 %collective-permute-start.6 = (bf16[512,256]{1,0:T(8,128)(2,1)S(1)}, bf16[512,256]{1,0:T(8,128)(2,1)S(1)}, u32[]{:S(2)}, u32[]{:S(2)}) collective-permute-start(bf16[512,256]{1,0:T(8,128)(2,1)S(1)} %get-tuple-element.33), channel_id=1, source_target_pairs={{0,15},{1,2},{2,1},{3,4},{4,3},{5,6},{6,5},{7,8},{8,7},{9,10},{10,... | collective-permute-start | bytes 786440 | tf_op jit(solution)/shard_map/ppermute | solution.py:280
  68.9 12.1 %collective-permute-start.5 = (bf16[256,256]{1,0:T(8,128)(2,1)S(1)}, bf16[256,256]{1,0:T(8,128)(2,1)S(1)}, u32[]{:S(2)}, u32[]{:S(2)}) collective-permute-start(bf16[256,256]{1,0:T(8,128)(2,1)S(1)} %get-tuple-element.32), channel_id=1, source_target_pairs={{0,15},{1,2},{2,1},{3,4},{4,3},{5,6},{6,5},{7,8},{8,7},{9,10},{10,... | collective-permute-start | bytes 393224 | tf_op jit(solution)/shard_map/ppermute | solution.py:280
